TPU v7x, 32 devices: a whole 2x2x4 slice. The times are simulated.
32 devices in a mesh: dp: 4 (over y, x), ctx: 8 (over z, core).
Axes of the slice: x: 2, y: 2, z: 4, core: 2. Of those that a mesh axis runs over, the one named last changes fastest.
Arguments:
- queries: bfloat16 [4, 1024, 2048], P('dp', 'ctx'), may hold values from -5 to 5
- key_rows: bfloat16 [4, 1024, 256], P('dp', 'ctx'), may hold values from -5 to 5
- value_stored_rows: bfloat16 [4, 1024, 256], P('dp', 'ctx'), may hold values from -6 to 6
- out_grad: bfloat16 [4, 1024, 2048], P('dp', 'ctx'), may hold values from -6 to 6
- documents: int32 [4, 1024], P('dp', 'ctx'), may hold values from 0 to 15, never falling along the last dimension, each value on 1 to 512 neighbouring positions
- swapped: int32 [4, 8, 4], P('dp', 'ctx'), may hold values from 0 to 1, as said below
Outputs:
- attended: bfloat16 [4, 1024, 2048], P('dp', 'ctx')
- query_grad: bfloat16 [4, 1024, 2048], P('dp', 'ctx')
- key_gradient_store: bfloat16 [4, 1024, 256], P('dp', 'ctx')
- value_gradient_store: bfloat16 [4, 1024, 256], P('dp', 'ctx')
Inputs may be any that keep to these rules, and one draw needn't show every extreme that they name: swapped[g, r, b] equals swapped[(g + 2) mod 4, r, b]. `documents`: document numbers never fall along a group's sequence; a document has 1 to 512 positions.
All inputs are finite; a program needn't handle non-finite values.
Results may differ from a plain program's by a relative error of at most 0.024.
Values may be sent and summed in bfloat16 or wider, within the bound.
No kernel may reach another device: no remote copies, remote signals or barrier semaphores. Data moves between devices by JAX's collectives and lax.ppermute only.
A program may use at most 64 MiB of HBM per device.

v0:
```python
import functools
import math

import jax
import jax.numpy as jnp
from jax import lax
from jax.experimental import pallas as pl
from jax.experimental.pallas import tpu as pltpu
from jax.sharding import Mesh
from jax.sharding import PartitionSpec as P

HEAD_SIZE = 128
QUERY_PER_KEY = 8
NBLK = 4
META = 16
DOC_ROW = NBLK
DOC_VALUES = 16
GROUPED = 4
HALF = QUERY_PER_KEY * HEAD_SIZE
NEG = -1e30
F32, BF16, I32 = jnp.float32, jnp.bfloat16, jnp.int32
NT = (((1,), (1,)), ((), ()))
VMEM = pl.BlockSpec(memory_space=pltpu.VMEM)
SMEM = pl.BlockSpec(memory_space=pltpu.SMEM)
HBM = pl.BlockSpec(memory_space=pltpu.HBM)


def core_index():
    return lax.rem(lax.axis_index("ctx"), 2)


def payload_kernel(swap_ref, key_ref, value_ref, docs_ref, own_ref, side_ref):
    rows = key_ref.shape[0]
    core = core_index()
    docs = jnp.broadcast_to(docs_ref[...].astype(F32), (META, rows))
    place = lax.broadcasted_iota(I32, docs.shape, 0)
    meta = jnp.where(place == DOC_ROW, docs, 0.0)
    for block in range(NBLK):
        meta = jnp.where(place == block, swap_ref[block].astype(F32), meta)
    meta = meta.astype(BF16)
    for ref, head in ((own_ref, core), (side_ref, 1 - core)):
        lane = pl.ds(pl.multiple_of(head * HEAD_SIZE, HEAD_SIZE), HEAD_SIZE)
        ref[:rows, :] = key_ref[:, lane]
        ref[rows : 2 * rows, :] = value_ref[:, lane]
        ref[2 * rows :, :] = meta


def rows_kernel(other, query_ref, grad_ref, rows_ref, sems):
    rows = query_ref.shape[0]
    core = core_index()
    head = 1 - core if other else core
    lanes = pl.ds(pl.multiple_of(head * HALF, HALF), HALF)
    copies = [
        pltpu.make_async_copy(
            source.at[:, lanes], rows_ref.at[pl.ds(part * rows, rows), :], sems.at[part]
        )
        for part, source in enumerate((query_ref, grad_ref))
    ]
    for copy in copies:
        copy.start()
    for copy in copies:
        copy.wait()


def write_heads(source_ref, head, out_ref, query_grad_ref, sems):
    rows = out_ref.shape[0]
    lanes = pl.ds(pl.multiple_of(head * HALF, HALF), HALF)
    copies = [
        pltpu.make_async_copy(
            source_ref.at[pl.ds(part * rows, rows), :], target.at[:, lanes], sems.at[part]
        )
        for part, target in enumerate((out_ref, query_grad_ref))
    ]
    for copy in copies:
        copy.start()
    for copy in copies:
        copy.wait()


def own_kernel(own_ref, out_ref, query_grad_ref, sems):
    write_heads(own_ref, core_index(), out_ref, query_grad_ref, sems)


def finish_kernel(side_ref, out_held, query_grad_held, out_ref, query_grad_ref, sems):
    write_heads(side_ref, 1 - core_index(), out_ref, query_grad_ref, sems)


def merge_hop(home, away, slots_at, rows, logs):
    key_log, value_log, key_turned, value_turned = logs
    per_block = rows // NBLK
    size = 2 * rows + META
    for who in range(2):
        base = pl.multiple_of(slots_at[who] * rows, rows)
        flags = home[who * size + 2 * rows : (who + 1) * size, :].astype(F32)
        for which, log, turned in ((0, key_log, key_turned), (1, value_log, value_turned)):
            merged = ([], [])
            for block in range(NBLK):
                mask = (
                    jnp.broadcast_to(flags[block : block + 1, :], (per_block, HEAD_SIZE)).astype(BF16)
                    > 0.5
                )
                first = who * size + which * rows + block * per_block
                own = home[first : first + per_block, :]
                other = away[first : first + per_block, :]
                merged[0].append(jnp.where(mask, other, own))
                merged[1].append(jnp.where(mask, own, other))
            for logical in range(2):
                whole = jnp.concatenate(merged[logical], axis=0)
                log[logical, pl.ds(base, rows), :] = whole
                turned[logical, :, pl.ds(base, rows)] = whole.T


def prepare_kernel(hops, *refs):
    homes, aways = refs[:hops], refs[hops : 2 * hops]
    logs = refs[2 * hops :]
    rows = (homes[0].shape[0] // 2 - META) // 2
    core = core_index()
    parity = (core, 1 - core)
    for k in range(hops):
        slots_at = [2 * (hops - 1 - k) + parity[who] for who in range(2)]
        merge_hop(homes[k], aways[k], slots_at, rows, logs)


def attention_kernel(hops, rows_ref, *refs):
    count = hops + 1
    slots = 2 * count
    window = slots - 1
    homes, aways = refs[:count], refs[count : 2 * count]
    ready = refs[2 * count : 2 * count + 4]
    out_all = refs[2 * count + 4]
    home_outs = refs[2 * count + 5 : 3 * count + 5]
    away_outs = refs[3 * count + 5 : 4 * count + 5]
    (
        key_log,
        value_log,
        key_turned,
        value_turned,
        doc_window,
        starts,
        flag_rows,
        key_total,
        value_total,
        logical_of,
        needed_of,
    ) = refs[4 * count + 5 :]
    rows = rows_ref.shape[0] // 4
    per_block = rows // NBLK
    lanes = QUERY_PER_KEY * per_block
    size = 2 * rows + META
    core = core_index()
    chip = lax.axis_index("ctx") // 2
    parity = (core, 1 - core)
    scale = 1.0 / math.sqrt(HEAD_SIZE)
    factor = scale * math.log2(math.e)

    key_total[...] = jnp.zeros_like(key_total)
    value_total[...] = jnp.zeros_like(value_total)
    doc_window[...] = jnp.full_like(doc_window, 1e4)

    def meta_of(ref, who):
        return ref[who * size + 2 * rows : (who + 1) * size, :].astype(F32)

    for k in range(count):
        for who in range(2):
            slot = 2 * (hops - k) + parity[who]
            base = pl.multiple_of(slot * rows, rows)
            for logical, ref in ((0, homes[k]), (1, aways[k])):
                docs = meta_of(ref, who)[DOC_ROW : DOC_ROW + 1, :]
                doc_window[logical, pl.ds(slot, 1), :] = jnp.where(chip >= k, docs, -1.0)
    logs = (key_log, value_log, key_turned, value_turned)
    for log, held in zip(logs[:2], ready[:2]):
        log[:, pl.ds(2 * rows, 2 * rows * hops), :] = held[...]
    for log, held in zip(logs[2:], ready[2:]):
        log[:, :, pl.ds(2 * rows, 2 * rows * hops)] = held[...]
    merge_hop(homes[hops], aways[hops], parity, rows, logs)

    values_down = lax.broadcasted_iota(I32, (DOC_VALUES, rows), 0).astype(F32)
    group = lax.broadcasted_iota(I32, (8, rows), 1) // per_block
    meta_rows = [meta_of(homes[0], who) for who in range(2)]
    for logical in range(2):
        lower = jnp.zeros((DOC_VALUES, rows), F32)
        for slot in range(slots):
            docs = jnp.broadcast_to(doc_window[logical, slot : slot + 1, :], lower.shape)
            lower = lower + jnp.where(docs < values_down, 1.0, 0.0)
        lower = jnp.broadcast_to(jnp.sum(lower, axis=1, keepdims=True), lower.shape)
        for who in range(2):
            docs = meta_of((homes, aways)[logical][0], who)[DOC_ROW : DOC_ROW + 1, :]
            docs = jnp.broadcast_to(docs, (8, rows))
            turns = [docs] + [pltpu.roll(docs, t * per_block, 1) for t in range(1, NBLK)]
            for block in range(NBLK):
                tiled = turns[0]
                for t in range(1, NBLK):
                    tiled = jnp.where(group == (block + t) % NBLK, turns[t], tiled)
                tiled = jnp.broadcast_to(tiled[:1], lower.shape)
                start = jnp.sum(jnp.where(tiled == values_down, lower, 0.0), axis=0, keepdims=True)
                starts[logical, who * NBLK + block : who * NBLK + block + 1, :] = start.astype(I32)
    for who in range(2):
        flag_rows[who * NBLK : (who + 1) * NBLK, :] = meta_rows[who][:NBLK, :]
    flags = flag_rows[...]
    firsts = [
        jnp.broadcast_to(
            jnp.min(starts[logical].astype(F32), axis=1, keepdims=True), flags.shape
        )
        for logical in range(2)
    ]
    first = jnp.where(flags > 0.5, firsts[1], firsts[0]).astype(I32)
    flags = flags.astype(I32)
    for unit_index in range(2 * NBLK):
        logical_of[unit_index] = flags[unit_index, 0]
        needed_of[unit_index] = window + parity[unit_index // NBLK] - first[unit_index, 0] // rows

    def unit(unit_index, chunks):
        who, block = unit_index // NBLK, lax.rem(unit_index, NBLK)
        logical = logical_of[unit_index]
        row_parity = jnp.where(who == 0, core, 1 - core)
        first_slot = window + row_parity - chunks
        first = pl.multiple_of(first_slot * rows, rows)
        span = pl.ds(first, chunks * rows)
        columns = [slice(h * HEAD_SIZE, (h + 1) * HEAD_SIZE) for h in range(QUERY_PER_KEY)]
        query_at = pl.ds(pl.multiple_of(2 * who * rows + block * per_block, per_block), per_block)
        grad_at = pl.ds(
            pl.multiple_of((2 * who + 1) * rows + block * per_block, per_block), per_block
        )
        query = jnp.concatenate([rows_ref[query_at, column] for column in columns], axis=0)
        grad = jnp.concatenate([rows_ref[grad_at, column] for column in columns], axis=0)
        scores = lax.dot_general(key_log[logical, span, :], query, NT, preferred_element_type=F32)
        shape = (chunks * rows, HEAD_SIZE)
        key_place = lax.broadcasted_iota(I32, shape, 0)
        row_first = starts[logical, pl.ds(unit_index, 1), :] - first
        row_last = (
            (chunks - 1) * rows
            + block * per_block
            + lax.rem(lax.broadcasted_iota(I32, (1, HEAD_SIZE), 1), per_block)
        )
        allowed = (key_place >= row_first) & (key_place <= row_last)
        scores = jnp.concatenate(
            [
                jnp.where(allowed, scores[:, lane : lane + HEAD_SIZE], NEG)
                for lane in range(0, lanes, HEAD_SIZE)
            ],
            axis=1,
        )
        peak = jnp.max(scores, axis=0, keepdims=True)
        powers = jnp.exp2((scores - peak) * factor)
        inverse = 1.0 / jnp.sum(powers, axis=0, keepdims=True)
        probs = powers * inverse
        weights = probs.astype(BF16)
        out_turned = jnp.dot(
            value_turned[logical, :, span], weights, preferred_element_type=F32
        ).astype(BF16)
        delta = jnp.sum(grad.T.astype(F32) * out_turned.astype(F32), axis=0, keepdims=True)
        prob_grad = lax.dot_general(
            value_log[logical, span, :], grad, NT, preferred_element_type=F32
        )
        score_grad = (probs * (prob_grad - delta)).astype(BF16)
        query_grad_turned = jnp.dot(
            key_turned[logical, :, span], score_grad, preferred_element_type=F32
        )
        key_add = jnp.dot(score_grad, query, preferred_element_type=F32)
        value_add = jnp.dot(weights, grad, preferred_element_type=F32)
        out = out_turned.T
        query_grad = (query_grad_turned * scale).astype(BF16).T
        return query_at, grad_at, logical, span, out, query_grad, key_add, value_add

    def step(pair, carry):
        members = [pair * GROUPED + m for m in range(GROUPED)]
        needed = needed_of[members[0]]
        for member in members[1:]:
            needed = jnp.maximum(needed, needed_of[member])
        for chunks in range(1, window + 1):

            @pl.when(needed == chunks)
            def _(chunks=chunks):
                results = [unit(member, chunks) for member in members]
                for query_at, grad_at, logical, span, out, query_grad, key_add, value_add in results:
                    key_total[logical, span, :] += key_add
                    value_total[logical, span, :] += value_add
                    for h in range(QUERY_PER_KEY):
                        column = slice(h * HEAD_SIZE, (h + 1) * HEAD_SIZE)
                        part = slice(h * per_block, (h + 1) * per_block)
                        out_all[query_at, column] = out[part, :]
                        out_all[grad_at, column] = query_grad[part, :]

        return carry

    lax.fori_loop(0, 2 * NBLK // GROUPED, step, 0)
    for k in range(count):
        for who in range(2):
            base = pl.multiple_of((2 * (hops - k) + parity[who]) * rows, rows)
            flags = meta_of(homes[k], who)
            for block in range(NBLK):
                at = pl.ds(base + block * per_block, per_block)
                mask = jnp.broadcast_to(flags[block : block + 1, :], (per_block, HEAD_SIZE)) > 0.5
                for which, total, gain in ((0, key_total, scale), (1, value_total, 1.0)):
                    part = (2 * who + which) * rows + block * per_block
                    first = total[0, at, :] * gain
                    second = total[1, at, :] * gain
                    home_outs[k][part : part + per_block, :] = jnp.where(mask, second, first).astype(BF16)
                    away_outs[k][part : part + per_block, :] = jnp.where(mask, first, second).astype(BF16)


def local(queries, key_rows, value_rows, out_grad, documents, swapped):
    ranks = lax.axis_size("ctx")
    hops = ranks // 4
    count = hops + 1
    slots = 2 * count
    rows, width = key_rows.shape[1:]
    keys = slots * rows
    size = 2 * rows + META
    queries, out_grad = queries[0], out_grad[0]

    def up(block, k):
        return lax.ppermute(block, "ctx", [(i, i + 2 * k) for i in range(ranks - 2 * k)])

    def down(block, k):
        return lax.ppermute(block, "ctx", [(i + 2 * k, i) for i in range(ranks - 2 * k)])

    def to_partner(block):
        return lax.ppermute(block, "half", [(0, 1), (1, 0)])

    def to_side(block):
        return lax.ppermute(block, "ctx", [(i, i ^ 1) for i in range(ranks)])

    payload, payload_side = pl.pallas_call(
        payload_kernel,
        out_shape=[pltpu.VMEM((size, HEAD_SIZE), BF16)] * 2,
        in_specs=[SMEM, VMEM, VMEM, VMEM],
        out_specs=[VMEM, VMEM],
    )(swapped[0, 0], key_rows[0], value_rows[0], documents)
    from_side = to_side(payload_side)

    def rows_of(other, queries, out_grad):
        return pl.pallas_call(
            functools.partial(rows_kernel, other),
            out_shape=pltpu.VMEM((2 * rows, HALF), BF16),
            in_specs=[HBM, HBM],
            out_specs=VMEM,
            scratch_shapes=[pltpu.SemaphoreType.DMA((2,))],
        )(queries, out_grad)

    both = jnp.concatenate([payload, from_side], axis=0)
    rows_side = rows_of(True, queries, out_grad)
    both, rows_side = lax.optimization_barrier((both, rows_side))
    rows_got = to_side(rows_side)
    home = [both] + [up(both, k) for k in range(1, count)]
    away = [to_partner(block) for block in home]
    *early, home[hops], queries, out_grad = lax.optimization_barrier(
        (*home[:hops], *away[:hops], home[hops], queries, out_grad)
    )
    rows_all = jnp.concatenate([rows_of(False, queries, out_grad), rows_got], axis=0)
    ready = pl.pallas_call(
        functools.partial(prepare_kernel, hops),
        out_shape=[pltpu.VMEM((2, 2 * rows * hops, HEAD_SIZE), BF16)] * 2
        + [pltpu.VMEM((2, HEAD_SIZE, 2 * rows * hops), BF16)] * 2,
        in_specs=[VMEM] * (2 * hops),
        out_specs=[VMEM] * 4,
        cost_estimate=pl.CostEstimate(flops=0, bytes_accessed=4 * 1024 * 1024, transcendentals=0),
    )(*early)
    chunk = pltpu.VMEM((4 * rows, HEAD_SIZE), BF16)
    outs = pl.pallas_call(
        functools.partial(attention_kernel, hops),
        out_shape=[pltpu.VMEM((4 * rows, HALF), BF16)] + [chunk] * (2 * count),
        in_specs=[VMEM] * (5 + 2 * count),
        out_specs=[VMEM] * (1 + 2 * count),
        scratch_shapes=[
            pltpu.VMEM((2, keys, HEAD_SIZE), BF16),
            pltpu.VMEM((2, keys, HEAD_SIZE), BF16),
            pltpu.VMEM((2, HEAD_SIZE, keys), BF16),
            pltpu.VMEM((2, HEAD_SIZE, keys), BF16),
            pltpu.VMEM((2, 16, rows), F32),
            pltpu.VMEM((2, 8, rows), I32),
            pltpu.VMEM((8, rows), F32),
            pltpu.VMEM((2, keys, HEAD_SIZE), F32),
            pltpu.VMEM((2, keys, HEAD_SIZE), F32),
            pltpu.SMEM((2 * NBLK,), I32),
            pltpu.SMEM((2 * NBLK,), I32),
        ],
        compiler_params=pltpu.CompilerParams(vmem_limit_bytes=40 * 1024 * 1024),
        cost_estimate=pl.CostEstimate(
            flops=12 * rows * keys * 2048,
            bytes_accessed=4 * 1024 * 1024,
            transcendentals=rows * keys * 16,
        ),
    )(rows_all, *home, *away, *ready)
    home_sum, away_sum = outs[1 : 1 + count], outs[1 + count :]
    side_out = outs[0][2 * rows :]
    out, query_grad = pl.pallas_call(
        own_kernel,
        out_shape=[jax.ShapeDtypeStruct(queries.shape, BF16)] * 2,
        in_specs=[VMEM],
        out_specs=[HBM] * 2,
        scratch_shapes=[pltpu.SemaphoreType.DMA((2,))],
        cost_estimate=pl.CostEstimate(flops=0, bytes_accessed=4 * 1024 * 1024, transcendentals=0),
    )(outs[0])

    parts = []
    for k in reversed(range(count)):
        crossed = to_partner(away_sum[k])
        if k == hops:
            crossed, out, query_grad = lax.optimization_barrier((crossed, out, query_grad))
        part = home_sum[k].astype(F32) + crossed.astype(F32)
        if k:
            part = part.astype(BF16)
            part = down(part, k)
        parts.append(part)
    out_got = to_side(side_out)
    out, query_grad = pl.pallas_call(
        finish_kernel,
        out_shape=[jax.ShapeDtypeStruct(queries.shape, BF16)] * 2,
        in_specs=[VMEM, HBM, HBM],
        out_specs=[HBM] * 2,
        input_output_aliases={1: 0, 2: 1},
        scratch_shapes=[pltpu.SemaphoreType.DMA((2,))],
    )(out_got, out, query_grad)
    parts[0], out, query_grad = lax.optimization_barrier((parts[0], out, query_grad))
    total = sum(part.astype(F32) for part in parts).astype(BF16)
    grads_got = to_side(total[2 * rows :])
    grads = total[: 2 * rows]
    first = core_index() == 0
    grads = jnp.concatenate(
        [jnp.where(first, grads, grads_got), jnp.where(first, grads_got, grads)], axis=1
    )
    return (out[None], query_grad[None], grads[None, :rows], grads[None, rows:])


def solution(mesh):
    groups, ranks = mesh.devices.shape
    wide = Mesh(mesh.devices.reshape(2, groups // 2, ranks), ("half", "pair", "ctx"))
    spec3 = P(("half", "pair"), "ctx", None)
    in_specs = (spec3, spec3, spec3, spec3, P(("half", "pair"), "ctx"), spec3)
    return jax.shard_map(
        local, mesh=wide, in_specs=in_specs, out_specs=(spec3,) * 4, check_vma=False
    )
```

profile of v0, /device:TPU:0, one launch (start us, length us, event | category | flops | bytes accessed | tf_op | source)
XLA Modules:
  0.0 52.6 jit_solution(14536824547986931468)
XLA Ops:
  0.6 0.9 %shard_map.93 = (bf16[272,128]{1,0:T(8,128)(2,1)S(1)}, bf16[272,128]{1,0:T(8,128)(2,1)S(1)}) custom-call(s32[4]{0:T(128)} %bitcast.19, bf16[128,256]{1,0:T(8,128)(2,1)} %bitcast.17, bf16[128,256]{1,0:T(8,128)(2,1)} %bitcast.18, s32[1,128]{1,0:T(1,128)} %docs_ref.1), custom_call_target="tpu_custom_call" | custom-call | tf_op jit(solution)/shard_map/pallas_call | solution.py:324
  1.6 0.5 collective-permute-start
  2.1 1.0 %shard_map.94 = bf16[256,1024]{1,0:T(8,128)(2,1)S(1)} custom-call(bf16[128,2048]{1,0:T(8,128)(2,1)} %bitcast.11, bf16[128,2048]{1,0:T(8,128)(2,1)} %bitcast.13), custom_call_target="tpu_custom_call" | custom-call | tf_op jit(solution)/shard_map/pallas_call | solution.py:333
  3.1 0.0 collective-permute-done
  3.2 0.0 copy-start.2
  3.2 0.3 collective-permute-start.5
  3.4 4.8 %collective-permute-start.1 = (bf16[544,128]{1,0:T(8,128)(2,1)S(1)}, bf16[544,128]{1,0:T(8,128)(2,1)S(1)}, u32[]{:S(2)}, u32[]{:S(2)}) collective-permute-start(bf16[544,128]{1,0:T(8,128)(2,1)S(1)} %pad_maximum_fusion.1.refs_0_), channel_id=1, source_target_pairs={{0,2},{1,3},{2,4},{3,5},{4,6},{5,7},{8,10},{9,11},{10,12},{11,13},... | collective-permute-start | bytes 417800 | tf_op jit(solution)/shard_map/ppermute | solution.py:313
  8.2 4.5 %collective-permute-start.4 = (bf16[544,128]{1,0:T(8,128)(2,1)S(1)}, bf16[544,128]{1,0:T(8,128)(2,1)S(1)}, u32[]{:S(2)}, u32[]{:S(2)}) collective-permute-start(bf16[544,128]{1,0:T(8,128)(2,1)S(1)} %pad_maximum_fusion.1.refs_0_), channel_id=1, source_target_pairs={{0,4},{1,5},{2,6},{3,7},{8,12},{9,13},{10,14},{11,15},{16,20},{17,... | collective-permute-start | bytes 417800 | tf_op jit(solution)/shard_map/ppermute | solution.py:313
  12.7 1.6 %collective-permute-start.2 = (bf16[544,128]{1,0:T(8,128)(2,1)S(1)}, bf16[544,128]{1,0:T(8,128)(2,1)S(1)}, u32[]{:S(2)}, u32[]{:S(2)}) collective-permute-start(bf16[544,128]{1,0:T(8,128)(2,1)S(1)} %pad_maximum_fusion.1.refs_0_), channel_id=1, source_target_pairs={{0,16},{16,0},{1,17},{17,1},{2,18},{18,2},{3,19},{19,3},{4,20},{20... | collective-permute-start | bytes 417800 | tf_op jit(solution)/shard_map/ppermute | solution.py:319
  14.3 0.0 collective-permute-done.1.refs_1_
  14.3 0.0 copy-start.4
  14.3 0.5 collective-permute-start.3
  14.8 0.9 %collective-permute-done.4.refs_2_ = bf16[544,128]{1,0:T(8,128)(2,1)S(1)} collective-permute-done((bf16[544,128]{1,0:T(8,128)(2,1)S(1)}, bf16[544,128]{1,0:T(8,128)(2,1)S(1)}, u32[]{:S(2)}, u32[]{:S(2)}) %collective-permute-start.4) | collective-permute-done | bytes 139296 | tf_op jit(solution)/shard_map/ppermute | solution.py:313
  15.8 1.5 %collective-permute-start.6 = (bf16[544,128]{1,0:T(8,128)(2,1)S(1)}, bf16[544,128]{1,0:T(8,128)(2,1)S(1)}, u32[]{:S(2)}, u32[]{:S(2)}) collective-permute-start(bf16[544,128]{1,0:T(8,128)(2,1)S(1)} %collective-permute-done.4.refs_2_), channel_id=1, source_target_pairs={{0,16},{16,0},{1,17},{17,1},{2,18},{18,2},{3,19},{19,3},{4,20},{20... | collective-permute-start | bytes 417800 | tf_op jit(solution)/shard_map/ppermute | solution.py:319
  17.3 2.1 %collective-permute-done.2.refs_2_.refs_3_ = bf16[544,128]{1,0:T(8,128)(2,1)S(1)} collective-permute-done((bf16[544,128]{1,0:T(8,128)(2,1)S(1)}, bf16[544,128]{1,0:T(8,128)(2,1)S(1)}, u32[]{:S(2)}, u32[]{:S(2)}) %collective-permute-start.2) | collective-permute-done | bytes 139296 | tf_op jit(solution)/shard_map/ppermute | solution.py:319
  19.4 0.0 copy-start.6
  19.4 3.0 %collective-permute-done.3.refs_3_.refs_4_ = bf16[544,128]{1,0:T(8,128)(2,1)S(1)} collective-permute-done((bf16[544,128]{1,0:T(8,128)(2,1)S(1)}, bf16[544,128]{1,0:T(8,128)(2,1)S(1)}, u32[]{:S(2)}, u32[]{:S(2)}) %collective-permute-start.3) | collective-permute-done | bytes 139296 | tf_op jit(solution)/shard_map/ppermute | solution.py:319
  22.4 0.0 copy-start.8
  22.4 1.1 %shard_map.95 = bf16[256,1024]{1,0:T(8,128)(2,1)S(1)} custom-call(bf16[128,2048]{1,0:T(8,128)(2,1)} %bitcast.12, bf16[128,2048]{1,0:T(8,128)(2,1)} %bitcast.14), custom_call_target="tpu_custom_call" | custom-call | tf_op jit(solution)/shard_map/pallas_call | solution.py:333
  23.5 0.0 copy-done.2
  23.5 0.0 copy-done.4
  23.5 0.0 copy-done.6
  23.5 0.0 copy-done.8
  23.5 1.3 %shard_map.96 = (bf16[2,512,128]{2,1,0:T(8,128)(2,1)S(1)}, bf16[2,512,128]{2,1,0:T(8,128)(2,1)S(1)}, bf16[2,128,512]{2,1,0:T(8,128)(2,1)S(1)}, bf16[2,128,512]{2,1,0:T(8,128)(2,1)S(1)}) custom-call(bf16[544,128]{1,0:T(8,128)(2,1)} %copy-done.2, bf16[544,128]{1,0:T(8,128)(2,1)} %copy-done.4, bf16[544,128]{1,0:T(8,128)(2,1)} %copy-done.6, ...), custom_call_target="tpu_custom_call" | custom-call | bytes 4194304 | tf_op jit(solution)/shard_map/pallas_call | solution.py:351
  24.8 0.0 copy-start.3
  24.8 0.0 copy-start.5
  24.9 0.0 copy-start.7
  24.9 0.0 copy-start.9
  24.9 0.0 collective-permute-done.5
  24.9 0.1 pad_maximum_fusion.rows_ref
  25.0 0.0 collective-permute-done.6.refs_5_
  25.0 0.8 %copy-done.3 = bf16[544,128]{1,0:T(8,128)(2,1)S(1)} copy-done((bf16[544,128]{1,0:T(8,128)(2,1)S(1)}, bf16[544,128]{1,0:T(8,128)(2,1)}, u32[]{:S(2)}) %copy-start.3) | copy-done | bytes 139288
  25.7 0.1 copy-done.5
  25.8 0.1 copy-done.7
  25.9 0.1 copy-done.9
  26.0 5.3 %shard_map.97 = (bf16[512,1024]{1,0:T(8,128)(2,1)S(1)}, bf16[512,128]{1,0:T(8,128)(2,1)S(1)}, bf16[512,128]{1,0:T(8,128)(2,1)S(1)}, bf16[512,128]{1,0:T(8,128)(2...) custom-call(bf16[512,1024]{1,0:T(8,128)(2,1)S(1)} %pad_maximum_fusion.rows_ref, ...), custom_call_target="tpu_custom_call" | custom-call | flops 2415919104 | bytes 4194304 | tf_op jit(solution)/shard_map/pallas_call | solution.py:360
  31.2 0.0 copy-start
  31.2 1.0 %copy-done = bf16[512,1024]{1,0:T(8,128)(2,1)} copy-done((bf16[512,1024]{1,0:T(8,128)(2,1)}, bf16[512,1024]{1,0:T(8,128)(2,1)S(1)}, u32[]{:S(2)}) %copy-start) | copy-done | bytes 1048600
  32.2 0.0 copy-start.1
  32.2 1.5 %collective-permute-start.7 = (bf16[512,128]{1,0:T(8,128)(2,1)S(1)}, bf16[512,128]{1,0:T(8,128)(2,1)S(1)}, u32[]{:S(2)}, u32[]{:S(2)}) collective-permute-start(bf16[512,128]{1,0:T(8,128)(2,1)S(1)} %get-tuple-element.52), channel_id=1, source_target_pairs={{0,16},{16,0},{1,17},{17,1},{2,18},{18,2},{3,19},{19,3},{4,20},{20... | collective-permute-start | bytes 393224 | tf_op jit(solution)/shard_map/ppermute | solution.py:319
  33.7 2.0 %shard_map.98 = (bf16[128,2048]{1,0:T(8,128)(2,1)}, bf16[128,2048]{1,0:T(8,128)(2,1)}) custom-call(bf16[512,1024]{1,0:T(8,128)(2,1)} %copy-done), custom_call_target="tpu_custom_call" | custom-call | bytes 4194304 | tf_op jit(solution)/shard_map/pallas_call | solution.py:387
  35.8 0.0 copy-done.1
  35.8 0.6 %collective-permute-start.10 = (bf16[512,128]{1,0:T(8,128)(2,1)S(1)}, bf16[512,128]{1,0:T(8,128)(2,1)S(1)}, u32[]{:S(2)}, u32[]{:S(2)}) collective-permute-start(bf16[512,128]{1,0:T(8,128)(2,1)S(1)} %get-tuple-element.65), channel_id=1, source_target_pairs={{0,16},{16,0},{1,17},{17,1},{2,18},{18,2},{3,19},{19,3},{4,20},{20... | collective-permute-start | bytes 393224 | tf_op jit(solution)/shard_map/ppermute | solution.py:319
  36.4 0.0 collective-permute-start.9
  36.4 1.5 %collective-permute-start.12 = (bf16[512,128]{1,0:T(8,128)(2,1)S(1)}, bf16[512,128]{1,0:T(8,128)(2,1)S(1)}, u32[]{:S(2)}, u32[]{:S(2)}) collective-permute-start(bf16[512,128]{1,0:T(8,128)(2,1)S(1)} %get-tuple-element.67), channel_id=1, source_target_pairs={{0,16},{16,0},{1,17},{17,1},{2,18},{18,2},{3,19},{19,3},{4,20},{20... | collective-permute-start | bytes 393224 | tf_op jit(solution)/shard_map/ppermute | solution.py:319
  37.9 0.4 collective-permute-done.7
  38.4 1.3 %collective-permute-start.8 = (bf16[512,128]{1,0:T(8,128)(2,1)S(1)}, bf16[512,128]{1,0:T(8,128)(2,1)S(1)}, u32[]{:S(2)}, u32[]{:S(2)}) collective-permute-start(bf16[512,128]{1,0:T(8,128)(2,1)S(1)} %add_convert_fusion.2), channel_id=1, source_target_pairs={{4,0},{5,1},{6,2},{7,3},{12,8},{13,9},{14,10},{15,11},{20,16},{21,... | collective-permute-start | bytes 393224 | tf_op jit(solution)/shard_map/ppermute | solution.py:316
  39.7 2.5 %collective-permute-done.10 = bf16[512,128]{1,0:T(8,128)(2,1)S(1)} collective-permute-done((bf16[512,128]{1,0:T(8,128)(2,1)S(1)}, bf16[512,128]{1,0:T(8,128)(2,1)S(1)}, u32[]{:S(2)}, u32[]{:S(2)}) %collective-permute-start.10) | collective-permute-done | bytes 131104 | tf_op jit(solution)/shard_map/ppermute | solution.py:319
  42.2 1.3 %collective-permute-start.11 = (bf16[512,128]{1,0:T(8,128)(2,1)S(1)}, bf16[512,128]{1,0:T(8,128)(2,1)S(1)}, u32[]{:S(2)}, u32[]{:S(2)}) collective-permute-start(bf16[512,128]{1,0:T(8,128)(2,1)S(1)} %add_convert_fusion.1), channel_id=1, source_target_pairs={{2,0},{3,1},{4,2},{5,3},{6,4},{7,5},{10,8},{11,9},{12,10},{13,11},... | collective-permute-start | bytes 393224 | tf_op jit(solution)/shard_map/ppermute | solution.py:316
  43.5 0.0 collective-permute-done.9.side_ref
  43.6 0.0 copy-start.10
  43.6 0.8 %copy-done.10 = bf16[256,1024]{1,0:T(8,128)(2,1)} copy-done((bf16[256,1024]{1,0:T(8,128)(2,1)}, bf16[256,1024]{1,0:T(8,128)(2,1)S(1)}, u32[]{:S(2)}) %copy-start.10) | copy-done | bytes 524312
  44.4 1.8 %shard_map.99 = (bf16[128,2048]{1,0:T(8,128)(2,1)}, bf16[128,2048]{1,0:T(8,128)(2,1)}) custom-call(bf16[256,1024]{1,0:T(8,128)(2,1)} %copy-done.10, bf16[128,2048]{1,0:T(8,128)(2,1)} %get-tuple-element.57.out_held, bf16[128,2048]{1,0:T(8,128)(2,1)} %get-tuple-element.58.query_grad_held), custom_call_target="tpu_custom_call", output_to_operand_aliasing={{0}: (1, {}), {1}: (2, {})} | custom-call | tf_op jit(solution)/shard_map/pallas_call | solution.py:407
  46.2 3.5 %collective-permute-done.8 = bf16[512,128]{1,0:T(8,128)(2,1)S(1)} collective-permute-done((bf16[512,128]{1,0:T(8,128)(2,1)S(1)}, bf16[512,128]{1,0:T(8,128)(2,1)S(1)}, u32[]{:S(2)}, u32[]{:S(2)}) %collective-permute-start.8) | collective-permute-done | bytes 131104 | tf_op jit(solution)/shard_map/ppermute | solution.py:316
  49.7 0.0 collective-permute-done.12
  49.7 0.9 %collective-permute-done.11 = bf16[512,128]{1,0:T(8,128)(2,1)S(1)} collective-permute-done((bf16[512,128]{1,0:T(8,128)(2,1)S(1)}, bf16[512,128]{1,0:T(8,128)(2,1)S(1)}, u32[]{:S(2)}, u32[]{:S(2)}) %collective-permute-start.11) | collective-permute-done | bytes 131104 | tf_op jit(solution)/shard_map/ppermute | solution.py:316
  50.6 0.1 add_convert_fusion
  50.6 0.1 collective-permute-start.13
  50.7 1.2 %collective-permute-done.13 = bf16[256,128]{1,0:T(8,128)(2,1)S(1)} collective-permute-done((bf16[256,128]{1,0:T(8,128)(2,1)S(1)}, bf16[256,128]{1,0:T(8,128)(2,1)S(1)}, u32[]{:S(2)}, u32[]{:S(2)}) %collective-permute-start.13) | collective-permute-done | bytes 65568 | tf_op jit(solution)/shard_map/ppermute | solution.py:322
  52.0 0.7 %fusion.2 = (bf16[1,128,256]{2,1,0:T(8,128)(2,1)}, bf16[1,128,256]{2,1,0:T(8,128)(2,1)}) fusion(bf16[256,128]{1,0:T(8,128)(2,1)S(1)} %get-tuple-element.68, bf16[256,128]{1,0:T(8,128)(2,1)S(1)} %get-tuple-element.69), kind=kLoop, calls=%fused_computation.10 | loop fusion | flops 262144 | bytes 262144 | tf_op jit(solution)/shard_map/broadcast_in_dim | solution.py:423
  (6 shorter events, 0.1 us)
Async XLA Ops:
  1.6 1.6 %collective-permute-start = (bf16[272,128]{1,0:T(8,128)(2,1)S(1)}, bf16[272,128]{1,0:T(8,128)(2,1)S(1)}, u32[]{:S(2)}, u32[]{:S(2)}) collective-permute-start(bf16[272,128]{1,0:T(8,128)(2,1)S(1)} %get-tuple-element.37), channel_id=1, source_target_pairs={{0,1},{1,0},{2,3},{3,2},{4,5},{5,4},{6,7},{7,6},{8,9},{9,8},{10,11... | collective-permute-start | bytes 208904 | tf_op jit(solution)/shard_map/ppermute | solution.py:322
  3.2 20.3 %copy-start.2 = (bf16[544,128]{1,0:T(8,128)(2,1)}, bf16[544,128]{1,0:T(8,128)(2,1)S(1)}, u32[]{:S(2)}) copy-start(bf16[544,128]{1,0:T(8,128)(2,1)S(1)} %pad_maximum_fusion.1.refs_0_) | copy-start | bytes 417796
  3.2 21.7 %collective-permute-start.5 = (bf16[256,1024]{1,0:T(8,128)(2,1)S(1)}, bf16[256,1024]{1,0:T(8,128)(2,1)S(1)}, u32[]{:S(2)}, u32[]{:S(2)}) collective-permute-start(bf16[256,1024]{1,0:T(8,128)(2,1)S(1)} %shard_map.94), channel_id=1, source_target_pairs={{0,1},{1,0},{2,3},{3,2},{4,5},{5,4},{6,7},{7,6},{8,9},{9,8},{10,11... | collective-permute-start | bytes 1572872 | tf_op jit(solution)/shard_map/ppermute | solution.py:322
  3.4 10.9 %collective-permute-start.1 = (bf16[544,128]{1,0:T(8,128)(2,1)S(1)}, bf16[544,128]{1,0:T(8,128)(2,1)S(1)}, u32[]{:S(2)}, u32[]{:S(2)}) collective-permute-start(bf16[544,128]{1,0:T(8,128)(2,1)S(1)} %pad_maximum_fusion.1.refs_0_), channel_id=1, source_target_pairs={{0,2},{1,3},{2,4},{3,5},{4,6},{5,7},{8,10},{9,11},{10,12},{11,13},... | collective-permute-start | bytes 417800 | tf_op jit(solution)/shard_map/ppermute | solution.py:313
  8.2 7.5 %collective-permute-start.4 = (bf16[544,128]{1,0:T(8,128)(2,1)S(1)}, bf16[544,128]{1,0:T(8,128)(2,1)S(1)}, u32[]{:S(2)}, u32[]{:S(2)}) collective-permute-start(bf16[544,128]{1,0:T(8,128)(2,1)S(1)} %pad_maximum_fusion.1.refs_0_), channel_id=1, source_target_pairs={{0,4},{1,5},{2,6},{3,7},{8,12},{9,13},{10,14},{11,15},{16,20},{17,... | collective-permute-start | bytes 417800 | tf_op jit(solution)/shard_map/ppermute | solution.py:313
  12.7 6.7 %collective-permute-start.2 = (bf16[544,128]{1,0:T(8,128)(2,1)S(1)}, bf16[544,128]{1,0:T(8,128)(2,1)S(1)}, u32[]{:S(2)}, u32[]{:S(2)}) collective-permute-start(bf16[544,128]{1,0:T(8,128)(2,1)S(1)} %pad_maximum_fusion.1.refs_0_), channel_id=1, source_target_pairs={{0,16},{16,0},{1,17},{17,1},{2,18},{18,2},{3,19},{19,3},{4,20},{20... | collective-permute-start | bytes 417800 | tf_op jit(solution)/shard_map/ppermute | solution.py:319
  14.3 9.2 %copy-start.4 = (bf16[544,128]{1,0:T(8,128)(2,1)}, bf16[544,128]{1,0:T(8,128)(2,1)S(1)}, u32[]{:S(2)}) copy-start(bf16[544,128]{1,0:T(8,128)(2,1)S(1)} %collective-permute-done.1.refs_1_) | copy-start | bytes 417796
  14.3 8.0 %collective-permute-start.3 = (bf16[544,128]{1,0:T(8,128)(2,1)S(1)}, bf16[544,128]{1,0:T(8,128)(2,1)S(1)}, u32[]{:S(2)}, u32[]{:S(2)}) collective-permute-start(bf16[544,128]{1,0:T(8,128)(2,1)S(1)} %collective-permute-done.1.refs_1_), channel_id=1, source_target_pairs={{0,16},{16,0},{1,17},{17,1},{2,18},{18,2},{3,19},{19,3},{4,20},{20... | collective-permute-start | bytes 417800 | tf_op jit(solution)/shard_map/ppermute | solution.py:319
  15.8 9.2 %collective-permute-start.6 = (bf16[544,128]{1,0:T(8,128)(2,1)S(1)}, bf16[544,128]{1,0:T(8,128)(2,1)S(1)}, u32[]{:S(2)}, u32[]{:S(2)}) collective-permute-start(bf16[544,128]{1,0:T(8,128)(2,1)S(1)} %collective-permute-done.4.refs_2_), channel_id=1, source_target_pairs={{0,16},{16,0},{1,17},{17,1},{2,18},{18,2},{3,19},{19,3},{4,20},{20... | collective-permute-start | bytes 417800 | tf_op jit(solution)/shard_map/ppermute | solution.py:319
  19.4 4.1 %copy-start.6 = (bf16[544,128]{1,0:T(8,128)(2,1)}, bf16[544,128]{1,0:T(8,128)(2,1)S(1)}, u32[]{:S(2)}) copy-start(bf16[544,128]{1,0:T(8,128)(2,1)S(1)} %collective-permute-done.2.refs_2_.refs_3_) | copy-start | bytes 417796
  22.4 1.1 %copy-start.8 = (bf16[544,128]{1,0:T(8,128)(2,1)}, bf16[544,128]{1,0:T(8,128)(2,1)S(1)}, u32[]{:S(2)}) copy-start(bf16[544,128]{1,0:T(8,128)(2,1)S(1)} %collective-permute-done.3.refs_3_.refs_4_) | copy-start | bytes 417796
  24.8 0.9 %copy-start.3 = (bf16[544,128]{1,0:T(8,128)(2,1)S(1)}, bf16[544,128]{1,0:T(8,128)(2,1)}, u32[]{:S(2)}) copy-start(bf16[544,128]{1,0:T(8,128)(2,1)} %copy-done.2) | copy-start | bytes 417796
  24.8 1.0 %copy-start.5 = (bf16[544,128]{1,0:T(8,128)(2,1)S(1)}, bf16[544,128]{1,0:T(8,128)(2,1)}, u32[]{:S(2)}) copy-start(bf16[544,128]{1,0:T(8,128)(2,1)} %copy-done.4) | copy-start | bytes 417796
  24.9 1.0 %copy-start.7 = (bf16[544,128]{1,0:T(8,128)(2,1)S(1)}, bf16[544,128]{1,0:T(8,128)(2,1)}, u32[]{:S(2)}) copy-start(bf16[544,128]{1,0:T(8,128)(2,1)} %copy-done.6) | copy-start | bytes 417796
  24.9 1.1 %copy-start.9 = (bf16[544,128]{1,0:T(8,128)(2,1)S(1)}, bf16[544,128]{1,0:T(8,128)(2,1)}, u32[]{:S(2)}) copy-start(bf16[544,128]{1,0:T(8,128)(2,1)} %copy-done.8) | copy-start | bytes 417796
  31.2 1.0 %copy-start = (bf16[512,1024]{1,0:T(8,128)(2,1)}, bf16[512,1024]{1,0:T(8,128)(2,1)S(1)}, u32[]{:S(2)}) copy-start(bf16[512,1024]{1,0:T(8,128)(2,1)S(1)} %get-tuple-element.53.own_ref) | copy-start | bytes 3145732
  32.2 3.6 %copy-start.1 = (bf16[512,1024]{1,0:T(8,128)(2,1)S(1)}, bf16[512,1024]{1,0:T(8,128)(2,1)}, u32[]{:S(2)}) copy-start(bf16[512,1024]{1,0:T(8,128)(2,1)} %copy-done) | copy-start | bytes 3145732
  32.2 6.2 %collective-permute-start.7 = (bf16[512,128]{1,0:T(8,128)(2,1)S(1)}, bf16[512,128]{1,0:T(8,128)(2,1)S(1)}, u32[]{:S(2)}, u32[]{:S(2)}) collective-permute-start(bf16[512,128]{1,0:T(8,128)(2,1)S(1)} %get-tuple-element.52), channel_id=1, source_target_pairs={{0,16},{16,0},{1,17},{17,1},{2,18},{18,2},{3,19},{19,3},{4,20},{20... | collective-permute-start | bytes 393224 | tf_op jit(solution)/shard_map/ppermute | solution.py:319
  35.8 6.4 %collective-permute-start.10 = (bf16[512,128]{1,0:T(8,128)(2,1)S(1)}, bf16[512,128]{1,0:T(8,128)(2,1)S(1)}, u32[]{:S(2)}, u32[]{:S(2)}) collective-permute-start(bf16[512,128]{1,0:T(8,128)(2,1)S(1)} %get-tuple-element.65), channel_id=1, source_target_pairs={{0,16},{16,0},{1,17},{17,1},{2,18},{18,2},{3,19},{19,3},{4,20},{20... | collective-permute-start | bytes 393224 | tf_op jit(solution)/shard_map/ppermute | solution.py:319
  36.4 7.2 %collective-permute-start.9 = (bf16[256,1024]{1,0:T(8,128)(2,1)S(1)}, bf16[256,1024]{1,0:T(8,128)(2,1)S(1)}, u32[]{:S(2)}, u32[]{:S(2)}) collective-permute-start(bf16[256,1024]{1,0:T(8,128)(2,1)S(1)} %slice.15), channel_id=1, source_target_pairs={{0,1},{1,0},{2,3},{3,2},{4,5},{5,4},{6,7},{7,6},{8,9},{9,8},{10,11... | collective-permute-start | bytes 1572872 | tf_op jit(solution)/shard_map/ppermute | solution.py:322
  36.4 13.3 %collective-permute-start.12 = (bf16[512,128]{1,0:T(8,128)(2,1)S(1)}, bf16[512,128]{1,0:T(8,128)(2,1)S(1)}, u32[]{:S(2)}, u32[]{:S(2)}) collective-permute-start(bf16[512,128]{1,0:T(8,128)(2,1)S(1)} %get-tuple-element.67), channel_id=1, source_target_pairs={{0,16},{16,0},{1,17},{17,1},{2,18},{18,2},{3,19},{19,3},{4,20},{20... | collective-permute-start | bytes 393224 | tf_op jit(solution)/shard_map/ppermute | solution.py:319
  38.4 11.3 %collective-permute-start.8 = (bf16[512,128]{1,0:T(8,128)(2,1)S(1)}, bf16[512,128]{1,0:T(8,128)(2,1)S(1)}, u32[]{:S(2)}, u32[]{:S(2)}) collective-permute-start(bf16[512,128]{1,0:T(8,128)(2,1)S(1)} %add_convert_fusion.2), channel_id=1, source_target_pairs={{4,0},{5,1},{6,2},{7,3},{12,8},{13,9},{14,10},{15,11},{20,16},{21,... | collective-permute-start | bytes 393224 | tf_op jit(solution)/shard_map/ppermute | solution.py:316
  42.2 8.3 %collective-permute-start.11 = (bf16[512,128]{1,0:T(8,128)(2,1)S(1)}, bf16[512,128]{1,0:T(8,128)(2,1)S(1)}, u32[]{:S(2)}, u32[]{:S(2)}) collective-permute-start(bf16[512,128]{1,0:T(8,128)(2,1)S(1)} %add_convert_fusion.1), channel_id=1, source_target_pairs={{2,0},{3,1},{4,2},{5,3},{6,4},{7,5},{10,8},{11,9},{12,10},{13,11},... | collective-permute-start | bytes 393224 | tf_op jit(solution)/shard_map/ppermute | solution.py:316
  43.6 0.8 %copy-start.10 = (bf16[256,1024]{1,0:T(8,128)(2,1)}, bf16[256,1024]{1,0:T(8,128)(2,1)S(1)}, u32[]{:S(2)}) copy-start(bf16[256,1024]{1,0:T(8,128)(2,1)S(1)} %collective-permute-done.9.side_ref) | copy-start | bytes 1572868
  50.6 1.3 %collective-permute-start.13 = (bf16[256,128]{1,0:T(8,128)(2,1)S(1)}, bf16[256,128]{1,0:T(8,128)(2,1)S(1)}, u32[]{:S(2)}, u32[]{:S(2)}) collective-permute-start(bf16[256,128]{1,0:T(8,128)(2,1)S(1)} %slice.21), channel_id=1, source_target_pairs={{0,1},{1,0},{2,3},{3,2},{4,5},{5,4},{6,7},{7,6},{8,9},{9,8},{10,11... | collective-permute-start | bytes 196616 | tf_op jit(solution)/shard_map/ppermute | solution.py:322
where the time goes:
time: 53.1 us; the launch traced here: 52.6 us
  starting transfers between devices  19.9 us (37%)
  waiting for transfers between devices  14.5 us (27%)
  Pallas kernels  13.5 us (25%)
  local copies, waits for them, and re-layouts  2.83 us (5%)
  other arithmetic  0.91 us (2%)
  between operations  0.91 us (2%)
    ppermute x2, starting transfers between devices, up(): lax.ppermute(block, 'ctx', [(i, i + 2 * k) for i in range(ranks - 2 * k)])  9.29 us
    ppermute x6, waiting for transfers between devices, to_partner(): return lax.ppermute(block, 'half', [(0, 1), (1, 0)])  8.04 us
    ppermute x6, starting transfers between devices, to_partner(): return lax.ppermute(block, 'half', [(0, 1), (1, 0)])  7.22 us
    pallas_call x1, Pallas kernels, local(): pl.pallas_call(functools.partial(attention_kernel, hops), out_shape=[pltp...  5.26 us
    ppermute x2, waiting for transfers between devices, down(): lax.ppermute(block, 'ctx', [(i + 2 * k, i) for i in range(ranks - 2 * k)])  4.33 us
    unnamed x22, local copies, waits for them, and re-layouts  2.78 us
    ppermute x2, starting transfers between devices, down(): lax.ppermute(block, 'ctx', [(i + 2 * k, i) for i in range(ranks - 2 * k)])  2.58 us
    pallas_call x2, Pallas kernels, rows_of(): pl.pallas_call(functools.partial(rows_kernel, other), out_shape=pltpu.VME...  2.14 us
  transfers between devices with their start and end apart: 14, of which 8 were waited for; matrix products, arithmetic and copies ran while one was open for 0% of the time, Pallas kernels for 14%

commit v1 on v0

--- a/solution.py
+++ b/solution.py
@@ -23,6 +23,7 @@
 VMEM = pl.BlockSpec(memory_space=pltpu.VMEM)
 SMEM = pl.BlockSpec(memory_space=pltpu.SMEM)
 HBM = pl.BlockSpec(memory_space=pltpu.HBM)
+SMALL = pltpu.CompilerParams(vmem_limit_bytes=8 * 1024 * 1024)
 
 
 def core_index():
@@ -326,6 +327,7 @@
         out_shape=[pltpu.VMEM((size, HEAD_SIZE), BF16)] * 2,
         in_specs=[SMEM, VMEM, VMEM, VMEM],
         out_specs=[VMEM, VMEM],
+        compiler_params=SMALL,
     )(swapped[0, 0], key_rows[0], value_rows[0], documents)
     from_side = to_side(payload_side)
 
@@ -336,6 +338,7 @@
             in_specs=[HBM, HBM],
             out_specs=VMEM,
             scratch_shapes=[pltpu.SemaphoreType.DMA((2,))],
+            compiler_params=SMALL,
         )(queries, out_grad)
 
     both = jnp.concatenate([payload, from_side], axis=0)
@@ -354,6 +357,7 @@
         + [pltpu.VMEM((2, HEAD_SIZE, 2 * rows * hops), BF16)] * 2,
         in_specs=[VMEM] * (2 * hops),
         out_specs=[VMEM] * 4,
+        compiler_params=SMALL,
         cost_estimate=pl.CostEstimate(flops=0, bytes_accessed=4 * 1024 * 1024, transcendentals=0),
     )(*early)
     chunk = pltpu.VMEM((4 * rows, HEAD_SIZE), BF16)
@@ -375,7 +379,7 @@
             pltpu.SMEM((2 * NBLK,), I32),
             pltpu.SMEM((2 * NBLK,), I32),
         ],
-        compiler_params=pltpu.CompilerParams(vmem_limit_bytes=40 * 1024 * 1024),
+        compiler_params=pltpu.CompilerParams(vmem_limit_bytes=32 * 1024 * 1024),
         cost_estimate=pl.CostEstimate(
             flops=12 * rows * keys * 2048,
             bytes_accessed=4 * 1024 * 1024,
@@ -389,6 +393,7 @@
         out_shape=[jax.ShapeDtypeStruct(queries.shape, BF16)] * 2,
         in_specs=[VMEM],
         out_specs=[HBM] * 2,
+        compiler_params=SMALL,
         scratch_shapes=[pltpu.SemaphoreType.DMA((2,))],
         cost_estimate=pl.CostEstimate(flops=0, bytes_accessed=4 * 1024 * 1024, transcendentals=0),
     )(outs[0])
@@ -396,8 +401,6 @@
     parts = []
     for k in reversed(range(count)):
         crossed = to_partner(away_sum[k])
-        if k == hops:
-            crossed, out, query_grad = lax.optimization_barrier((crossed, out, query_grad))
         part = home_sum[k].astype(F32) + crossed.astype(F32)
         if k:
             part = part.astype(BF16)
@@ -409,6 +412,7 @@
         out_shape=[jax.ShapeDtypeStruct(queries.shape, BF16)] * 2,
         in_specs=[VMEM, HBM, HBM],
         out_specs=[HBM] * 2,
+        compiler_params=SMALL,
         input_output_aliases={1: 0, 2: 1},
         scratch_shapes=[pltpu.SemaphoreType.DMA((2,))],
     )(out_got, out, query_grad)

time: 53.1 us -> 53 us (level)
  Pallas kernels: 13.5 us -> 7.79 us
  waiting for transfers between devices: 14.5 us -> 17.6 us
  local copies, waits for them, and re-layouts: 2.83 us -> 5.11 us
    unnamed x22 -> x16, local copies, waits for them, and re-layouts: 2.78 us -> 5.07 us
    pallas_call x2, Pallas kernels: 2.14 us -> 0.12 us  [rows_of(): pl.pallas_call(functools.partial(rows_kernel, other), out_shape=pltpu.VME...]
    ppermute x2, waiting for transfers between devices: 4.33 us -> 5.92 us  [down(): lax.ppermute(block, 'ctx', [(i + 2 * k, i) for i in range(ranks - 2 * k)])]
    ppermute x6, waiting for transfers between devices: 8.04 us -> 9.55 us  [to_partner(): return lax.ppermute(block, 'half', [(0, 1), (1, 0)])]
    pallas_call x1, Pallas kernels: 2.03 us -> 0.82 us  [local(): pl.pallas_call(own_kernel, out_shape=[jax.ShapeDtypeStruct(queries.shape,...]
    pallas_call x1, Pallas kernels: 1.32 us -> 0.21 us  [local(): pl.pallas_call(functools.partial(prepare_kernel, hops), out_shape=[pltpu....]
    pallas_call x1, Pallas kernels: 1.85 us -> 0.82 us  [local(): pl.pallas_call(finish_kernel, out_shape=[jax.ShapeDtypeStruct(queries.sha...]
  transfers between devices with their start and end apart: 14 -> 14, of which waited for: 8 -> 8; matrix products, arithmetic and copies ran while one was open for 0% -> 0% of each run, Pallas kernels for 14% -> 4%
where the time goes in v1:
time: 53 us; the launch traced here: 52.3 us
  starting transfers between devices  20.1 us (38%)
  waiting for transfers between devices  17.6 us (33%)
  Pallas kernels  7.79 us (15%)
  local copies, waits for them, and re-layouts  5.11 us (10%)
  other arithmetic  0.91 us (2%)
  between operations  0.83 us (2%)
    ppermute x6, waiting for transfers between devices, to_partner(): return lax.ppermute(block, 'half', [(0, 1), (1, 0)])  9.55 us
    ppermute x2, starting transfers between devices, up(): lax.ppermute(block, 'ctx', [(i, i + 2 * k) for i in range(ranks - 2 * k)])  9.42 us
    ppermute x6, starting transfers between devices, to_partner(): return lax.ppermute(block, 'half', [(0, 1), (1, 0)])  7.29 us
    ppermute x2, waiting for transfers between devices, down(): lax.ppermute(block, 'ctx', [(i + 2 * k, i) for i in range(ranks - 2 * k)])  5.92 us
    pallas_call x1, Pallas kernels, local(): pl.pallas_call(functools.partial(attention_kernel, hops), out_shape=[pltp...  5.25 us
    unnamed x16, local copies, waits for them, and re-layouts  5.07 us
    ppermute x2, starting transfers between devices, down(): lax.ppermute(block, 'ctx', [(i + 2 * k, i) for i in range(ranks - 2 * k)])  2.58 us
    ppermute x4, waiting for transfers between devices, to_side(): return lax.ppermute(block, 'ctx', [(i, i ^ 1) for i in range(ranks)])  1.24 us
  transfers between devices with their start and end apart: 14, of which 8 were waited for; matrix products, arithmetic and copies ran while one was open for 0% of the time, Pallas kernels for 4%

profile of v1, /device:TPU:0, one launch (start us, length us, event | category | flops | bytes accessed | tf_op | source)
XLA Modules:
  0.0 52.3 jit_solution(9002860222180723995)
XLA Ops:
  0.6 0.0 copy-start.4
  0.6 0.8 %copy-done.4 = bf16[1,128,256]{2,1,0:T(8,128)(2,1)S(1)} copy-done((bf16[1,128,256]{2,1,0:T(8,128)(2,1)S(1)}, bf16[1,128,256]{2,1,0:T(8,128)(2,1)}, u32[]{:S(2)}) %copy-start.4) | copy-done | bytes 65560
  1.5 0.0 copy-start.5
  1.5 0.8 %copy-done.5 = bf16[1,128,256]{2,1,0:T(8,128)(2,1)S(1)} copy-done((bf16[1,128,256]{2,1,0:T(8,128)(2,1)S(1)}, bf16[1,128,256]{2,1,0:T(8,128)(2,1)}, u32[]{:S(2)}) %copy-start.5) | copy-done | bytes 65560
  2.3 0.0 copy-start.6
  2.3 0.7 %copy-done.6 = s32[1,1,4]{2,1,0:T(1,128)S(1)} copy-done((s32[1,1,4]{2,1,0:T(1,128)S(1)}, s32[1,1,4]{2,1,0:T(1,128)}, u32[]{:S(2)}) %copy-start.6) | copy-done | bytes 40
  3.0 0.0 copy-start.7
  3.0 0.7 %copy-done.7 = s32[1,128]{1,0:T(1,128)S(1)} copy-done((s32[1,128]{1,0:T(1,128)S(1)}, s32[1,128]{1,0:T(1,128)}, u32[]{:S(2)}) %copy-start.7) | copy-done | bytes 536
  3.6 0.6 %shard_map.93 = (bf16[272,128]{1,0:T(8,128)(2,1)S(1)}, bf16[272,128]{1,0:T(8,128)(2,1)S(1)}) custom-call(s32[4]{0:T(128)S(1)} %bitcast.17, bf16[128,256]{1,0:T(8,128)(2,1)S(1)} %bitcast.15, bf16[128,256]{1,0:T(8,128)(2,1)S(1)} %bitcast.16, s32[1,128]{1,0:T(1,128)S(1)} %copy-done.7), custom_call_target="tpu_custom_call" | custom-call | tf_op jit(solution)/shard_map/pallas_call | solution.py:325
  4.2 0.5 collective-permute-start
  4.7 0.0 copy-start
  4.7 1.0 %copy-done = bf16[1,128,2048]{2,1,0:T(8,128)(2,1)S(1)} copy-done((bf16[1,128,2048]{2,1,0:T(8,128)(2,1)S(1)}, bf16[1,128,2048]{2,1,0:T(8,128)(2,1)}, u32[]{:S(2)}) %copy-start) | copy-done | bytes 524312
  5.8 0.0 copy-start.2
  5.8 1.0 %copy-done.2 = bf16[1,128,2048]{2,1,0:T(8,128)(2,1)S(1)} copy-done((bf16[1,128,2048]{2,1,0:T(8,128)(2,1)S(1)}, bf16[1,128,2048]{2,1,0:T(8,128)(2,1)}, u32[]{:S(2)}) %copy-start.2) | copy-done | bytes 524312
  6.8 0.0 copy-start.1
  6.8 0.0 copy-start.3
  6.8 0.1 shard_map.94
  6.9 0.0 collective-permute-done
  6.9 0.1 collective-permute-start.5
  7.0 4.9 %collective-permute-start.1 = (bf16[544,128]{1,0:T(8,128)(2,1)S(1)}, bf16[544,128]{1,0:T(8,128)(2,1)S(1)}, u32[]{:S(2)}, u32[]{:S(2)}) collective-permute-start(bf16[544,128]{1,0:T(8,128)(2,1)S(1)} %pad_maximum_fusion.1.refs_0_), channel_id=1, source_target_pairs={{0,2},{1,3},{2,4},{3,5},{4,6},{5,7},{8,10},{9,11},{10,12},{11,13},... | collective-permute-start | bytes 417800 | tf_op jit(solution)/shard_map/ppermute | solution.py:314
  12.0 4.5 %collective-permute-start.4 = (bf16[544,128]{1,0:T(8,128)(2,1)S(1)}, bf16[544,128]{1,0:T(8,128)(2,1)S(1)}, u32[]{:S(2)}, u32[]{:S(2)}) collective-permute-start(bf16[544,128]{1,0:T(8,128)(2,1)S(1)} %pad_maximum_fusion.1.refs_0_), channel_id=1, source_target_pairs={{0,4},{1,5},{2,6},{3,7},{8,12},{9,13},{10,14},{11,15},{16,20},{17,... | collective-permute-start | bytes 417800 | tf_op jit(solution)/shard_map/ppermute | solution.py:314
  16.5 1.6 %collective-permute-start.2 = (bf16[544,128]{1,0:T(8,128)(2,1)S(1)}, bf16[544,128]{1,0:T(8,128)(2,1)S(1)}, u32[]{:S(2)}, u32[]{:S(2)}) collective-permute-start(bf16[544,128]{1,0:T(8,128)(2,1)S(1)} %pad_maximum_fusion.1.refs_0_), channel_id=1, source_target_pairs={{0,16},{16,0},{1,17},{17,1},{2,18},{18,2},{3,19},{19,3},{4,20},{20... | collective-permute-start | bytes 417800 | tf_op jit(solution)/shard_map/ppermute | solution.py:320
  18.1 0.0 collective-permute-done.1.refs_1_
  18.1 0.5 collective-permute-start.3
  18.6 0.9 %collective-permute-done.4.refs_2_ = bf16[544,128]{1,0:T(8,128)(2,1)S(1)} collective-permute-done((bf16[544,128]{1,0:T(8,128)(2,1)S(1)}, bf16[544,128]{1,0:T(8,128)(2,1)S(1)}, u32[]{:S(2)}, u32[]{:S(2)}) %collective-permute-start.4) | collective-permute-done | bytes 139296 | tf_op jit(solution)/shard_map/ppermute | solution.py:314
  19.5 1.5 %collective-permute-start.6 = (bf16[544,128]{1,0:T(8,128)(2,1)S(1)}, bf16[544,128]{1,0:T(8,128)(2,1)S(1)}, u32[]{:S(2)}, u32[]{:S(2)}) collective-permute-start(bf16[544,128]{1,0:T(8,128)(2,1)S(1)} %collective-permute-done.4.refs_2_), channel_id=1, source_target_pairs={{0,16},{16,0},{1,17},{17,1},{2,18},{18,2},{3,19},{19,3},{4,20},{20... | collective-permute-start | bytes 417800 | tf_op jit(solution)/shard_map/ppermute | solution.py:320
  21.0 2.1 %collective-permute-done.2.refs_2_.refs_3_ = bf16[544,128]{1,0:T(8,128)(2,1)S(1)} collective-permute-done((bf16[544,128]{1,0:T(8,128)(2,1)S(1)}, bf16[544,128]{1,0:T(8,128)(2,1)S(1)}, u32[]{:S(2)}, u32[]{:S(2)}) %collective-permute-start.2) | collective-permute-done | bytes 139296 | tf_op jit(solution)/shard_map/ppermute | solution.py:320
  23.1 3.0 %collective-permute-done.3.refs_3_.refs_4_ = bf16[544,128]{1,0:T(8,128)(2,1)S(1)} collective-permute-done((bf16[544,128]{1,0:T(8,128)(2,1)S(1)}, bf16[544,128]{1,0:T(8,128)(2,1)S(1)}, u32[]{:S(2)}, u32[]{:S(2)}) %collective-permute-start.3) | collective-permute-done | bytes 139296 | tf_op jit(solution)/shard_map/ppermute | solution.py:320
  26.1 0.0 copy-done.1
  26.1 0.0 copy-done.3
  26.1 0.1 shard_map.95
  26.2 0.2 shard_map.96
  26.4 0.0 collective-permute-done.5
  26.4 0.1 pad_maximum_fusion.rows_ref
  26.5 1.2 %collective-permute-done.6.refs_5_ = bf16[544,128]{1,0:T(8,128)(2,1)S(1)} collective-permute-done((bf16[544,128]{1,0:T(8,128)(2,1)S(1)}, bf16[544,128]{1,0:T(8,128)(2,1)S(1)}, u32[]{:S(2)}, u32[]{:S(2)}) %collective-permute-start.6) | collective-permute-done | bytes 139296 | tf_op jit(solution)/shard_map/ppermute | solution.py:320
  27.7 5.3 %shard_map.97 = (bf16[512,1024]{1,0:T(8,128)(2,1)S(1)}, bf16[512,128]{1,0:T(8,128)(2,1)S(1)}, bf16[512,128]{1,0:T(8,128)(2,1)S(1)}, bf16[512,128]{1,0:T(8,128)(2...) custom-call(bf16[512,1024]{1,0:T(8,128)(2,1)S(1)} %pad_maximum_fusion.rows_ref, ...), custom_call_target="tpu_custom_call" | custom-call | flops 2415919104 | bytes 4194304 | tf_op jit(solution)/shard_map/pallas_call | solution.py:364
  32.9 1.6 %collective-permute-start.7 = (bf16[512,128]{1,0:T(8,128)(2,1)S(1)}, bf16[512,128]{1,0:T(8,128)(2,1)S(1)}, u32[]{:S(2)}, u32[]{:S(2)}) collective-permute-start(bf16[512,128]{1,0:T(8,128)(2,1)S(1)} %get-tuple-element.49), channel_id=1, source_target_pairs={{0,16},{16,0},{1,17},{17,1},{2,18},{18,2},{3,19},{19,3},{4,20},{20... | collective-permute-start | bytes 393224 | tf_op jit(solution)/shard_map/ppermute | solution.py:320
  34.5 0.5 collective-permute-start.10
  35.1 0.1 collective-permute-start.9
  35.1 1.6 %collective-permute-start.12 = (bf16[512,128]{1,0:T(8,128)(2,1)S(1)}, bf16[512,128]{1,0:T(8,128)(2,1)S(1)}, u32[]{:S(2)}, u32[]{:S(2)}) collective-permute-start(bf16[512,128]{1,0:T(8,128)(2,1)S(1)} %get-tuple-element.61), channel_id=1, source_target_pairs={{0,16},{16,0},{1,17},{17,1},{2,18},{18,2},{3,19},{19,3},{4,20},{20... | collective-permute-start | bytes 393224 | tf_op jit(solution)/shard_map/ppermute | solution.py:320
  36.7 1.9 %collective-permute-done.7 = bf16[512,128]{1,0:T(8,128)(2,1)S(1)} collective-permute-done((bf16[512,128]{1,0:T(8,128)(2,1)S(1)}, bf16[512,128]{1,0:T(8,128)(2,1)S(1)}, u32[]{:S(2)}, u32[]{:S(2)}) %collective-permute-start.7) | collective-permute-done | bytes 131104 | tf_op jit(solution)/shard_map/ppermute | solution.py:320
  38.7 1.3 %collective-permute-start.8 = (bf16[512,128]{1,0:T(8,128)(2,1)S(1)}, bf16[512,128]{1,0:T(8,128)(2,1)S(1)}, u32[]{:S(2)}, u32[]{:S(2)}) collective-permute-start(bf16[512,128]{1,0:T(8,128)(2,1)S(1)} %add_convert_fusion.2), channel_id=1, source_target_pairs={{4,0},{5,1},{6,2},{7,3},{12,8},{13,9},{14,10},{15,11},{20,16},{21,... | collective-permute-start | bytes 393224 | tf_op jit(solution)/shard_map/ppermute | solution.py:317
  40.0 1.3 %collective-permute-done.10 = bf16[512,128]{1,0:T(8,128)(2,1)S(1)} collective-permute-done((bf16[512,128]{1,0:T(8,128)(2,1)S(1)}, bf16[512,128]{1,0:T(8,128)(2,1)S(1)}, u32[]{:S(2)}, u32[]{:S(2)}) %collective-permute-start.10) | collective-permute-done | bytes 131104 | tf_op jit(solution)/shard_map/ppermute | solution.py:320
  41.4 1.3 %collective-permute-start.11 = (bf16[512,128]{1,0:T(8,128)(2,1)S(1)}, bf16[512,128]{1,0:T(8,128)(2,1)S(1)}, u32[]{:S(2)}, u32[]{:S(2)}) collective-permute-start(bf16[512,128]{1,0:T(8,128)(2,1)S(1)} %add_convert_fusion.1), channel_id=1, source_target_pairs={{2,0},{3,1},{4,2},{5,3},{6,4},{7,5},{10,8},{11,9},{12,10},{13,11},... | collective-permute-start | bytes 393224 | tf_op jit(solution)/shard_map/ppermute | solution.py:317
  42.7 0.8 %shard_map.98 = (bf16[128,2048]{1,0:T(8,128)(2,1)}, bf16[128,2048]{1,0:T(8,128)(2,1)}) custom-call(bf16[512,1024]{1,0:T(8,128)(2,1)S(1)} %get-tuple-element.50.own_ref), custom_call_target="tpu_custom_call" | custom-call | bytes 4194304 | tf_op jit(solution)/shard_map/pallas_call | solution.py:391
  43.5 0.0 collective-permute-done.9.side_ref
  43.5 0.8 %shard_map.99 = (bf16[128,2048]{1,0:T(8,128)(2,1)}, bf16[128,2048]{1,0:T(8,128)(2,1)}) custom-call(bf16[256,1024]{1,0:T(8,128)(2,1)S(1)} %collective-permute-done.9.side_ref, bf16[128,2048]{1,0:T(8,128)(2,1)} %get-tuple-element.51.out_held, bf16[128,2048]{1,0:T(8,128)(2,1)} %get-tuple-element.52.query_grad_held), custom_call_target="tpu_custom_call", output_to_operand_aliasing={{0}: (1, {}), {1}: (2, {})} | custom-call | tf_op jit(solution)/shard_map/pallas_call | solution.py:410
  44.3 5.9 %collective-permute-done.8 = bf16[512,128]{1,0:T(8,128)(2,1)S(1)} collective-permute-done((bf16[512,128]{1,0:T(8,128)(2,1)S(1)}, bf16[512,128]{1,0:T(8,128)(2,1)S(1)}, u32[]{:S(2)}, u32[]{:S(2)}) %collective-permute-start.8) | collective-permute-done | bytes 131104 | tf_op jit(solution)/shard_map/ppermute | solution.py:317
  50.2 0.0 collective-permute-done.12
  50.2 0.0 collective-permute-done.11
  50.2 0.1 add_convert_fusion
  50.3 0.1 collective-permute-start.13
  50.4 1.2 %collective-permute-done.13 = bf16[256,128]{1,0:T(8,128)(2,1)S(1)} collective-permute-done((bf16[256,128]{1,0:T(8,128)(2,1)S(1)}, bf16[256,128]{1,0:T(8,128)(2,1)S(1)}, u32[]{:S(2)}, u32[]{:S(2)}) %collective-permute-start.13) | collective-permute-done | bytes 65568 | tf_op jit(solution)/shard_map/ppermute | solution.py:323
  51.7 0.7 %fusion.2 = (bf16[1,128,256]{2,1,0:T(8,128)(2,1)}, bf16[1,128,256]{2,1,0:T(8,128)(2,1)}) fusion(bf16[256,128]{1,0:T(8,128)(2,1)S(1)} %get-tuple-element.62, bf16[256,128]{1,0:T(8,128)(2,1)S(1)} %get-tuple-element.63), kind=kLoop, calls=%fused_computation.10 | loop fusion | flops 262144 | bytes 262144 | tf_op jit(solution)/shard_map/broadcast_in_dim | solution.py:427
  (6 shorter events, 0.1 us)
Async XLA Ops:
  0.6 0.8 %copy-start.4 = (bf16[1,128,256]{2,1,0:T(8,128)(2,1)S(1)}, bf16[1,128,256]{2,1,0:T(8,128)(2,1)}, u32[]{:S(2)}) copy-start(bf16[1,128,256]{2,1,0:T(8,128)(2,1)} %param.7) | copy-start | bytes 196612
  1.5 0.8 %copy-start.5 = (bf16[1,128,256]{2,1,0:T(8,128)(2,1)S(1)}, bf16[1,128,256]{2,1,0:T(8,128)(2,1)}, u32[]{:S(2)}) copy-start(bf16[1,128,256]{2,1,0:T(8,128)(2,1)} %param.8) | copy-start | bytes 196612
  2.3 0.7 %copy-start.6 = (s32[1,1,4]{2,1,0:T(1,128)S(1)}, s32[1,1,4]{2,1,0:T(1,128)}, u32[]{:S(2)}) copy-start(s32[1,1,4]{2,1,0:T(1,128)} %param.11) | copy-start | bytes 52
  3.0 0.7 %copy-start.7 = (s32[1,128]{1,0:T(1,128)S(1)}, s32[1,128]{1,0:T(1,128)}, u32[]{:S(2)}) copy-start(s32[1,128]{1,0:T(1,128)} %docs_ref.1) | copy-start | bytes 1540
  4.2 2.7 %collective-permute-start = (bf16[272,128]{1,0:T(8,128)(2,1)S(1)}, bf16[272,128]{1,0:T(8,128)(2,1)S(1)}, u32[]{:S(2)}, u32[]{:S(2)}) collective-permute-start(bf16[272,128]{1,0:T(8,128)(2,1)S(1)} %get-tuple-element.34), channel_id=1, source_target_pairs={{0,1},{1,0},{2,3},{3,2},{4,5},{5,4},{6,7},{7,6},{8,9},{9,8},{10,11... | collective-permute-start | bytes 208904 | tf_op jit(solution)/shard_map/ppermute | solution.py:323
  4.7 1.0 %copy-start = (bf16[1,128,2048]{2,1,0:T(8,128)(2,1)S(1)}, bf16[1,128,2048]{2,1,0:T(8,128)(2,1)}, u32[]{:S(2)}) copy-start(bf16[1,128,2048]{2,1,0:T(8,128)(2,1)} %param.6) | copy-start | bytes 1572868
  5.8 1.0 %copy-start.2 = (bf16[1,128,2048]{2,1,0:T(8,128)(2,1)S(1)}, bf16[1,128,2048]{2,1,0:T(8,128)(2,1)}, u32[]{:S(2)}) copy-start(bf16[1,128,2048]{2,1,0:T(8,128)(2,1)} %param.9) | copy-start | bytes 1572868
  6.8 19.3 %copy-start.1 = (bf16[1,128,2048]{2,1,0:T(8,128)(2,1)S(1)}, bf16[1,128,2048]{2,1,0:T(8,128)(2,1)}, u32[]{:S(2)}) copy-start(bf16[1,128,2048]{2,1,0:T(8,128)(2,1)} %param.6) | copy-start | bytes 1572868
  6.8 19.3 %copy-start.3 = (bf16[1,128,2048]{2,1,0:T(8,128)(2,1)S(1)}, bf16[1,128,2048]{2,1,0:T(8,128)(2,1)}, u32[]{:S(2)}) copy-start(bf16[1,128,2048]{2,1,0:T(8,128)(2,1)} %param.9) | copy-start | bytes 1572868
  6.9 19.5 %collective-permute-start.5 = (bf16[256,1024]{1,0:T(8,128)(2,1)S(1)}, bf16[256,1024]{1,0:T(8,128)(2,1)S(1)}, u32[]{:S(2)}, u32[]{:S(2)}) collective-permute-start(bf16[256,1024]{1,0:T(8,128)(2,1)S(1)} %shard_map.94), channel_id=1, source_target_pairs={{0,1},{1,0},{2,3},{3,2},{4,5},{5,4},{6,7},{7,6},{8,9},{9,8},{10,11... | collective-permute-start | bytes 1572872 | tf_op jit(solution)/shard_map/ppermute | solution.py:323
  7.0 11.0 %collective-permute-start.1 = (bf16[544,128]{1,0:T(8,128)(2,1)S(1)}, bf16[544,128]{1,0:T(8,128)(2,1)S(1)}, u32[]{:S(2)}, u32[]{:S(2)}) collective-permute-start(bf16[544,128]{1,0:T(8,128)(2,1)S(1)} %pad_maximum_fusion.1.refs_0_), channel_id=1, source_target_pairs={{0,2},{1,3},{2,4},{3,5},{4,6},{5,7},{8,10},{9,11},{10,12},{11,13},... | collective-permute-start | bytes 417800 | tf_op jit(solution)/shard_map/ppermute | solution.py:314
  12.0 7.5 %collective-permute-start.4 = (bf16[544,128]{1,0:T(8,128)(2,1)S(1)}, bf16[544,128]{1,0:T(8,128)(2,1)S(1)}, u32[]{:S(2)}, u32[]{:S(2)}) collective-permute-start(bf16[544,128]{1,0:T(8,128)(2,1)S(1)} %pad_maximum_fusion.1.refs_0_), channel_id=1, source_target_pairs={{0,4},{1,5},{2,6},{3,7},{8,12},{9,13},{10,14},{11,15},{16,20},{17,... | collective-permute-start | bytes 417800 | tf_op jit(solution)/shard_map/ppermute | solution.py:314
  16.5 6.7 %collective-permute-start.2 = (bf16[544,128]{1,0:T(8,128)(2,1)S(1)}, bf16[544,128]{1,0:T(8,128)(2,1)S(1)}, u32[]{:S(2)}, u32[]{:S(2)}) collective-permute-start(bf16[544,128]{1,0:T(8,128)(2,1)S(1)} %pad_maximum_fusion.1.refs_0_), channel_id=1, source_target_pairs={{0,16},{16,0},{1,17},{17,1},{2,18},{18,2},{3,19},{19,3},{4,20},{20... | collective-permute-start | bytes 417800 | tf_op jit(solution)/shard_map/ppermute | solution.py:320
  18.1 8.1 %collective-permute-start.3 = (bf16[544,128]{1,0:T(8,128)(2,1)S(1)}, bf16[544,128]{1,0:T(8,128)(2,1)S(1)}, u32[]{:S(2)}, u32[]{:S(2)}) collective-permute-start(bf16[544,128]{1,0:T(8,128)(2,1)S(1)} %collective-permute-done.1.refs_1_), channel_id=1, source_target_pairs={{0,16},{16,0},{1,17},{17,1},{2,18},{18,2},{3,19},{19,3},{4,20},{20... | collective-permute-start | bytes 417800 | tf_op jit(solution)/shard_map/ppermute | solution.py:320
  19.5 8.2 %collective-permute-start.6 = (bf16[544,128]{1,0:T(8,128)(2,1)S(1)}, bf16[544,128]{1,0:T(8,128)(2,1)S(1)}, u32[]{:S(2)}, u32[]{:S(2)}) collective-permute-start(bf16[544,128]{1,0:T(8,128)(2,1)S(1)} %collective-permute-done.4.refs_2_), channel_id=1, source_target_pairs={{0,16},{16,0},{1,17},{17,1},{2,18},{18,2},{3,19},{19,3},{4,20},{20... | collective-permute-start | bytes 417800 | tf_op jit(solution)/shard_map/ppermute | solution.py:320
  32.9 5.7 %collective-permute-start.7 = (bf16[512,128]{1,0:T(8,128)(2,1)S(1)}, bf16[512,128]{1,0:T(8,128)(2,1)S(1)}, u32[]{:S(2)}, u32[]{:S(2)}) collective-permute-start(bf16[512,128]{1,0:T(8,128)(2,1)S(1)} %get-tuple-element.49), channel_id=1, source_target_pairs={{0,16},{16,0},{1,17},{17,1},{2,18},{18,2},{3,19},{19,3},{4,20},{20... | collective-permute-start | bytes 393224 | tf_op jit(solution)/shard_map/ppermute | solution.py:320
  34.5 6.8 %collective-permute-start.10 = (bf16[512,128]{1,0:T(8,128)(2,1)S(1)}, bf16[512,128]{1,0:T(8,128)(2,1)S(1)}, u32[]{:S(2)}, u32[]{:S(2)}) collective-permute-start(bf16[512,128]{1,0:T(8,128)(2,1)S(1)} %get-tuple-element.59), channel_id=1, source_target_pairs={{0,16},{16,0},{1,17},{17,1},{2,18},{18,2},{3,19},{19,3},{4,20},{20... | collective-permute-start | bytes 393224 | tf_op jit(solution)/shard_map/ppermute | solution.py:320
  35.1 8.4 %collective-permute-start.9 = (bf16[256,1024]{1,0:T(8,128)(2,1)S(1)}, bf16[256,1024]{1,0:T(8,128)(2,1)S(1)}, u32[]{:S(2)}, u32[]{:S(2)}) collective-permute-start(bf16[256,1024]{1,0:T(8,128)(2,1)S(1)} %slice.15), channel_id=1, source_target_pairs={{0,1},{1,0},{2,3},{3,2},{4,5},{5,4},{6,7},{7,6},{8,9},{9,8},{10,11... | collective-permute-start | bytes 1572872 | tf_op jit(solution)/shard_map/ppermute | solution.py:323
  35.1 15.1 %collective-permute-start.12 = (bf16[512,128]{1,0:T(8,128)(2,1)S(1)}, bf16[512,128]{1,0:T(8,128)(2,1)S(1)}, u32[]{:S(2)}, u32[]{:S(2)}) collective-permute-start(bf16[512,128]{1,0:T(8,128)(2,1)S(1)} %get-tuple-element.61), channel_id=1, source_target_pairs={{0,16},{16,0},{1,17},{17,1},{2,18},{18,2},{3,19},{19,3},{4,20},{20... | collective-permute-start | bytes 393224 | tf_op jit(solution)/shard_map/ppermute | solution.py:320
  38.7 11.5 %collective-permute-start.8 = (bf16[512,128]{1,0:T(8,128)(2,1)S(1)}, bf16[512,128]{1,0:T(8,128)(2,1)S(1)}, u32[]{:S(2)}, u32[]{:S(2)}) collective-permute-start(bf16[512,128]{1,0:T(8,128)(2,1)S(1)} %add_convert_fusion.2), channel_id=1, source_target_pairs={{4,0},{5,1},{6,2},{7,3},{12,8},{13,9},{14,10},{15,11},{20,16},{21,... | collective-permute-start | bytes 393224 | tf_op jit(solution)/shard_map/ppermute | solution.py:317
  41.4 8.9 %collective-permute-start.11 = (bf16[512,128]{1,0:T(8,128)(2,1)S(1)}, bf16[512,128]{1,0:T(8,128)(2,1)S(1)}, u32[]{:S(2)}, u32[]{:S(2)}) collective-permute-start(bf16[512,128]{1,0:T(8,128)(2,1)S(1)} %add_convert_fusion.1), channel_id=1, source_target_pairs={{2,0},{3,1},{4,2},{5,3},{6,4},{7,5},{10,8},{11,9},{12,10},{13,11},... | collective-permute-start | bytes 393224 | tf_op jit(solution)/shard_map/ppermute | solution.py:317
  50.3 1.3 %collective-permute-start.13 = (bf16[256,128]{1,0:T(8,128)(2,1)S(1)}, bf16[256,128]{1,0:T(8,128)(2,1)S(1)}, u32[]{:S(2)}, u32[]{:S(2)}) collective-permute-start(bf16[256,128]{1,0:T(8,128)(2,1)S(1)} %slice.21), channel_id=1, source_target_pairs={{0,1},{1,0},{2,3},{3,2},{4,5},{5,4},{6,7},{7,6},{8,9},{9,8},{10,11... | collective-permute-start | bytes 196616 | tf_op jit(solution)/shard_map/ppermute | solution.py:323

commit v2 on v1

--- a/solution.py
+++ b/solution.py
@@ -327,7 +327,6 @@
         out_shape=[pltpu.VMEM((size, HEAD_SIZE), BF16)] * 2,
         in_specs=[SMEM, VMEM, VMEM, VMEM],
         out_specs=[VMEM, VMEM],
-        compiler_params=SMALL,
     )(swapped[0, 0], key_rows[0], value_rows[0], documents)
     from_side = to_side(payload_side)
 
@@ -338,7 +337,7 @@
             in_specs=[HBM, HBM],
             out_specs=VMEM,
             scratch_shapes=[pltpu.SemaphoreType.DMA((2,))],
-            compiler_params=SMALL,
+            compiler_params=None if other else SMALL,
         )(queries, out_grad)
 
     both = jnp.concatenate([payload, from_side], axis=0)

time: 53 us -> 49.2 us (0.928)
  local copies, waits for them, and re-layouts: 5.11 us -> 0.05 us
  Pallas kernels: 7.79 us -> 9.21 us
    unnamed x16 -> x4, local copies, waits for them, and re-layouts: 5.07 us -> 0.01 us
    pallas_call x2, Pallas kernels: 0.12 us -> 1.1 us  [rows_of(): pl.pallas_call(functools.partial(rows_kernel, other), out_shape=pltpu.VME...]
  transfers between devices with their start and end apart: 14 -> 14, of which waited for: 8 -> 8; matrix products, arithmetic and copies ran while one was open for 0% -> 0% of each run, Pallas kernels for 4% -> 6%
where the time goes in v2:
time: 49.2 us; the launch traced here: 48.7 us
  starting transfers between devices  20.1 us (41%)
  waiting for transfers between devices  17.6 us (36%)
  Pallas kernels  9.21 us (19%)
  other arithmetic  0.91 us (2%)
  between operations  0.83 us (2%)
    ppermute x6, waiting for transfers between devices, to_partner(): return lax.ppermute(block, 'half', [(0, 1), (1, 0)])  9.6 us
    ppermute x2, starting transfers between devices, up(): lax.ppermute(block, 'ctx', [(i, i + 2 * k) for i in range(ranks - 2 * k)])  9.29 us
    ppermute x6, starting transfers between devices, to_partner(): return lax.ppermute(block, 'half', [(0, 1), (1, 0)])  7.29 us
    ppermute x2, waiting for transfers between devices, down(): lax.ppermute(block, 'ctx', [(i + 2 * k, i) for i in range(ranks - 2 * k)])  5.84 us
    pallas_call x1, Pallas kernels, local(): pl.pallas_call(functools.partial(attention_kernel, hops), out_shape=[pltp...  5.26 us
    ppermute x2, starting transfers between devices, down(): lax.ppermute(block, 'ctx', [(i + 2 * k, i) for i in range(ranks - 2 * k)])  2.58 us
    ppermute x4, waiting for transfers between devices, to_side(): return lax.ppermute(block, 'ctx', [(i, i ^ 1) for i in range(ranks)])  1.24 us
    pallas_call x2, Pallas kernels, rows_of(): pl.pallas_call(functools.partial(rows_kernel, other), out_shape=pltpu.VME...  1.1 us
  transfers between devices with their start and end apart: 14, of which 8 were waited for; matrix products, arithmetic and copies ran while one was open for 0% of the time, Pallas kernels for 6%

profile of v2, /device:TPU:0, one launch (start us, length us, event | category | flops | bytes accessed | tf_op | source)
XLA Modules:
  0.0 48.7 jit_solution(17708080425219757407)
XLA Ops:
  0.6 0.0 copy-start
  0.6 0.0 copy-start.1
  0.7 1.0 %shard_map.93 = (bf16[272,128]{1,0:T(8,128)(2,1)S(1)}, bf16[272,128]{1,0:T(8,128)(2,1)S(1)}) custom-call(s32[4]{0:T(128)} %bitcast.19, bf16[128,256]{1,0:T(8,128)(2,1)} %bitcast.17, bf16[128,256]{1,0:T(8,128)(2,1)} %bitcast.18, s32[1,128]{1,0:T(1,128)} %docs_ref.1), custom_call_target="tpu_custom_call" | custom-call | tf_op jit(solution)/shard_map/pallas_call | solution.py:325
  1.7 0.5 %collective-permute-start = (bf16[272,128]{1,0:T(8,128)(2,1)S(1)}, bf16[272,128]{1,0:T(8,128)(2,1)S(1)}, u32[]{:S(2)}, u32[]{:S(2)}) collective-permute-start(bf16[272,128]{1,0:T(8,128)(2,1)S(1)} %get-tuple-element.34), channel_id=1, source_target_pairs={{0,1},{1,0},{2,3},{3,2},{4,5},{5,4},{6,7},{7,6},{8,9},{9,8},{10,11... | collective-permute-start | bytes 208904 | tf_op jit(solution)/shard_map/ppermute | solution.py:323
  2.2 1.0 %shard_map.94 = bf16[256,1024]{1,0:T(8,128)(2,1)S(1)} custom-call(bf16[128,2048]{1,0:T(8,128)(2,1)} %bitcast.11, bf16[128,2048]{1,0:T(8,128)(2,1)} %bitcast.13), custom_call_target="tpu_custom_call" | custom-call | tf_op jit(solution)/shard_map/pallas_call | solution.py:334
  3.2 0.0 collective-permute-done
  3.3 0.3 collective-permute-start.5
  3.5 4.8 %collective-permute-start.1 = (bf16[544,128]{1,0:T(8,128)(2,1)S(1)}, bf16[544,128]{1,0:T(8,128)(2,1)S(1)}, u32[]{:S(2)}, u32[]{:S(2)}) collective-permute-start(bf16[544,128]{1,0:T(8,128)(2,1)S(1)} %pad_maximum_fusion.1.refs_0_), channel_id=1, source_target_pairs={{0,2},{1,3},{2,4},{3,5},{4,6},{5,7},{8,10},{9,11},{10,12},{11,13},... | collective-permute-start | bytes 417800 | tf_op jit(solution)/shard_map/ppermute | solution.py:314
  8.3 4.5 %collective-permute-start.4 = (bf16[544,128]{1,0:T(8,128)(2,1)S(1)}, bf16[544,128]{1,0:T(8,128)(2,1)S(1)}, u32[]{:S(2)}, u32[]{:S(2)}) collective-permute-start(bf16[544,128]{1,0:T(8,128)(2,1)S(1)} %pad_maximum_fusion.1.refs_0_), channel_id=1, source_target_pairs={{0,4},{1,5},{2,6},{3,7},{8,12},{9,13},{10,14},{11,15},{16,20},{17,... | collective-permute-start | bytes 417800 | tf_op jit(solution)/shard_map/ppermute | solution.py:314
  12.8 1.6 %collective-permute-start.2 = (bf16[544,128]{1,0:T(8,128)(2,1)S(1)}, bf16[544,128]{1,0:T(8,128)(2,1)S(1)}, u32[]{:S(2)}, u32[]{:S(2)}) collective-permute-start(bf16[544,128]{1,0:T(8,128)(2,1)S(1)} %pad_maximum_fusion.1.refs_0_), channel_id=1, source_target_pairs={{0,16},{16,0},{1,17},{17,1},{2,18},{18,2},{3,19},{19,3},{4,20},{20... | collective-permute-start | bytes 417800 | tf_op jit(solution)/shard_map/ppermute | solution.py:320
  14.4 0.0 collective-permute-done.1.refs_1_
  14.4 0.5 %collective-permute-start.3 = (bf16[544,128]{1,0:T(8,128)(2,1)S(1)}, bf16[544,128]{1,0:T(8,128)(2,1)S(1)}, u32[]{:S(2)}, u32[]{:S(2)}) collective-permute-start(bf16[544,128]{1,0:T(8,128)(2,1)S(1)} %collective-permute-done.1.refs_1_), channel_id=1, source_target_pairs={{0,16},{16,0},{1,17},{17,1},{2,18},{18,2},{3,19},{19,3},{4,20},{20... | collective-permute-start | bytes 417800 | tf_op jit(solution)/shard_map/ppermute | solution.py:320
  14.9 0.9 %collective-permute-done.4.refs_2_ = bf16[544,128]{1,0:T(8,128)(2,1)S(1)} collective-permute-done((bf16[544,128]{1,0:T(8,128)(2,1)S(1)}, bf16[544,128]{1,0:T(8,128)(2,1)S(1)}, u32[]{:S(2)}, u32[]{:S(2)}) %collective-permute-start.4) | collective-permute-done | bytes 139296 | tf_op jit(solution)/shard_map/ppermute | solution.py:314
  15.9 1.5 %collective-permute-start.6 = (bf16[544,128]{1,0:T(8,128)(2,1)S(1)}, bf16[544,128]{1,0:T(8,128)(2,1)S(1)}, u32[]{:S(2)}, u32[]{:S(2)}) collective-permute-start(bf16[544,128]{1,0:T(8,128)(2,1)S(1)} %collective-permute-done.4.refs_2_), channel_id=1, source_target_pairs={{0,16},{16,0},{1,17},{17,1},{2,18},{18,2},{3,19},{19,3},{4,20},{20... | collective-permute-start | bytes 417800 | tf_op jit(solution)/shard_map/ppermute | solution.py:320
  17.4 2.1 %collective-permute-done.2.refs_2_.refs_3_ = bf16[544,128]{1,0:T(8,128)(2,1)S(1)} collective-permute-done((bf16[544,128]{1,0:T(8,128)(2,1)S(1)}, bf16[544,128]{1,0:T(8,128)(2,1)S(1)}, u32[]{:S(2)}, u32[]{:S(2)}) %collective-permute-start.2) | collective-permute-done | bytes 139296 | tf_op jit(solution)/shard_map/ppermute | solution.py:320
  19.5 3.0 %collective-permute-done.3.refs_3_.refs_4_ = bf16[544,128]{1,0:T(8,128)(2,1)S(1)} collective-permute-done((bf16[544,128]{1,0:T(8,128)(2,1)S(1)}, bf16[544,128]{1,0:T(8,128)(2,1)S(1)}, u32[]{:S(2)}, u32[]{:S(2)}) %collective-permute-start.3) | collective-permute-done | bytes 139296 | tf_op jit(solution)/shard_map/ppermute | solution.py:320
  22.5 0.0 copy-done
  22.5 0.0 copy-done.1
  22.5 0.1 shard_map.95
  22.5 0.2 shard_map.96
  22.8 0.0 collective-permute-done.5
  22.8 0.1 pad_maximum_fusion.rows_ref
  22.8 1.2 %collective-permute-done.6.refs_5_ = bf16[544,128]{1,0:T(8,128)(2,1)S(1)} collective-permute-done((bf16[544,128]{1,0:T(8,128)(2,1)S(1)}, bf16[544,128]{1,0:T(8,128)(2,1)S(1)}, u32[]{:S(2)}, u32[]{:S(2)}) %collective-permute-start.6) | collective-permute-done | bytes 139296 | tf_op jit(solution)/shard_map/ppermute | solution.py:320
  24.1 5.3 %shard_map.97 = (bf16[512,1024]{1,0:T(8,128)(2,1)S(1)}, bf16[512,128]{1,0:T(8,128)(2,1)S(1)}, bf16[512,128]{1,0:T(8,128)(2,1)S(1)}, bf16[512,128]{1,0:T(8,128)(2...) custom-call(bf16[512,1024]{1,0:T(8,128)(2,1)S(1)} %pad_maximum_fusion.rows_ref, ...), custom_call_target="tpu_custom_call" | custom-call | flops 2415919104 | bytes 4194304 | tf_op jit(solution)/shard_map/pallas_call | solution.py:363
  29.3 1.6 %collective-permute-start.7 = (bf16[512,128]{1,0:T(8,128)(2,1)S(1)}, bf16[512,128]{1,0:T(8,128)(2,1)S(1)}, u32[]{:S(2)}, u32[]{:S(2)}) collective-permute-start(bf16[512,128]{1,0:T(8,128)(2,1)S(1)} %get-tuple-element.49), channel_id=1, source_target_pairs={{0,16},{16,0},{1,17},{17,1},{2,18},{18,2},{3,19},{19,3},{4,20},{20... | collective-permute-start | bytes 393224 | tf_op jit(solution)/shard_map/ppermute | solution.py:320
  30.9 0.5 %collective-permute-start.10 = (bf16[512,128]{1,0:T(8,128)(2,1)S(1)}, bf16[512,128]{1,0:T(8,128)(2,1)S(1)}, u32[]{:S(2)}, u32[]{:S(2)}) collective-permute-start(bf16[512,128]{1,0:T(8,128)(2,1)S(1)} %get-tuple-element.59), channel_id=1, source_target_pairs={{0,16},{16,0},{1,17},{17,1},{2,18},{18,2},{3,19},{19,3},{4,20},{20... | collective-permute-start | bytes 393224 | tf_op jit(solution)/shard_map/ppermute | solution.py:320
  31.5 0.1 collective-permute-start.9
  31.5 1.6 %collective-permute-start.12 = (bf16[512,128]{1,0:T(8,128)(2,1)S(1)}, bf16[512,128]{1,0:T(8,128)(2,1)S(1)}, u32[]{:S(2)}, u32[]{:S(2)}) collective-permute-start(bf16[512,128]{1,0:T(8,128)(2,1)S(1)} %get-tuple-element.61), channel_id=1, source_target_pairs={{0,16},{16,0},{1,17},{17,1},{2,18},{18,2},{3,19},{19,3},{4,20},{20... | collective-permute-start | bytes 393224 | tf_op jit(solution)/shard_map/ppermute | solution.py:320
  33.1 2.0 %collective-permute-done.7 = bf16[512,128]{1,0:T(8,128)(2,1)S(1)} collective-permute-done((bf16[512,128]{1,0:T(8,128)(2,1)S(1)}, bf16[512,128]{1,0:T(8,128)(2,1)S(1)}, u32[]{:S(2)}, u32[]{:S(2)}) %collective-permute-start.7) | collective-permute-done | bytes 131104 | tf_op jit(solution)/shard_map/ppermute | solution.py:320
  35.2 1.3 %collective-permute-start.8 = (bf16[512,128]{1,0:T(8,128)(2,1)S(1)}, bf16[512,128]{1,0:T(8,128)(2,1)S(1)}, u32[]{:S(2)}, u32[]{:S(2)}) collective-permute-start(bf16[512,128]{1,0:T(8,128)(2,1)S(1)} %add_convert_fusion.2), channel_id=1, source_target_pairs={{4,0},{5,1},{6,2},{7,3},{12,8},{13,9},{14,10},{15,11},{20,16},{21,... | collective-permute-start | bytes 393224 | tf_op jit(solution)/shard_map/ppermute | solution.py:317
  36.5 1.2 %collective-permute-done.10 = bf16[512,128]{1,0:T(8,128)(2,1)S(1)} collective-permute-done((bf16[512,128]{1,0:T(8,128)(2,1)S(1)}, bf16[512,128]{1,0:T(8,128)(2,1)S(1)}, u32[]{:S(2)}, u32[]{:S(2)}) %collective-permute-start.10) | collective-permute-done | bytes 131104 | tf_op jit(solution)/shard_map/ppermute | solution.py:320
  37.8 1.3 %collective-permute-start.11 = (bf16[512,128]{1,0:T(8,128)(2,1)S(1)}, bf16[512,128]{1,0:T(8,128)(2,1)S(1)}, u32[]{:S(2)}, u32[]{:S(2)}) collective-permute-start(bf16[512,128]{1,0:T(8,128)(2,1)S(1)} %add_convert_fusion.1), channel_id=1, source_target_pairs={{2,0},{3,1},{4,2},{5,3},{6,4},{7,5},{10,8},{11,9},{12,10},{13,11},... | collective-permute-start | bytes 393224 | tf_op jit(solution)/shard_map/ppermute | solution.py:317
  39.1 0.8 %shard_map.98 = (bf16[128,2048]{1,0:T(8,128)(2,1)}, bf16[128,2048]{1,0:T(8,128)(2,1)}) custom-call(bf16[512,1024]{1,0:T(8,128)(2,1)S(1)} %get-tuple-element.50.own_ref), custom_call_target="tpu_custom_call" | custom-call | bytes 4194304 | tf_op jit(solution)/shard_map/pallas_call | solution.py:390
  39.9 0.0 collective-permute-done.9.side_ref
  39.9 0.8 %shard_map.99 = (bf16[128,2048]{1,0:T(8,128)(2,1)}, bf16[128,2048]{1,0:T(8,128)(2,1)}) custom-call(bf16[256,1024]{1,0:T(8,128)(2,1)S(1)} %collective-permute-done.9.side_ref, bf16[128,2048]{1,0:T(8,128)(2,1)} %get-tuple-element.51.out_held, bf16[128,2048]{1,0:T(8,128)(2,1)} %get-tuple-element.52.query_grad_held), custom_call_target="tpu_custom_call", output_to_operand_aliasing={{0}: (1, {}), {1}: (2, {})} | custom-call | tf_op jit(solution)/shard_map/pallas_call | solution.py:409
  40.8 5.8 %collective-permute-done.8 = bf16[512,128]{1,0:T(8,128)(2,1)S(1)} collective-permute-done((bf16[512,128]{1,0:T(8,128)(2,1)S(1)}, bf16[512,128]{1,0:T(8,128)(2,1)S(1)}, u32[]{:S(2)}, u32[]{:S(2)}) %collective-permute-start.8) | collective-permute-done | bytes 131104 | tf_op jit(solution)/shard_map/ppermute | solution.py:317
  46.6 0.0 collective-permute-done.12
  46.6 0.0 collective-permute-done.11
  46.6 0.1 add_convert_fusion
  46.7 0.1 collective-permute-start.13
  46.8 1.2 %collective-permute-done.13 = bf16[256,128]{1,0:T(8,128)(2,1)S(1)} collective-permute-done((bf16[256,128]{1,0:T(8,128)(2,1)S(1)}, bf16[256,128]{1,0:T(8,128)(2,1)S(1)}, u32[]{:S(2)}, u32[]{:S(2)}) %collective-permute-start.13) | collective-permute-done | bytes 65568 | tf_op jit(solution)/shard_map/ppermute | solution.py:323
  48.0 0.7 %fusion.2 = (bf16[1,128,256]{2,1,0:T(8,128)(2,1)}, bf16[1,128,256]{2,1,0:T(8,128)(2,1)}) fusion(bf16[256,128]{1,0:T(8,128)(2,1)S(1)} %get-tuple-element.62, bf16[256,128]{1,0:T(8,128)(2,1)S(1)} %get-tuple-element.63), kind=kLoop, calls=%fused_computation.10 | loop fusion | flops 262144 | bytes 262144 | tf_op jit(solution)/shard_map/broadcast_in_dim | solution.py:426
  (6 shorter events, 0.1 us)
Async XLA Ops:
  0.6 21.8 %copy-start = (bf16[1,128,2048]{2,1,0:T(8,128)(2,1)S(1)}, bf16[1,128,2048]{2,1,0:T(8,128)(2,1)}, u32[]{:S(2)}) copy-start(bf16[1,128,2048]{2,1,0:T(8,128)(2,1)} %param.6) | copy-start | bytes 1572868
  0.6 21.8 %copy-start.1 = (bf16[1,128,2048]{2,1,0:T(8,128)(2,1)S(1)}, bf16[1,128,2048]{2,1,0:T(8,128)(2,1)}, u32[]{:S(2)}) copy-start(bf16[1,128,2048]{2,1,0:T(8,128)(2,1)} %param.9) | copy-start | bytes 1572868
  1.7 1.6 %collective-permute-start = (bf16[272,128]{1,0:T(8,128)(2,1)S(1)}, bf16[272,128]{1,0:T(8,128)(2,1)S(1)}, u32[]{:S(2)}, u32[]{:S(2)}) collective-permute-start(bf16[272,128]{1,0:T(8,128)(2,1)S(1)} %get-tuple-element.34), channel_id=1, source_target_pairs={{0,1},{1,0},{2,3},{3,2},{4,5},{5,4},{6,7},{7,6},{8,9},{9,8},{10,11... | collective-permute-start | bytes 208904 | tf_op jit(solution)/shard_map/ppermute | solution.py:323
  3.3 19.5 %collective-permute-start.5 = (bf16[256,1024]{1,0:T(8,128)(2,1)S(1)}, bf16[256,1024]{1,0:T(8,128)(2,1)S(1)}, u32[]{:S(2)}, u32[]{:S(2)}) collective-permute-start(bf16[256,1024]{1,0:T(8,128)(2,1)S(1)} %shard_map.94), channel_id=1, source_target_pairs={{0,1},{1,0},{2,3},{3,2},{4,5},{5,4},{6,7},{7,6},{8,9},{9,8},{10,11... | collective-permute-start | bytes 1572872 | tf_op jit(solution)/shard_map/ppermute | solution.py:323
  3.5 10.9 %collective-permute-start.1 = (bf16[544,128]{1,0:T(8,128)(2,1)S(1)}, bf16[544,128]{1,0:T(8,128)(2,1)S(1)}, u32[]{:S(2)}, u32[]{:S(2)}) collective-permute-start(bf16[544,128]{1,0:T(8,128)(2,1)S(1)} %pad_maximum_fusion.1.refs_0_), channel_id=1, source_target_pairs={{0,2},{1,3},{2,4},{3,5},{4,6},{5,7},{8,10},{9,11},{10,12},{11,13},... | collective-permute-start | bytes 417800 | tf_op jit(solution)/shard_map/ppermute | solution.py:314
  8.3 7.5 %collective-permute-start.4 = (bf16[544,128]{1,0:T(8,128)(2,1)S(1)}, bf16[544,128]{1,0:T(8,128)(2,1)S(1)}, u32[]{:S(2)}, u32[]{:S(2)}) collective-permute-start(bf16[544,128]{1,0:T(8,128)(2,1)S(1)} %pad_maximum_fusion.1.refs_0_), channel_id=1, source_target_pairs={{0,4},{1,5},{2,6},{3,7},{8,12},{9,13},{10,14},{11,15},{16,20},{17,... | collective-permute-start | bytes 417800 | tf_op jit(solution)/shard_map/ppermute | solution.py:314
  12.8 6.7 %collective-permute-start.2 = (bf16[544,128]{1,0:T(8,128)(2,1)S(1)}, bf16[544,128]{1,0:T(8,128)(2,1)S(1)}, u32[]{:S(2)}, u32[]{:S(2)}) collective-permute-start(bf16[544,128]{1,0:T(8,128)(2,1)S(1)} %pad_maximum_fusion.1.refs_0_), channel_id=1, source_target_pairs={{0,16},{16,0},{1,17},{17,1},{2,18},{18,2},{3,19},{19,3},{4,20},{20... | collective-permute-start | bytes 417800 | tf_op jit(solution)/shard_map/ppermute | solution.py:320
  14.4 8.0 %collective-permute-start.3 = (bf16[544,128]{1,0:T(8,128)(2,1)S(1)}, bf16[544,128]{1,0:T(8,128)(2,1)S(1)}, u32[]{:S(2)}, u32[]{:S(2)}) collective-permute-start(bf16[544,128]{1,0:T(8,128)(2,1)S(1)} %collective-permute-done.1.refs_1_), channel_id=1, source_target_pairs={{0,16},{16,0},{1,17},{17,1},{2,18},{18,2},{3,19},{19,3},{4,20},{20... | collective-permute-start | bytes 417800 | tf_op jit(solution)/shard_map/ppermute | solution.py:320
  15.9 8.2 %collective-permute-start.6 = (bf16[544,128]{1,0:T(8,128)(2,1)S(1)}, bf16[544,128]{1,0:T(8,128)(2,1)S(1)}, u32[]{:S(2)}, u32[]{:S(2)}) collective-permute-start(bf16[544,128]{1,0:T(8,128)(2,1)S(1)} %collective-permute-done.4.refs_2_), channel_id=1, source_target_pairs={{0,16},{16,0},{1,17},{17,1},{2,18},{18,2},{3,19},{19,3},{4,20},{20... | collective-permute-start | bytes 417800 | tf_op jit(solution)/shard_map/ppermute | solution.py:320
  29.3 5.8 %collective-permute-start.7 = (bf16[512,128]{1,0:T(8,128)(2,1)S(1)}, bf16[512,128]{1,0:T(8,128)(2,1)S(1)}, u32[]{:S(2)}, u32[]{:S(2)}) collective-permute-start(bf16[512,128]{1,0:T(8,128)(2,1)S(1)} %get-tuple-element.49), channel_id=1, source_target_pairs={{0,16},{16,0},{1,17},{17,1},{2,18},{18,2},{3,19},{19,3},{4,20},{20... | collective-permute-start | bytes 393224 | tf_op jit(solution)/shard_map/ppermute | solution.py:320
  30.9 6.8 %collective-permute-start.10 = (bf16[512,128]{1,0:T(8,128)(2,1)S(1)}, bf16[512,128]{1,0:T(8,128)(2,1)S(1)}, u32[]{:S(2)}, u32[]{:S(2)}) collective-permute-start(bf16[512,128]{1,0:T(8,128)(2,1)S(1)} %get-tuple-element.59), channel_id=1, source_target_pairs={{0,16},{16,0},{1,17},{17,1},{2,18},{18,2},{3,19},{19,3},{4,20},{20... | collective-permute-start | bytes 393224 | tf_op jit(solution)/shard_map/ppermute | solution.py:320
  31.5 8.5 %collective-permute-start.9 = (bf16[256,1024]{1,0:T(8,128)(2,1)S(1)}, bf16[256,1024]{1,0:T(8,128)(2,1)S(1)}, u32[]{:S(2)}, u32[]{:S(2)}) collective-permute-start(bf16[256,1024]{1,0:T(8,128)(2,1)S(1)} %slice.15), channel_id=1, source_target_pairs={{0,1},{1,0},{2,3},{3,2},{4,5},{5,4},{6,7},{7,6},{8,9},{9,8},{10,11... | collective-permute-start | bytes 1572872 | tf_op jit(solution)/shard_map/ppermute | solution.py:323
  31.5 15.1 %collective-permute-start.12 = (bf16[512,128]{1,0:T(8,128)(2,1)S(1)}, bf16[512,128]{1,0:T(8,128)(2,1)S(1)}, u32[]{:S(2)}, u32[]{:S(2)}) collective-permute-start(bf16[512,128]{1,0:T(8,128)(2,1)S(1)} %get-tuple-element.61), channel_id=1, source_target_pairs={{0,16},{16,0},{1,17},{17,1},{2,18},{18,2},{3,19},{19,3},{4,20},{20... | collective-permute-start | bytes 393224 | tf_op jit(solution)/shard_map/ppermute | solution.py:320
  35.2 11.4 %collective-permute-start.8 = (bf16[512,128]{1,0:T(8,128)(2,1)S(1)}, bf16[512,128]{1,0:T(8,128)(2,1)S(1)}, u32[]{:S(2)}, u32[]{:S(2)}) collective-permute-start(bf16[512,128]{1,0:T(8,128)(2,1)S(1)} %add_convert_fusion.2), channel_id=1, source_target_pairs={{4,0},{5,1},{6,2},{7,3},{12,8},{13,9},{14,10},{15,11},{20,16},{21,... | collective-permute-start | bytes 393224 | tf_op jit(solution)/shard_map/ppermute | solution.py:317
  37.8 8.8 %collective-permute-start.11 = (bf16[512,128]{1,0:T(8,128)(2,1)S(1)}, bf16[512,128]{1,0:T(8,128)(2,1)S(1)}, u32[]{:S(2)}, u32[]{:S(2)}) collective-permute-start(bf16[512,128]{1,0:T(8,128)(2,1)S(1)} %add_convert_fusion.1), channel_id=1, source_target_pairs={{2,0},{3,1},{4,2},{5,3},{6,4},{7,5},{10,8},{11,9},{12,10},{13,11},... | collective-permute-start | bytes 393224 | tf_op jit(solution)/shard_map/ppermute | solution.py:317
  46.7 1.3 %collective-permute-start.13 = (bf16[256,128]{1,0:T(8,128)(2,1)S(1)}, bf16[256,128]{1,0:T(8,128)(2,1)S(1)}, u32[]{:S(2)}, u32[]{:S(2)}) collective-permute-start(bf16[256,128]{1,0:T(8,128)(2,1)S(1)} %slice.21), channel_id=1, source_target_pairs={{0,1},{1,0},{2,3},{3,2},{4,5},{5,4},{6,7},{7,6},{8,9},{9,8},{10,11... | collective-permute-start | bytes 196616 | tf_op jit(solution)/shard_map/ppermute | solution.py:323

commit v3 on v2

--- a/solution.py
+++ b/solution.py
@@ -233,13 +233,24 @@
             + block * per_block
             + lax.rem(lax.broadcasted_iota(I32, (1, HEAD_SIZE), 1), per_block)
         )
-        allowed = (key_place >= row_first) & (key_place <= row_last)
+        early = (chunks - 1) * rows
+        allowed = [
+            (slice(early, None), (key_place[early:] >= row_first) & (key_place[early:] <= row_last))
+        ]
+        if early:
+            allowed.insert(0, (slice(0, early), key_place[:early] >= row_first))
         scores = jnp.concatenate(
             [
-                jnp.where(allowed, scores[:, lane : lane + HEAD_SIZE], NEG)
-                for lane in range(0, lanes, HEAD_SIZE)
+                jnp.concatenate(
+                    [
+                        jnp.where(keep, scores[part, lane : lane + HEAD_SIZE], NEG)
+                        for lane in range(0, lanes, HEAD_SIZE)
+                    ],
+                    axis=1,
+                )
+                for part, keep in allowed
             ],
-            axis=1,
+            axis=0,
         )
         peak = jnp.max(scores, axis=0, keepdims=True)
         powers = jnp.exp2((scores - peak) * factor)
@@ -291,13 +302,16 @@
             flags = meta_of(homes[k], who)
             for block in range(NBLK):
                 at = pl.ds(base + block * per_block, per_block)
-                mask = jnp.broadcast_to(flags[block : block + 1, :], (per_block, HEAD_SIZE)) > 0.5
+                mask = (
+                    jnp.broadcast_to(flags[block : block + 1, :], (per_block, HEAD_SIZE)).astype(BF16)
+                    > 0.5
+                )
                 for which, total, gain in ((0, key_total, scale), (1, value_total, 1.0)):
                     part = (2 * who + which) * rows + block * per_block
-                    first = total[0, at, :] * gain
-                    second = total[1, at, :] * gain
-                    home_outs[k][part : part + per_block, :] = jnp.where(mask, second, first).astype(BF16)
-                    away_outs[k][part : part + per_block, :] = jnp.where(mask, first, second).astype(BF16)
+                    first = (total[0, at, :] * gain).astype(BF16)
+                    second = (total[1, at, :] * gain).astype(BF16)
+                    home_outs[k][part : part + per_block, :] = jnp.where(mask, second, first)
+                    away_outs[k][part : part + per_block, :] = jnp.where(mask, first, second)
 
 
 def local(queries, key_rows, value_rows, out_grad, documents, swapped):

time: 49.2 us -> 48.4 us (0.984)
  waiting for transfers between devices: 17.6 us -> 16.4 us
    ppermute x2, waiting for transfers between devices: 5.84 us -> 4.58 us  [down(): lax.ppermute(block, 'ctx', [(i + 2 * k, i) for i in range(ranks - 2 * k)])]
where the time goes in v3:
time: 48.4 us; the launch traced here: 47.5 us
  starting transfers between devices  20.1 us (42%)
  waiting for transfers between devices  16.4 us (34%)
  Pallas kernels  9.25 us (19%)
  other arithmetic  0.91 us (2%)
  between operations  0.83 us (2%)
    ppermute x6, waiting for transfers between devices, to_partner(): return lax.ppermute(block, 'half', [(0, 1), (1, 0)])  9.6 us
    ppermute x2, starting transfers between devices, up(): lax.ppermute(block, 'ctx', [(i, i + 2 * k) for i in range(ranks - 2 * k)])  9.29 us
    ppermute x6, starting transfers between devices, to_partner(): return lax.ppermute(block, 'half', [(0, 1), (1, 0)])  7.29 us
    pallas_call x1, Pallas kernels, local(): pl.pallas_call(functools.partial(attention_kernel, hops), out_shape=[pltp...  5.3 us
    ppermute x2, waiting for transfers between devices, down(): lax.ppermute(block, 'ctx', [(i + 2 * k, i) for i in range(ranks - 2 * k)])  4.58 us
    ppermute x2, starting transfers between devices, down(): lax.ppermute(block, 'ctx', [(i + 2 * k, i) for i in range(ranks - 2 * k)])  2.58 us
    ppermute x4, waiting for transfers between devices, to_side(): return lax.ppermute(block, 'ctx', [(i, i ^ 1) for i in range(ranks)])  1.24 us
    pallas_call x2, Pallas kernels, rows_of(): pl.pallas_call(functools.partial(rows_kernel, other), out_shape=pltpu.VME...  1.1 us
  transfers between devices with their start and end apart: 14, of which 8 were waited for; matrix products, arithmetic and copies ran while one was open for 0% of the time, Pallas kernels for 6%

profile of v3, /device:TPU:0, one launch (start us, length us, event | category | flops | bytes accessed | tf_op | source)
XLA Modules:
  0.0 47.5 jit_solution(13836290028727813001)
XLA Ops:
  0.6 0.0 copy-start
  0.6 0.0 copy-start.1
  0.7 1.0 %shard_map.93 = (bf16[272,128]{1,0:T(8,128)(2,1)S(1)}, bf16[272,128]{1,0:T(8,128)(2,1)S(1)}) custom-call(s32[4]{0:T(128)} %bitcast.19, bf16[128,256]{1,0:T(8,128)(2,1)} %bitcast.17, bf16[128,256]{1,0:T(8,128)(2,1)} %bitcast.18, s32[1,128]{1,0:T(1,128)} %docs_ref.1), custom_call_target="tpu_custom_call" | custom-call | tf_op jit(solution)/shard_map/pallas_call | solution.py:339
  1.7 0.5 %collective-permute-start = (bf16[272,128]{1,0:T(8,128)(2,1)S(1)}, bf16[272,128]{1,0:T(8,128)(2,1)S(1)}, u32[]{:S(2)}, u32[]{:S(2)}) collective-permute-start(bf16[272,128]{1,0:T(8,128)(2,1)S(1)} %get-tuple-element.34), channel_id=1, source_target_pairs={{0,1},{1,0},{2,3},{3,2},{4,5},{5,4},{6,7},{7,6},{8,9},{9,8},{10,11... | collective-permute-start | bytes 208904 | tf_op jit(solution)/shard_map/ppermute | solution.py:337
  2.2 1.0 %shard_map.94 = bf16[256,1024]{1,0:T(8,128)(2,1)S(1)} custom-call(bf16[128,2048]{1,0:T(8,128)(2,1)} %bitcast.11, bf16[128,2048]{1,0:T(8,128)(2,1)} %bitcast.13), custom_call_target="tpu_custom_call" | custom-call | tf_op jit(solution)/shard_map/pallas_call | solution.py:348
  3.2 0.0 collective-permute-done
  3.3 0.3 collective-permute-start.5
  3.5 4.8 %collective-permute-start.1 = (bf16[544,128]{1,0:T(8,128)(2,1)S(1)}, bf16[544,128]{1,0:T(8,128)(2,1)S(1)}, u32[]{:S(2)}, u32[]{:S(2)}) collective-permute-start(bf16[544,128]{1,0:T(8,128)(2,1)S(1)} %pad_maximum_fusion.1.refs_0_), channel_id=1, source_target_pairs={{0,2},{1,3},{2,4},{3,5},{4,6},{5,7},{8,10},{9,11},{10,12},{11,13},... | collective-permute-start | bytes 417800 | tf_op jit(solution)/shard_map/ppermute | solution.py:328
  8.3 4.5 %collective-permute-start.4 = (bf16[544,128]{1,0:T(8,128)(2,1)S(1)}, bf16[544,128]{1,0:T(8,128)(2,1)S(1)}, u32[]{:S(2)}, u32[]{:S(2)}) collective-permute-start(bf16[544,128]{1,0:T(8,128)(2,1)S(1)} %pad_maximum_fusion.1.refs_0_), channel_id=1, source_target_pairs={{0,4},{1,5},{2,6},{3,7},{8,12},{9,13},{10,14},{11,15},{16,20},{17,... | collective-permute-start | bytes 417800 | tf_op jit(solution)/shard_map/ppermute | solution.py:328
  12.8 1.6 %collective-permute-start.2 = (bf16[544,128]{1,0:T(8,128)(2,1)S(1)}, bf16[544,128]{1,0:T(8,128)(2,1)S(1)}, u32[]{:S(2)}, u32[]{:S(2)}) collective-permute-start(bf16[544,128]{1,0:T(8,128)(2,1)S(1)} %pad_maximum_fusion.1.refs_0_), channel_id=1, source_target_pairs={{0,16},{16,0},{1,17},{17,1},{2,18},{18,2},{3,19},{19,3},{4,20},{20... | collective-permute-start | bytes 417800 | tf_op jit(solution)/shard_map/ppermute | solution.py:334
  14.4 0.0 collective-permute-done.1.refs_1_
  14.4 0.5 %collective-permute-start.3 = (bf16[544,128]{1,0:T(8,128)(2,1)S(1)}, bf16[544,128]{1,0:T(8,128)(2,1)S(1)}, u32[]{:S(2)}, u32[]{:S(2)}) collective-permute-start(bf16[544,128]{1,0:T(8,128)(2,1)S(1)} %collective-permute-done.1.refs_1_), channel_id=1, source_target_pairs={{0,16},{16,0},{1,17},{17,1},{2,18},{18,2},{3,19},{19,3},{4,20},{20... | collective-permute-start | bytes 417800 | tf_op jit(solution)/shard_map/ppermute | solution.py:334
  14.9 0.9 %collective-permute-done.4.refs_2_ = bf16[544,128]{1,0:T(8,128)(2,1)S(1)} collective-permute-done((bf16[544,128]{1,0:T(8,128)(2,1)S(1)}, bf16[544,128]{1,0:T(8,128)(2,1)S(1)}, u32[]{:S(2)}, u32[]{:S(2)}) %collective-permute-start.4) | collective-permute-done | bytes 139296 | tf_op jit(solution)/shard_map/ppermute | solution.py:328
  15.9 1.5 %collective-permute-start.6 = (bf16[544,128]{1,0:T(8,128)(2,1)S(1)}, bf16[544,128]{1,0:T(8,128)(2,1)S(1)}, u32[]{:S(2)}, u32[]{:S(2)}) collective-permute-start(bf16[544,128]{1,0:T(8,128)(2,1)S(1)} %collective-permute-done.4.refs_2_), channel_id=1, source_target_pairs={{0,16},{16,0},{1,17},{17,1},{2,18},{18,2},{3,19},{19,3},{4,20},{20... | collective-permute-start | bytes 417800 | tf_op jit(solution)/shard_map/ppermute | solution.py:334
  17.4 2.1 %collective-permute-done.2.refs_2_.refs_3_ = bf16[544,128]{1,0:T(8,128)(2,1)S(1)} collective-permute-done((bf16[544,128]{1,0:T(8,128)(2,1)S(1)}, bf16[544,128]{1,0:T(8,128)(2,1)S(1)}, u32[]{:S(2)}, u32[]{:S(2)}) %collective-permute-start.2) | collective-permute-done | bytes 139296 | tf_op jit(solution)/shard_map/ppermute | solution.py:334
  19.5 3.0 %collective-permute-done.3.refs_3_.refs_4_ = bf16[544,128]{1,0:T(8,128)(2,1)S(1)} collective-permute-done((bf16[544,128]{1,0:T(8,128)(2,1)S(1)}, bf16[544,128]{1,0:T(8,128)(2,1)S(1)}, u32[]{:S(2)}, u32[]{:S(2)}) %collective-permute-start.3) | collective-permute-done | bytes 139296 | tf_op jit(solution)/shard_map/ppermute | solution.py:334
  22.5 0.0 copy-done
  22.5 0.0 copy-done.1
  22.5 0.1 shard_map.95
  22.5 0.2 shard_map.96
  22.8 0.0 collective-permute-done.5
  22.8 0.1 pad_maximum_fusion.rows_ref
  22.8 1.2 %collective-permute-done.6.refs_5_ = bf16[544,128]{1,0:T(8,128)(2,1)S(1)} collective-permute-done((bf16[544,128]{1,0:T(8,128)(2,1)S(1)}, bf16[544,128]{1,0:T(8,128)(2,1)S(1)}, u32[]{:S(2)}, u32[]{:S(2)}) %collective-permute-start.6) | collective-permute-done | bytes 139296 | tf_op jit(solution)/shard_map/ppermute | solution.py:334
  24.1 5.3 %shard_map.97 = (bf16[512,1024]{1,0:T(8,128)(2,1)S(1)}, bf16[512,128]{1,0:T(8,128)(2,1)S(1)}, bf16[512,128]{1,0:T(8,128)(2,1)S(1)}, bf16[512,128]{1,0:T(8,128)(2...) custom-call(bf16[512,1024]{1,0:T(8,128)(2,1)S(1)} %pad_maximum_fusion.rows_ref, ...), custom_call_target="tpu_custom_call" | custom-call | flops 2415919104 | bytes 4194304 | tf_op jit(solution)/shard_map/pallas_call | solution.py:377
  29.4 1.6 %collective-permute-start.7 = (bf16[512,128]{1,0:T(8,128)(2,1)S(1)}, bf16[512,128]{1,0:T(8,128)(2,1)S(1)}, u32[]{:S(2)}, u32[]{:S(2)}) collective-permute-start(bf16[512,128]{1,0:T(8,128)(2,1)S(1)} %get-tuple-element.49), channel_id=1, source_target_pairs={{0,16},{16,0},{1,17},{17,1},{2,18},{18,2},{3,19},{19,3},{4,20},{20... | collective-permute-start | bytes 393224 | tf_op jit(solution)/shard_map/ppermute | solution.py:334
  31.0 0.5 %collective-permute-start.10 = (bf16[512,128]{1,0:T(8,128)(2,1)S(1)}, bf16[512,128]{1,0:T(8,128)(2,1)S(1)}, u32[]{:S(2)}, u32[]{:S(2)}) collective-permute-start(bf16[512,128]{1,0:T(8,128)(2,1)S(1)} %get-tuple-element.59), channel_id=1, source_target_pairs={{0,16},{16,0},{1,17},{17,1},{2,18},{18,2},{3,19},{19,3},{4,20},{20... | collective-permute-start | bytes 393224 | tf_op jit(solution)/shard_map/ppermute | solution.py:334
  31.5 0.1 collective-permute-start.9
  31.6 1.6 %collective-permute-start.12 = (bf16[512,128]{1,0:T(8,128)(2,1)S(1)}, bf16[512,128]{1,0:T(8,128)(2,1)S(1)}, u32[]{:S(2)}, u32[]{:S(2)}) collective-permute-start(bf16[512,128]{1,0:T(8,128)(2,1)S(1)} %get-tuple-element.61), channel_id=1, source_target_pairs={{0,16},{16,0},{1,17},{17,1},{2,18},{18,2},{3,19},{19,3},{4,20},{20... | collective-permute-start | bytes 393224 | tf_op jit(solution)/shard_map/ppermute | solution.py:334
  33.2 2.0 %collective-permute-done.7 = bf16[512,128]{1,0:T(8,128)(2,1)S(1)} collective-permute-done((bf16[512,128]{1,0:T(8,128)(2,1)S(1)}, bf16[512,128]{1,0:T(8,128)(2,1)S(1)}, u32[]{:S(2)}, u32[]{:S(2)}) %collective-permute-start.7) | collective-permute-done | bytes 131104 | tf_op jit(solution)/shard_map/ppermute | solution.py:334
  35.3 1.3 %collective-permute-start.8 = (bf16[512,128]{1,0:T(8,128)(2,1)S(1)}, bf16[512,128]{1,0:T(8,128)(2,1)S(1)}, u32[]{:S(2)}, u32[]{:S(2)}) collective-permute-start(bf16[512,128]{1,0:T(8,128)(2,1)S(1)} %add_convert_fusion.2), channel_id=1, source_target_pairs={{4,0},{5,1},{6,2},{7,3},{12,8},{13,9},{14,10},{15,11},{20,16},{21,... | collective-permute-start | bytes 393224 | tf_op jit(solution)/shard_map/ppermute | solution.py:331
  36.6 1.2 %collective-permute-done.10 = bf16[512,128]{1,0:T(8,128)(2,1)S(1)} collective-permute-done((bf16[512,128]{1,0:T(8,128)(2,1)S(1)}, bf16[512,128]{1,0:T(8,128)(2,1)S(1)}, u32[]{:S(2)}, u32[]{:S(2)}) %collective-permute-start.10) | collective-permute-done | bytes 131104 | tf_op jit(solution)/shard_map/ppermute | solution.py:334
  37.8 1.3 %collective-permute-start.11 = (bf16[512,128]{1,0:T(8,128)(2,1)S(1)}, bf16[512,128]{1,0:T(8,128)(2,1)S(1)}, u32[]{:S(2)}, u32[]{:S(2)}) collective-permute-start(bf16[512,128]{1,0:T(8,128)(2,1)S(1)} %add_convert_fusion.1), channel_id=1, source_target_pairs={{2,0},{3,1},{4,2},{5,3},{6,4},{7,5},{10,8},{11,9},{12,10},{13,11},... | collective-permute-start | bytes 393224 | tf_op jit(solution)/shard_map/ppermute | solution.py:331
  39.1 0.8 %shard_map.98 = (bf16[128,2048]{1,0:T(8,128)(2,1)}, bf16[128,2048]{1,0:T(8,128)(2,1)}) custom-call(bf16[512,1024]{1,0:T(8,128)(2,1)S(1)} %get-tuple-element.50.own_ref), custom_call_target="tpu_custom_call" | custom-call | bytes 4194304 | tf_op jit(solution)/shard_map/pallas_call | solution.py:404
  40.0 0.0 collective-permute-done.9.side_ref
  40.0 0.8 %shard_map.99 = (bf16[128,2048]{1,0:T(8,128)(2,1)}, bf16[128,2048]{1,0:T(8,128)(2,1)}) custom-call(bf16[256,1024]{1,0:T(8,128)(2,1)S(1)} %collective-permute-done.9.side_ref, bf16[128,2048]{1,0:T(8,128)(2,1)} %get-tuple-element.51.out_held, bf16[128,2048]{1,0:T(8,128)(2,1)} %get-tuple-element.52.query_grad_held), custom_call_target="tpu_custom_call", output_to_operand_aliasing={{0}: (1, {}), {1}: (2, {})} | custom-call | tf_op jit(solution)/shard_map/pallas_call | solution.py:423
  40.8 4.5 %collective-permute-done.8 = bf16[512,128]{1,0:T(8,128)(2,1)S(1)} collective-permute-done((bf16[512,128]{1,0:T(8,128)(2,1)S(1)}, bf16[512,128]{1,0:T(8,128)(2,1)S(1)}, u32[]{:S(2)}, u32[]{:S(2)}) %collective-permute-start.8) | collective-permute-done | bytes 131104 | tf_op jit(solution)/shard_map/ppermute | solution.py:331
  45.3 0.0 collective-permute-done.12
  45.3 0.0 collective-permute-done.11
  45.4 0.1 add_convert_fusion
  45.5 0.1 collective-permute-start.13
  45.6 1.2 %collective-permute-done.13 = bf16[256,128]{1,0:T(8,128)(2,1)S(1)} collective-permute-done((bf16[256,128]{1,0:T(8,128)(2,1)S(1)}, bf16[256,128]{1,0:T(8,128)(2,1)S(1)}, u32[]{:S(2)}, u32[]{:S(2)}) %collective-permute-start.13) | collective-permute-done | bytes 65568 | tf_op jit(solution)/shard_map/ppermute | solution.py:337
  46.8 0.7 %fusion.2 = (bf16[1,128,256]{2,1,0:T(8,128)(2,1)}, bf16[1,128,256]{2,1,0:T(8,128)(2,1)}) fusion(bf16[256,128]{1,0:T(8,128)(2,1)S(1)} %get-tuple-element.62, bf16[256,128]{1,0:T(8,128)(2,1)S(1)} %get-tuple-element.63), kind=kLoop, calls=%fused_computation.10 | loop fusion | flops 262144 | bytes 262144 | tf_op jit(solution)/shard_map/broadcast_in_dim | solution.py:440
  (6 shorter events, 0.1 us)
Async XLA Ops:
  0.6 21.8 %copy-start = (bf16[1,128,2048]{2,1,0:T(8,128)(2,1)S(1)}, bf16[1,128,2048]{2,1,0:T(8,128)(2,1)}, u32[]{:S(2)}) copy-start(bf16[1,128,2048]{2,1,0:T(8,128)(2,1)} %param.6) | copy-start | bytes 1572868
  0.6 21.8 %copy-start.1 = (bf16[1,128,2048]{2,1,0:T(8,128)(2,1)S(1)}, bf16[1,128,2048]{2,1,0:T(8,128)(2,1)}, u32[]{:S(2)}) copy-start(bf16[1,128,2048]{2,1,0:T(8,128)(2,1)} %param.9) | copy-start | bytes 1572868
  1.7 1.6 %collective-permute-start = (bf16[272,128]{1,0:T(8,128)(2,1)S(1)}, bf16[272,128]{1,0:T(8,128)(2,1)S(1)}, u32[]{:S(2)}, u32[]{:S(2)}) collective-permute-start(bf16[272,128]{1,0:T(8,128)(2,1)S(1)} %get-tuple-element.34), channel_id=1, source_target_pairs={{0,1},{1,0},{2,3},{3,2},{4,5},{5,4},{6,7},{7,6},{8,9},{9,8},{10,11... | collective-permute-start | bytes 208904 | tf_op jit(solution)/shard_map/ppermute | solution.py:337
  3.3 19.5 %collective-permute-start.5 = (bf16[256,1024]{1,0:T(8,128)(2,1)S(1)}, bf16[256,1024]{1,0:T(8,128)(2,1)S(1)}, u32[]{:S(2)}, u32[]{:S(2)}) collective-permute-start(bf16[256,1024]{1,0:T(8,128)(2,1)S(1)} %shard_map.94), channel_id=1, source_target_pairs={{0,1},{1,0},{2,3},{3,2},{4,5},{5,4},{6,7},{7,6},{8,9},{9,8},{10,11... | collective-permute-start | bytes 1572872 | tf_op jit(solution)/shard_map/ppermute | solution.py:337
  3.5 10.9 %collective-permute-start.1 = (bf16[544,128]{1,0:T(8,128)(2,1)S(1)}, bf16[544,128]{1,0:T(8,128)(2,1)S(1)}, u32[]{:S(2)}, u32[]{:S(2)}) collective-permute-start(bf16[544,128]{1,0:T(8,128)(2,1)S(1)} %pad_maximum_fusion.1.refs_0_), channel_id=1, source_target_pairs={{0,2},{1,3},{2,4},{3,5},{4,6},{5,7},{8,10},{9,11},{10,12},{11,13},... | collective-permute-start | bytes 417800 | tf_op jit(solution)/shard_map/ppermute | solution.py:328
  8.3 7.5 %collective-permute-start.4 = (bf16[544,128]{1,0:T(8,128)(2,1)S(1)}, bf16[544,128]{1,0:T(8,128)(2,1)S(1)}, u32[]{:S(2)}, u32[]{:S(2)}) collective-permute-start(bf16[544,128]{1,0:T(8,128)(2,1)S(1)} %pad_maximum_fusion.1.refs_0_), channel_id=1, source_target_pairs={{0,4},{1,5},{2,6},{3,7},{8,12},{9,13},{10,14},{11,15},{16,20},{17,... | collective-permute-start | bytes 417800 | tf_op jit(solution)/shard_map/ppermute | solution.py:328
  12.8 6.7 %collective-permute-start.2 = (bf16[544,128]{1,0:T(8,128)(2,1)S(1)}, bf16[544,128]{1,0:T(8,128)(2,1)S(1)}, u32[]{:S(2)}, u32[]{:S(2)}) collective-permute-start(bf16[544,128]{1,0:T(8,128)(2,1)S(1)} %pad_maximum_fusion.1.refs_0_), channel_id=1, source_target_pairs={{0,16},{16,0},{1,17},{17,1},{2,18},{18,2},{3,19},{19,3},{4,20},{20... | collective-permute-start | bytes 417800 | tf_op jit(solution)/shard_map/ppermute | solution.py:334
  14.4 8.0 %collective-permute-start.3 = (bf16[544,128]{1,0:T(8,128)(2,1)S(1)}, bf16[544,128]{1,0:T(8,128)(2,1)S(1)}, u32[]{:S(2)}, u32[]{:S(2)}) collective-permute-start(bf16[544,128]{1,0:T(8,128)(2,1)S(1)} %collective-permute-done.1.refs_1_), channel_id=1, source_target_pairs={{0,16},{16,0},{1,17},{17,1},{2,18},{18,2},{3,19},{19,3},{4,20},{20... | collective-permute-start | bytes 417800 | tf_op jit(solution)/shard_map/ppermute | solution.py:334
  15.9 8.2 %collective-permute-start.6 = (bf16[544,128]{1,0:T(8,128)(2,1)S(1)}, bf16[544,128]{1,0:T(8,128)(2,1)S(1)}, u32[]{:S(2)}, u32[]{:S(2)}) collective-permute-start(bf16[544,128]{1,0:T(8,128)(2,1)S(1)} %collective-permute-done.4.refs_2_), channel_id=1, source_target_pairs={{0,16},{16,0},{1,17},{17,1},{2,18},{18,2},{3,19},{19,3},{4,20},{20... | collective-permute-start | bytes 417800 | tf_op jit(solution)/shard_map/ppermute | solution.py:334
  29.4 5.8 %collective-permute-start.7 = (bf16[512,128]{1,0:T(8,128)(2,1)S(1)}, bf16[512,128]{1,0:T(8,128)(2,1)S(1)}, u32[]{:S(2)}, u32[]{:S(2)}) collective-permute-start(bf16[512,128]{1,0:T(8,128)(2,1)S(1)} %get-tuple-element.49), channel_id=1, source_target_pairs={{0,16},{16,0},{1,17},{17,1},{2,18},{18,2},{3,19},{19,3},{4,20},{20... | collective-permute-start | bytes 393224 | tf_op jit(solution)/shard_map/ppermute | solution.py:334
  31.0 6.8 %collective-permute-start.10 = (bf16[512,128]{1,0:T(8,128)(2,1)S(1)}, bf16[512,128]{1,0:T(8,128)(2,1)S(1)}, u32[]{:S(2)}, u32[]{:S(2)}) collective-permute-start(bf16[512,128]{1,0:T(8,128)(2,1)S(1)} %get-tuple-element.59), channel_id=1, source_target_pairs={{0,16},{16,0},{1,17},{17,1},{2,18},{18,2},{3,19},{19,3},{4,20},{20... | collective-permute-start | bytes 393224 | tf_op jit(solution)/shard_map/ppermute | solution.py:334
  31.5 8.5 %collective-permute-start.9 = (bf16[256,1024]{1,0:T(8,128)(2,1)S(1)}, bf16[256,1024]{1,0:T(8,128)(2,1)S(1)}, u32[]{:S(2)}, u32[]{:S(2)}) collective-permute-start(bf16[256,1024]{1,0:T(8,128)(2,1)S(1)} %slice.15), channel_id=1, source_target_pairs={{0,1},{1,0},{2,3},{3,2},{4,5},{5,4},{6,7},{7,6},{8,9},{9,8},{10,11... | collective-permute-start | bytes 1572872 | tf_op jit(solution)/shard_map/ppermute | solution.py:337
  31.6 13.8 %collective-permute-start.12 = (bf16[512,128]{1,0:T(8,128)(2,1)S(1)}, bf16[512,128]{1,0:T(8,128)(2,1)S(1)}, u32[]{:S(2)}, u32[]{:S(2)}) collective-permute-start(bf16[512,128]{1,0:T(8,128)(2,1)S(1)} %get-tuple-element.61), channel_id=1, source_target_pairs={{0,16},{16,0},{1,17},{17,1},{2,18},{18,2},{3,19},{19,3},{4,20},{20... | collective-permute-start | bytes 393224 | tf_op jit(solution)/shard_map/ppermute | solution.py:334
  35.3 10.1 %collective-permute-start.8 = (bf16[512,128]{1,0:T(8,128)(2,1)S(1)}, bf16[512,128]{1,0:T(8,128)(2,1)S(1)}, u32[]{:S(2)}, u32[]{:S(2)}) collective-permute-start(bf16[512,128]{1,0:T(8,128)(2,1)S(1)} %add_convert_fusion.2), channel_id=1, source_target_pairs={{4,0},{5,1},{6,2},{7,3},{12,8},{13,9},{14,10},{15,11},{20,16},{21,... | collective-permute-start | bytes 393224 | tf_op jit(solution)/shard_map/ppermute | solution.py:331
  37.8 7.5 %collective-permute-start.11 = (bf16[512,128]{1,0:T(8,128)(2,1)S(1)}, bf16[512,128]{1,0:T(8,128)(2,1)S(1)}, u32[]{:S(2)}, u32[]{:S(2)}) collective-permute-start(bf16[512,128]{1,0:T(8,128)(2,1)S(1)} %add_convert_fusion.1), channel_id=1, source_target_pairs={{2,0},{3,1},{4,2},{5,3},{6,4},{7,5},{10,8},{11,9},{12,10},{13,11},... | collective-permute-start | bytes 393224 | tf_op jit(solution)/shard_map/ppermute | solution.py:331
  45.5 1.3 %collective-permute-start.13 = (bf16[256,128]{1,0:T(8,128)(2,1)S(1)}, bf16[256,128]{1,0:T(8,128)(2,1)S(1)}, u32[]{:S(2)}, u32[]{:S(2)}) collective-permute-start(bf16[256,128]{1,0:T(8,128)(2,1)S(1)} %slice.21), channel_id=1, source_target_pairs={{0,1},{1,0},{2,3},{3,2},{4,5},{5,4},{6,7},{7,6},{8,9},{9,8},{10,11... | collective-permute-start | bytes 196616 | tf_op jit(solution)/shard_map/ppermute | solution.py:337

commit v4 on v2

--- a/solution.py
+++ b/solution.py
@@ -315,6 +315,9 @@
 
     def down(block, k):
         return lax.ppermute(block, "ctx", [(i + 2 * k, i) for i in range(ranks - 2 * k)])
+
+    def down_across(block, k):
+        return lax.ppermute(block, "ctx", [(i + 2 * k, i ^ 1) for i in range(ranks - 2 * k)])
 
     def to_partner(block):
         return lax.ppermute(block, "half", [(0, 1), (1, 0)])
@@ -397,14 +400,17 @@
         cost_estimate=pl.CostEstimate(flops=0, bytes_accessed=4 * 1024 * 1024, transcendentals=0),
     )(outs[0])
 
-    parts = []
+    parts, side_parts = [], []
     for k in reversed(range(count)):
         crossed = to_partner(away_sum[k])
         part = home_sum[k].astype(F32) + crossed.astype(F32)
+        near, far = part[: 2 * rows], part[2 * rows :].astype(BF16)
         if k:
-            part = part.astype(BF16)
-            part = down(part, k)
-        parts.append(part)
+            parts.append(down(near.astype(BF16), k))
+            side_parts.append(down_across(far, k))
+        else:
+            parts.append(near)
+            side_parts.append(to_side(far))
     out_got = to_side(side_out)
     out, query_grad = pl.pallas_call(
         finish_kernel,
@@ -416,9 +422,9 @@
         scratch_shapes=[pltpu.SemaphoreType.DMA((2,))],
     )(out_got, out, query_grad)
     parts[0], out, query_grad = lax.optimization_barrier((parts[0], out, query_grad))
-    total = sum(part.astype(F32) for part in parts).astype(BF16)
-    grads_got = to_side(total[2 * rows :])
-    grads = total[: 2 * rows]
+    grads, grads_got = (
+        sum(part.astype(F32) for part in group).astype(BF16) for group in (parts, side_parts)
+    )
     first = core_index() == 0
     grads = jnp.concatenate(
         [jnp.where(first, grads, grads_got), jnp.where(first, grads_got, grads)], axis=1

time: 49.2 us -> 50.4 us (1.024)
  starting transfers between devices: 20.1 us -> 22.7 us
  waiting for transfers between devices: 17.6 us -> 16.3 us
    ppermute x2, waiting for transfers between devices: 5.84 us -> 2.69 us  [down(): lax.ppermute(block, 'ctx', [(i + 2 * k, i) for i in range(ranks - 2 * k)])]
    ppermute x0 -> x2, waiting for transfers between devices: none -> 3.01 us  [down_across(): lax.ppermute(block, 'ctx', [(i + 2 * k, i ^ 1) for i in range(ranks - 2 *...]
    ppermute x0 -> x2, starting transfers between devices: none -> 2.58 us  [down_across(): lax.ppermute(block, 'ctx', [(i + 2 * k, i ^ 1) for i in range(ranks - 2 *...]
    ppermute x4, waiting for transfers between devices: 1.24 us -> 0.01 us  [to_side(): return lax.ppermute(block, 'ctx', [(i, i ^ 1) for i in range(ranks)])]
  transfers between devices with their start and end apart: 14 -> 16, of which waited for: 8 -> 8; matrix products, arithmetic and copies ran while one was open for 0% -> 0% of each run, Pallas kernels for 6% -> 6%
where the time goes in v4:
time: 50.4 us; the launch traced here: 50.1 us
  starting transfers between devices  22.7 us (45%)
  waiting for transfers between devices  16.3 us (32%)
  Pallas kernels  9.21 us (18%)
  other arithmetic  0.95 us (2%)
  between operations  0.88 us (2%)
    ppermute x6, waiting for transfers between devices, to_partner(): return lax.ppermute(block, 'half', [(0, 1), (1, 0)])  9.69 us
    ppermute x2, starting transfers between devices, up(): lax.ppermute(block, 'ctx', [(i, i + 2 * k) for i in range(ranks - 2 * k)])  9.29 us
    ppermute x6, starting transfers between devices, to_partner(): return lax.ppermute(block, 'half', [(0, 1), (1, 0)])  7.29 us
    pallas_call x1, Pallas kernels, local(): pl.pallas_call(functools.partial(attention_kernel, hops), out_shape=[pltp...  5.26 us
    ppermute x2, waiting for transfers between devices, down_across(): lax.ppermute(block, 'ctx', [(i + 2 * k, i ^ 1) for i in range(ranks - 2 *...  3.01 us
    ppermute x2, waiting for transfers between devices, down(): lax.ppermute(block, 'ctx', [(i + 2 * k, i) for i in range(ranks - 2 * k)])  2.69 us
    ppermute x2, starting transfers between devices, down(): lax.ppermute(block, 'ctx', [(i + 2 * k, i) for i in range(ranks - 2 * k)])  2.58 us
    ppermute x2, starting transfers between devices, down_across(): lax.ppermute(block, 'ctx', [(i + 2 * k, i ^ 1) for i in range(ranks - 2 *...  2.58 us
  transfers between devices with their start and end apart: 16, of which 8 were waited for; matrix products, arithmetic and copies ran while one was open for 0% of the time, Pallas kernels for 6%

profile of v4, /device:TPU:0, one launch (start us, length us, event | category | flops | bytes accessed | tf_op | source)
XLA Modules:
  0.0 50.1 jit_solution(12167087509473978442)
XLA Ops:
  0.6 0.0 copy-start
  0.6 0.0 copy-start.1
  0.7 1.0 %shard_map.93 = (bf16[272,128]{1,0:T(8,128)(2,1)S(1)}, bf16[272,128]{1,0:T(8,128)(2,1)S(1)}) custom-call(s32[4]{0:T(128)} %bitcast.19, bf16[128,256]{1,0:T(8,128)(2,1)} %bitcast.17, bf16[128,256]{1,0:T(8,128)(2,1)} %bitcast.18, s32[1,128]{1,0:T(1,128)} %docs_ref.1), custom_call_target="tpu_custom_call" | custom-call | tf_op jit(solution)/shard_map/pallas_call | solution.py:328
  1.7 0.5 %collective-permute-start = (bf16[272,128]{1,0:T(8,128)(2,1)S(1)}, bf16[272,128]{1,0:T(8,128)(2,1)S(1)}, u32[]{:S(2)}, u32[]{:S(2)}) collective-permute-start(bf16[272,128]{1,0:T(8,128)(2,1)S(1)} %get-tuple-element.34), channel_id=1, source_target_pairs={{0,1},{1,0},{2,3},{3,2},{4,5},{5,4},{6,7},{7,6},{8,9},{9,8},{10,11... | collective-permute-start | bytes 208904 | tf_op jit(solution)/shard_map/ppermute | solution.py:326
  2.2 1.0 %shard_map.94 = bf16[256,1024]{1,0:T(8,128)(2,1)S(1)} custom-call(bf16[128,2048]{1,0:T(8,128)(2,1)} %bitcast.11, bf16[128,2048]{1,0:T(8,128)(2,1)} %bitcast.13), custom_call_target="tpu_custom_call" | custom-call | tf_op jit(solution)/shard_map/pallas_call | solution.py:337
  3.2 0.0 collective-permute-done
  3.3 0.3 collective-permute-start.5
  3.5 4.8 %collective-permute-start.1 = (bf16[544,128]{1,0:T(8,128)(2,1)S(1)}, bf16[544,128]{1,0:T(8,128)(2,1)S(1)}, u32[]{:S(2)}, u32[]{:S(2)}) collective-permute-start(bf16[544,128]{1,0:T(8,128)(2,1)S(1)} %pad_maximum_fusion.1.refs_0_), channel_id=1, source_target_pairs={{0,2},{1,3},{2,4},{3,5},{4,6},{5,7},{8,10},{9,11},{10,12},{11,13},... | collective-permute-start | bytes 417800 | tf_op jit(solution)/shard_map/ppermute | solution.py:314
  8.3 4.5 %collective-permute-start.4 = (bf16[544,128]{1,0:T(8,128)(2,1)S(1)}, bf16[544,128]{1,0:T(8,128)(2,1)S(1)}, u32[]{:S(2)}, u32[]{:S(2)}) collective-permute-start(bf16[544,128]{1,0:T(8,128)(2,1)S(1)} %pad_maximum_fusion.1.refs_0_), channel_id=1, source_target_pairs={{0,4},{1,5},{2,6},{3,7},{8,12},{9,13},{10,14},{11,15},{16,20},{17,... | collective-permute-start | bytes 417800 | tf_op jit(solution)/shard_map/ppermute | solution.py:314
  12.8 1.6 %collective-permute-start.2 = (bf16[544,128]{1,0:T(8,128)(2,1)S(1)}, bf16[544,128]{1,0:T(8,128)(2,1)S(1)}, u32[]{:S(2)}, u32[]{:S(2)}) collective-permute-start(bf16[544,128]{1,0:T(8,128)(2,1)S(1)} %pad_maximum_fusion.1.refs_0_), channel_id=1, source_target_pairs={{0,16},{16,0},{1,17},{17,1},{2,18},{18,2},{3,19},{19,3},{4,20},{20... | collective-permute-start | bytes 417800 | tf_op jit(solution)/shard_map/ppermute | solution.py:323
  14.4 0.0 collective-permute-done.1.refs_1_
  14.4 0.5 %collective-permute-start.3 = (bf16[544,128]{1,0:T(8,128)(2,1)S(1)}, bf16[544,128]{1,0:T(8,128)(2,1)S(1)}, u32[]{:S(2)}, u32[]{:S(2)}) collective-permute-start(bf16[544,128]{1,0:T(8,128)(2,1)S(1)} %collective-permute-done.1.refs_1_), channel_id=1, source_target_pairs={{0,16},{16,0},{1,17},{17,1},{2,18},{18,2},{3,19},{19,3},{4,20},{20... | collective-permute-start | bytes 417800 | tf_op jit(solution)/shard_map/ppermute | solution.py:323
  14.9 0.9 %collective-permute-done.4.refs_2_ = bf16[544,128]{1,0:T(8,128)(2,1)S(1)} collective-permute-done((bf16[544,128]{1,0:T(8,128)(2,1)S(1)}, bf16[544,128]{1,0:T(8,128)(2,1)S(1)}, u32[]{:S(2)}, u32[]{:S(2)}) %collective-permute-start.4) | collective-permute-done | bytes 139296 | tf_op jit(solution)/shard_map/ppermute | solution.py:314
  15.9 1.5 %collective-permute-start.6 = (bf16[544,128]{1,0:T(8,128)(2,1)S(1)}, bf16[544,128]{1,0:T(8,128)(2,1)S(1)}, u32[]{:S(2)}, u32[]{:S(2)}) collective-permute-start(bf16[544,128]{1,0:T(8,128)(2,1)S(1)} %collective-permute-done.4.refs_2_), channel_id=1, source_target_pairs={{0,16},{16,0},{1,17},{17,1},{2,18},{18,2},{3,19},{19,3},{4,20},{20... | collective-permute-start | bytes 417800 | tf_op jit(solution)/shard_map/ppermute | solution.py:323
  17.4 2.1 %collective-permute-done.2.refs_2_.refs_3_ = bf16[544,128]{1,0:T(8,128)(2,1)S(1)} collective-permute-done((bf16[544,128]{1,0:T(8,128)(2,1)S(1)}, bf16[544,128]{1,0:T(8,128)(2,1)S(1)}, u32[]{:S(2)}, u32[]{:S(2)}) %collective-permute-start.2) | collective-permute-done | bytes 139296 | tf_op jit(solution)/shard_map/ppermute | solution.py:323
  19.5 3.0 %collective-permute-done.3.refs_3_.refs_4_ = bf16[544,128]{1,0:T(8,128)(2,1)S(1)} collective-permute-done((bf16[544,128]{1,0:T(8,128)(2,1)S(1)}, bf16[544,128]{1,0:T(8,128)(2,1)S(1)}, u32[]{:S(2)}, u32[]{:S(2)}) %collective-permute-start.3) | collective-permute-done | bytes 139296 | tf_op jit(solution)/shard_map/ppermute | solution.py:323
  22.5 0.0 copy-done
  22.5 0.0 copy-done.1
  22.5 0.1 shard_map.95
  22.5 0.2 shard_map.96
  22.8 0.0 collective-permute-done.5
  22.8 0.1 pad_maximum_fusion.rows_ref
  22.8 1.2 %collective-permute-done.6.refs_5_ = bf16[544,128]{1,0:T(8,128)(2,1)S(1)} collective-permute-done((bf16[544,128]{1,0:T(8,128)(2,1)S(1)}, bf16[544,128]{1,0:T(8,128)(2,1)S(1)}, u32[]{:S(2)}, u32[]{:S(2)}) %collective-permute-start.6) | collective-permute-done | bytes 139296 | tf_op jit(solution)/shard_map/ppermute | solution.py:323
  24.1 5.3 %shard_map.97 = (bf16[512,1024]{1,0:T(8,128)(2,1)S(1)}, bf16[512,128]{1,0:T(8,128)(2,1)S(1)}, bf16[512,128]{1,0:T(8,128)(2,1)S(1)}, bf16[512,128]{1,0:T(8,128)(2...) custom-call(bf16[512,1024]{1,0:T(8,128)(2,1)S(1)} %pad_maximum_fusion.rows_ref, ...), custom_call_target="tpu_custom_call" | custom-call | flops 2415919104 | bytes 4194304 | tf_op jit(solution)/shard_map/pallas_call | solution.py:366
  29.3 1.6 %collective-permute-start.10 = (bf16[512,128]{1,0:T(8,128)(2,1)S(1)}, bf16[512,128]{1,0:T(8,128)(2,1)S(1)}, u32[]{:S(2)}, u32[]{:S(2)}) collective-permute-start(bf16[512,128]{1,0:T(8,128)(2,1)S(1)} %get-tuple-element.59), channel_id=1, source_target_pairs={{0,16},{16,0},{1,17},{17,1},{2,18},{18,2},{3,19},{19,3},{4,20},{20... | collective-permute-start | bytes 393224 | tf_op jit(solution)/shard_map/ppermute | solution.py:323
  30.9 0.5 %collective-permute-start.12 = (bf16[512,128]{1,0:T(8,128)(2,1)S(1)}, bf16[512,128]{1,0:T(8,128)(2,1)S(1)}, u32[]{:S(2)}, u32[]{:S(2)}) collective-permute-start(bf16[512,128]{1,0:T(8,128)(2,1)S(1)} %get-tuple-element.61), channel_id=1, source_target_pairs={{0,16},{16,0},{1,17},{17,1},{2,18},{18,2},{3,19},{19,3},{4,20},{20... | collective-permute-start | bytes 393224 | tf_op jit(solution)/shard_map/ppermute | solution.py:323
  31.5 0.1 collective-permute-start.9
  31.5 1.6 %collective-permute-start.7 = (bf16[512,128]{1,0:T(8,128)(2,1)S(1)}, bf16[512,128]{1,0:T(8,128)(2,1)S(1)}, u32[]{:S(2)}, u32[]{:S(2)}) collective-permute-start(bf16[512,128]{1,0:T(8,128)(2,1)S(1)} %get-tuple-element.49), channel_id=1, source_target_pairs={{0,16},{16,0},{1,17},{17,1},{2,18},{18,2},{3,19},{19,3},{4,20},{20... | collective-permute-start | bytes 393224 | tf_op jit(solution)/shard_map/ppermute | solution.py:323
  33.1 2.0 %collective-permute-done.10 = bf16[512,128]{1,0:T(8,128)(2,1)S(1)} collective-permute-done((bf16[512,128]{1,0:T(8,128)(2,1)S(1)}, bf16[512,128]{1,0:T(8,128)(2,1)S(1)}, u32[]{:S(2)}, u32[]{:S(2)}) %collective-permute-start.10) | collective-permute-done | bytes 131104 | tf_op jit(solution)/shard_map/ppermute | solution.py:323
  35.2 1.3 %collective-permute-start.11 = (bf16[256,128]{1,0:T(8,128)(2,1)S(1)}, bf16[256,128]{1,0:T(8,128)(2,1)S(1)}, u32[]{:S(2)}, u32[]{:S(2)}) collective-permute-start(bf16[256,128]{1,0:T(8,128)(2,1)S(1)} %get-tuple-element.66), channel_id=1, source_target_pairs={{2,0},{3,1},{4,2},{5,3},{6,4},{7,5},{10,8},{11,9},{12,10},{13,11},... | collective-permute-start | bytes 196616 | tf_op jit(solution)/shard_map/ppermute | solution.py:317
  36.5 1.3 %collective-permute-start.14 = (bf16[256,128]{1,0:T(8,128)(2,1)S(1)}, bf16[256,128]{1,0:T(8,128)(2,1)S(1)}, u32[]{:S(2)}, u32[]{:S(2)}) collective-permute-start(bf16[256,128]{1,0:T(8,128)(2,1)S(1)} %get-tuple-element.67), channel_id=1, source_target_pairs={{2,1},{3,0},{4,3},{5,2},{6,5},{7,4},{10,9},{11,8},{12,11},{13,10},... | collective-permute-start | bytes 196616 | tf_op jit(solution)/shard_map/ppermute | solution.py:320
  37.8 1.3 %collective-permute-done.7 = bf16[512,128]{1,0:T(8,128)(2,1)S(1)} collective-permute-done((bf16[512,128]{1,0:T(8,128)(2,1)S(1)}, bf16[512,128]{1,0:T(8,128)(2,1)S(1)}, u32[]{:S(2)}, u32[]{:S(2)}) %collective-permute-start.7) | collective-permute-done | bytes 131104 | tf_op jit(solution)/shard_map/ppermute | solution.py:323
  39.2 1.3 %collective-permute-start.8 = (bf16[256,128]{1,0:T(8,128)(2,1)S(1)}, bf16[256,128]{1,0:T(8,128)(2,1)S(1)}, u32[]{:S(2)}, u32[]{:S(2)}) collective-permute-start(bf16[256,128]{1,0:T(8,128)(2,1)S(1)} %get-tuple-element.69), channel_id=1, source_target_pairs={{4,0},{5,1},{6,2},{7,3},{12,8},{13,9},{14,10},{15,11},{20,16},{21,... | collective-permute-start | bytes 196616 | tf_op jit(solution)/shard_map/ppermute | solution.py:317
  40.5 0.0 collective-permute-done.12
  40.6 0.1 collective-permute-start.15
  40.7 0.0 collective-permute-done.9.side_ref
  40.7 1.3 %collective-permute-start.13 = (bf16[256,128]{1,0:T(8,128)(2,1)S(1)}, bf16[256,128]{1,0:T(8,128)(2,1)S(1)}, u32[]{:S(2)}, u32[]{:S(2)}) collective-permute-start(bf16[256,128]{1,0:T(8,128)(2,1)S(1)} %get-tuple-element.68), channel_id=1, source_target_pairs={{4,1},{5,0},{6,3},{7,2},{12,9},{13,8},{14,11},{15,10},{20,17},{21,... | collective-permute-start | bytes 196616 | tf_op jit(solution)/shard_map/ppermute | solution.py:320
  42.0 0.8 %shard_map.98 = (bf16[128,2048]{1,0:T(8,128)(2,1)}, bf16[128,2048]{1,0:T(8,128)(2,1)}) custom-call(bf16[512,1024]{1,0:T(8,128)(2,1)S(1)} %get-tuple-element.50.own_ref), custom_call_target="tpu_custom_call" | custom-call | bytes 4194304 | tf_op jit(solution)/shard_map/pallas_call | solution.py:393
  42.8 0.8 %shard_map.99 = (bf16[128,2048]{1,0:T(8,128)(2,1)}, bf16[128,2048]{1,0:T(8,128)(2,1)}) custom-call(bf16[256,1024]{1,0:T(8,128)(2,1)S(1)} %collective-permute-done.9.side_ref, bf16[128,2048]{1,0:T(8,128)(2,1)} %get-tuple-element.51.out_held, bf16[128,2048]{1,0:T(8,128)(2,1)} %get-tuple-element.52.query_grad_held), custom_call_target="tpu_custom_call", output_to_operand_aliasing={{0}: (1, {}), {1}: (2, {})} | custom-call | tf_op jit(solution)/shard_map/pallas_call | solution.py:415
  43.6 2.7 %collective-permute-done.8 = bf16[256,128]{1,0:T(8,128)(2,1)S(1)} collective-permute-done((bf16[256,128]{1,0:T(8,128)(2,1)S(1)}, bf16[256,128]{1,0:T(8,128)(2,1)S(1)}, u32[]{:S(2)}, u32[]{:S(2)}) %collective-permute-start.8) | collective-permute-done | bytes 65568 | tf_op jit(solution)/shard_map/ppermute | solution.py:317
  46.3 0.0 collective-permute-done.11
  46.3 0.0 collective-permute-done.14
  46.3 0.0 collective-permute-done.15
  46.3 3.0 %collective-permute-done.13 = bf16[256,128]{1,0:T(8,128)(2,1)S(1)} collective-permute-done((bf16[256,128]{1,0:T(8,128)(2,1)S(1)}, bf16[256,128]{1,0:T(8,128)(2,1)S(1)}, u32[]{:S(2)}, u32[]{:S(2)}) %collective-permute-start.13) | collective-permute-done | bytes 65568 | tf_op jit(solution)/shard_map/ppermute | solution.py:320
  49.3 0.1 broadcast_select_fusion
  49.4 0.7 %fusion.3 = (bf16[1,128,256]{2,1,0:T(8,128)(2,1)}, bf16[1,128,256]{2,1,0:T(8,128)(2,1)}) fusion(bf16[256,128]{1,0:T(8,128)(2,1)S(1)} %get-tuple-element.62, bf16[256,128]{1,0:T(8,128)(2,1)S(1)} %broadcast_select_fusion.1), kind=kLoop, calls=%fused_computation.14 | loop fusion | flops 262144 | bytes 262144 | tf_op jit(solution)/shard_map/broadcast_in_dim | solution.py:432
  (9 shorter events, 0.2 us)
Async XLA Ops:
  0.6 21.8 %copy-start = (bf16[1,128,2048]{2,1,0:T(8,128)(2,1)S(1)}, bf16[1,128,2048]{2,1,0:T(8,128)(2,1)}, u32[]{:S(2)}) copy-start(bf16[1,128,2048]{2,1,0:T(8,128)(2,1)} %param.6) | copy-start | bytes 1572868
  0.6 21.8 %copy-start.1 = (bf16[1,128,2048]{2,1,0:T(8,128)(2,1)S(1)}, bf16[1,128,2048]{2,1,0:T(8,128)(2,1)}, u32[]{:S(2)}) copy-start(bf16[1,128,2048]{2,1,0:T(8,128)(2,1)} %param.9) | copy-start | bytes 1572868
  1.7 1.6 %collective-permute-start = (bf16[272,128]{1,0:T(8,128)(2,1)S(1)}, bf16[272,128]{1,0:T(8,128)(2,1)S(1)}, u32[]{:S(2)}, u32[]{:S(2)}) collective-permute-start(bf16[272,128]{1,0:T(8,128)(2,1)S(1)} %get-tuple-element.34), channel_id=1, source_target_pairs={{0,1},{1,0},{2,3},{3,2},{4,5},{5,4},{6,7},{7,6},{8,9},{9,8},{10,11... | collective-permute-start | bytes 208904 | tf_op jit(solution)/shard_map/ppermute | solution.py:326
  3.3 19.5 %collective-permute-start.5 = (bf16[256,1024]{1,0:T(8,128)(2,1)S(1)}, bf16[256,1024]{1,0:T(8,128)(2,1)S(1)}, u32[]{:S(2)}, u32[]{:S(2)}) collective-permute-start(bf16[256,1024]{1,0:T(8,128)(2,1)S(1)} %shard_map.94), channel_id=1, source_target_pairs={{0,1},{1,0},{2,3},{3,2},{4,5},{5,4},{6,7},{7,6},{8,9},{9,8},{10,11... | collective-permute-start | bytes 1572872 | tf_op jit(solution)/shard_map/ppermute | solution.py:326
  3.5 10.9 %collective-permute-start.1 = (bf16[544,128]{1,0:T(8,128)(2,1)S(1)}, bf16[544,128]{1,0:T(8,128)(2,1)S(1)}, u32[]{:S(2)}, u32[]{:S(2)}) collective-permute-start(bf16[544,128]{1,0:T(8,128)(2,1)S(1)} %pad_maximum_fusion.1.refs_0_), channel_id=1, source_target_pairs={{0,2},{1,3},{2,4},{3,5},{4,6},{5,7},{8,10},{9,11},{10,12},{11,13},... | collective-permute-start | bytes 417800 | tf_op jit(solution)/shard_map/ppermute | solution.py:314
  8.3 7.5 %collective-permute-start.4 = (bf16[544,128]{1,0:T(8,128)(2,1)S(1)}, bf16[544,128]{1,0:T(8,128)(2,1)S(1)}, u32[]{:S(2)}, u32[]{:S(2)}) collective-permute-start(bf16[544,128]{1,0:T(8,128)(2,1)S(1)} %pad_maximum_fusion.1.refs_0_), channel_id=1, source_target_pairs={{0,4},{1,5},{2,6},{3,7},{8,12},{9,13},{10,14},{11,15},{16,20},{17,... | collective-permute-start | bytes 417800 | tf_op jit(solution)/shard_map/ppermute | solution.py:314
  12.8 6.7 %collective-permute-start.2 = (bf16[544,128]{1,0:T(8,128)(2,1)S(1)}, bf16[544,128]{1,0:T(8,128)(2,1)S(1)}, u32[]{:S(2)}, u32[]{:S(2)}) collective-permute-start(bf16[544,128]{1,0:T(8,128)(2,1)S(1)} %pad_maximum_fusion.1.refs_0_), channel_id=1, source_target_pairs={{0,16},{16,0},{1,17},{17,1},{2,18},{18,2},{3,19},{19,3},{4,20},{20... | collective-permute-start | bytes 417800 | tf_op jit(solution)/shard_map/ppermute | solution.py:323
  14.4 8.0 %collective-permute-start.3 = (bf16[544,128]{1,0:T(8,128)(2,1)S(1)}, bf16[544,128]{1,0:T(8,128)(2,1)S(1)}, u32[]{:S(2)}, u32[]{:S(2)}) collective-permute-start(bf16[544,128]{1,0:T(8,128)(2,1)S(1)} %collective-permute-done.1.refs_1_), channel_id=1, source_target_pairs={{0,16},{16,0},{1,17},{17,1},{2,18},{18,2},{3,19},{19,3},{4,20},{20... | collective-permute-start | bytes 417800 | tf_op jit(solution)/shard_map/ppermute | solution.py:323
  15.9 8.2 %collective-permute-start.6 = (bf16[544,128]{1,0:T(8,128)(2,1)S(1)}, bf16[544,128]{1,0:T(8,128)(2,1)S(1)}, u32[]{:S(2)}, u32[]{:S(2)}) collective-permute-start(bf16[544,128]{1,0:T(8,128)(2,1)S(1)} %collective-permute-done.4.refs_2_), channel_id=1, source_target_pairs={{0,16},{16,0},{1,17},{17,1},{2,18},{18,2},{3,19},{19,3},{4,20},{20... | collective-permute-start | bytes 417800 | tf_op jit(solution)/shard_map/ppermute | solution.py:323
  29.3 5.8 %collective-permute-start.10 = (bf16[512,128]{1,0:T(8,128)(2,1)S(1)}, bf16[512,128]{1,0:T(8,128)(2,1)S(1)}, u32[]{:S(2)}, u32[]{:S(2)}) collective-permute-start(bf16[512,128]{1,0:T(8,128)(2,1)S(1)} %get-tuple-element.59), channel_id=1, source_target_pairs={{0,16},{16,0},{1,17},{17,1},{2,18},{18,2},{3,19},{19,3},{4,20},{20... | collective-permute-start | bytes 393224 | tf_op jit(solution)/shard_map/ppermute | solution.py:323
  30.9 9.6 %collective-permute-start.12 = (bf16[512,128]{1,0:T(8,128)(2,1)S(1)}, bf16[512,128]{1,0:T(8,128)(2,1)S(1)}, u32[]{:S(2)}, u32[]{:S(2)}) collective-permute-start(bf16[512,128]{1,0:T(8,128)(2,1)S(1)} %get-tuple-element.61), channel_id=1, source_target_pairs={{0,16},{16,0},{1,17},{17,1},{2,18},{18,2},{3,19},{19,3},{4,20},{20... | collective-permute-start | bytes 393224 | tf_op jit(solution)/shard_map/ppermute | solution.py:323
  31.5 9.2 %collective-permute-start.9 = (bf16[256,1024]{1,0:T(8,128)(2,1)S(1)}, bf16[256,1024]{1,0:T(8,128)(2,1)S(1)}, u32[]{:S(2)}, u32[]{:S(2)}) collective-permute-start(bf16[256,1024]{1,0:T(8,128)(2,1)S(1)} %slice.33), channel_id=1, source_target_pairs={{0,1},{1,0},{2,3},{3,2},{4,5},{5,4},{6,7},{7,6},{8,9},{9,8},{10,11... | collective-permute-start | bytes 1572872 | tf_op jit(solution)/shard_map/ppermute | solution.py:326
  31.5 7.6 %collective-permute-start.7 = (bf16[512,128]{1,0:T(8,128)(2,1)S(1)}, bf16[512,128]{1,0:T(8,128)(2,1)S(1)}, u32[]{:S(2)}, u32[]{:S(2)}) collective-permute-start(bf16[512,128]{1,0:T(8,128)(2,1)S(1)} %get-tuple-element.49), channel_id=1, source_target_pairs={{0,16},{16,0},{1,17},{17,1},{2,18},{18,2},{3,19},{19,3},{4,20},{20... | collective-permute-start | bytes 393224 | tf_op jit(solution)/shard_map/ppermute | solution.py:323
  35.2 11.1 %collective-permute-start.11 = (bf16[256,128]{1,0:T(8,128)(2,1)S(1)}, bf16[256,128]{1,0:T(8,128)(2,1)S(1)}, u32[]{:S(2)}, u32[]{:S(2)}) collective-permute-start(bf16[256,128]{1,0:T(8,128)(2,1)S(1)} %get-tuple-element.66), channel_id=1, source_target_pairs={{2,0},{3,1},{4,2},{5,3},{6,4},{7,5},{10,8},{11,9},{12,10},{13,11},... | collective-permute-start | bytes 196616 | tf_op jit(solution)/shard_map/ppermute | solution.py:317
  36.5 9.8 %collective-permute-start.14 = (bf16[256,128]{1,0:T(8,128)(2,1)S(1)}, bf16[256,128]{1,0:T(8,128)(2,1)S(1)}, u32[]{:S(2)}, u32[]{:S(2)}) collective-permute-start(bf16[256,128]{1,0:T(8,128)(2,1)S(1)} %get-tuple-element.67), channel_id=1, source_target_pairs={{2,1},{3,0},{4,3},{5,2},{6,5},{7,4},{10,9},{11,8},{12,11},{13,10},... | collective-permute-start | bytes 196616 | tf_op jit(solution)/shard_map/ppermute | solution.py:320
  39.2 7.1 %collective-permute-start.8 = (bf16[256,128]{1,0:T(8,128)(2,1)S(1)}, bf16[256,128]{1,0:T(8,128)(2,1)S(1)}, u32[]{:S(2)}, u32[]{:S(2)}) collective-permute-start(bf16[256,128]{1,0:T(8,128)(2,1)S(1)} %get-tuple-element.69), channel_id=1, source_target_pairs={{4,0},{5,1},{6,2},{7,3},{12,8},{13,9},{14,10},{15,11},{20,16},{21,... | collective-permute-start | bytes 196616 | tf_op jit(solution)/shard_map/ppermute | solution.py:317
  40.6 5.7 %collective-permute-start.15 = (bf16[256,128]{1,0:T(8,128)(2,1)S(1)}, bf16[256,128]{1,0:T(8,128)(2,1)S(1)}, u32[]{:S(2)}, u32[]{:S(2)}) collective-permute-start(bf16[256,128]{1,0:T(8,128)(2,1)S(1)} %slice.61), channel_id=1, source_target_pairs={{0,1},{1,0},{2,3},{3,2},{4,5},{5,4},{6,7},{7,6},{8,9},{9,8},{10,11... | collective-permute-start | bytes 196616 | tf_op jit(solution)/shard_map/ppermute | solution.py:326
  40.7 8.7 %collective-permute-start.13 = (bf16[256,128]{1,0:T(8,128)(2,1)S(1)}, bf16[256,128]{1,0:T(8,128)(2,1)S(1)}, u32[]{:S(2)}, u32[]{:S(2)}) collective-permute-start(bf16[256,128]{1,0:T(8,128)(2,1)S(1)} %get-tuple-element.68), channel_id=1, source_target_pairs={{4,1},{5,0},{6,3},{7,2},{12,9},{13,8},{14,11},{15,10},{20,17},{21,... | collective-permute-start | bytes 196616 | tf_op jit(solution)/shard_map/ppermute | solution.py:320

commit v5 on v2

--- a/solution.py
+++ b/solution.py
@@ -143,6 +143,7 @@
         value_total,
         logical_of,
         needed_of,
+        order_of,
     ) = refs[4 * count + 5 :]
     rows = rows_ref.shape[0] // 4
     per_block = rows // NBLK
@@ -206,9 +207,18 @@
     ]
     first = jnp.where(flags > 0.5, firsts[1], firsts[0]).astype(I32)
     flags = flags.astype(I32)
-    for unit_index in range(2 * NBLK):
-        logical_of[unit_index] = flags[unit_index, 0]
-        needed_of[unit_index] = window + parity[unit_index // NBLK] - first[unit_index, 0] // rows
+    needs = [
+        window + parity[index // NBLK] - first[index, 0] // rows for index in range(2 * NBLK)
+    ]
+    for index, need in enumerate(needs):
+        place = jnp.int32(0)
+        for other, its_need in enumerate(needs):
+            if other != index:
+                ahead = its_need >= need if other < index else its_need > need
+                place = place + ahead.astype(I32)
+        order_of[place] = index
+        logical_of[index] = flags[index, 0]
+        needed_of[index] = need
 
     def unit(unit_index, chunks):
         who, block = unit_index // NBLK, lax.rem(unit_index, NBLK)
@@ -264,10 +274,8 @@
         return query_at, grad_at, logical, span, out, query_grad, key_add, value_add
 
     def step(pair, carry):
-        members = [pair * GROUPED + m for m in range(GROUPED)]
+        members = [order_of[pair * GROUPED + m] for m in range(GROUPED)]
         needed = needed_of[members[0]]
-        for member in members[1:]:
-            needed = jnp.maximum(needed, needed_of[member])
         for chunks in range(1, window + 1):
 
             @pl.when(needed == chunks)
@@ -377,6 +385,7 @@
             pltpu.VMEM((2, keys, HEAD_SIZE), F32),
             pltpu.SMEM((2 * NBLK,), I32),
             pltpu.SMEM((2 * NBLK,), I32),
+            pltpu.SMEM((2 * NBLK,), I32),
         ],
         compiler_params=pltpu.CompilerParams(vmem_limit_bytes=32 * 1024 * 1024),
         cost_estimate=pl.CostEstimate(

time: 49.2 us -> 48.6 us (0.988)
  no operation moved by 1% of the time
where the time goes in v5:
time: 48.6 us; the launch traced here: 48.5 us
  starting transfers between devices  20.1 us (41%)
  waiting for transfers between devices  17.4 us (36%)
  Pallas kernels  9.28 us (19%)
  other arithmetic  0.91 us (2%)
  between operations  0.83 us (2%)
    ppermute x6, waiting for transfers between devices, to_partner(): return lax.ppermute(block, 'half', [(0, 1), (1, 0)])  9.6 us
    ppermute x2, starting transfers between devices, up(): lax.ppermute(block, 'ctx', [(i, i + 2 * k) for i in range(ranks - 2 * k)])  9.29 us
    ppermute x6, starting transfers between devices, to_partner(): return lax.ppermute(block, 'half', [(0, 1), (1, 0)])  7.29 us
    ppermute x2, waiting for transfers between devices, down(): lax.ppermute(block, 'ctx', [(i + 2 * k, i) for i in range(ranks - 2 * k)])  5.58 us
    pallas_call x1, Pallas kernels, local(): pl.pallas_call(functools.partial(attention_kernel, hops), out_shape=[pltp...  5.32 us
    ppermute x2, starting transfers between devices, down(): lax.ppermute(block, 'ctx', [(i + 2 * k, i) for i in range(ranks - 2 * k)])  2.58 us
    ppermute x4, waiting for transfers between devices, to_side(): return lax.ppermute(block, 'ctx', [(i, i ^ 1) for i in range(ranks)])  1.24 us
    pallas_call x2, Pallas kernels, rows_of(): pl.pallas_call(functools.partial(rows_kernel, other), out_shape=pltpu.VME...  1.1 us
  transfers between devices with their start and end apart: 14, of which 8 were waited for; matrix products, arithmetic and copies ran while one was open for 0% of the time, Pallas kernels for 6%

profile of v5, /device:TPU:0, one launch (start us, length us, event | category | flops | bytes accessed | tf_op | source)
XLA Modules:
  0.0 48.5 jit_solution(10644924704891992866)
XLA Ops:
  0.6 0.0 copy-start
  0.6 0.0 copy-start.1
  0.7 1.0 %shard_map.93 = (bf16[272,128]{1,0:T(8,128)(2,1)S(1)}, bf16[272,128]{1,0:T(8,128)(2,1)S(1)}) custom-call(s32[4]{0:T(128)} %bitcast.19, bf16[128,256]{1,0:T(8,128)(2,1)} %bitcast.17, bf16[128,256]{1,0:T(8,128)(2,1)} %bitcast.18, s32[1,128]{1,0:T(1,128)} %docs_ref.1), custom_call_target="tpu_custom_call" | custom-call | tf_op jit(solution)/shard_map/pallas_call | solution.py:333
  1.7 0.5 %collective-permute-start = (bf16[272,128]{1,0:T(8,128)(2,1)S(1)}, bf16[272,128]{1,0:T(8,128)(2,1)S(1)}, u32[]{:S(2)}, u32[]{:S(2)}) collective-permute-start(bf16[272,128]{1,0:T(8,128)(2,1)S(1)} %get-tuple-element.34), channel_id=1, source_target_pairs={{0,1},{1,0},{2,3},{3,2},{4,5},{5,4},{6,7},{7,6},{8,9},{9,8},{10,11... | collective-permute-start | bytes 208904 | tf_op jit(solution)/shard_map/ppermute | solution.py:331
  2.2 1.0 %shard_map.94 = bf16[256,1024]{1,0:T(8,128)(2,1)S(1)} custom-call(bf16[128,2048]{1,0:T(8,128)(2,1)} %bitcast.11, bf16[128,2048]{1,0:T(8,128)(2,1)} %bitcast.13), custom_call_target="tpu_custom_call" | custom-call | tf_op jit(solution)/shard_map/pallas_call | solution.py:342
  3.2 0.0 collective-permute-done
  3.3 0.3 collective-permute-start.5
  3.5 4.8 %collective-permute-start.1 = (bf16[544,128]{1,0:T(8,128)(2,1)S(1)}, bf16[544,128]{1,0:T(8,128)(2,1)S(1)}, u32[]{:S(2)}, u32[]{:S(2)}) collective-permute-start(bf16[544,128]{1,0:T(8,128)(2,1)S(1)} %pad_maximum_fusion.1.refs_0_), channel_id=1, source_target_pairs={{0,2},{1,3},{2,4},{3,5},{4,6},{5,7},{8,10},{9,11},{10,12},{11,13},... | collective-permute-start | bytes 417800 | tf_op jit(solution)/shard_map/ppermute | solution.py:322
  8.3 4.5 %collective-permute-start.4 = (bf16[544,128]{1,0:T(8,128)(2,1)S(1)}, bf16[544,128]{1,0:T(8,128)(2,1)S(1)}, u32[]{:S(2)}, u32[]{:S(2)}) collective-permute-start(bf16[544,128]{1,0:T(8,128)(2,1)S(1)} %pad_maximum_fusion.1.refs_0_), channel_id=1, source_target_pairs={{0,4},{1,5},{2,6},{3,7},{8,12},{9,13},{10,14},{11,15},{16,20},{17,... | collective-permute-start | bytes 417800 | tf_op jit(solution)/shard_map/ppermute | solution.py:322
  12.8 1.6 %collective-permute-start.2 = (bf16[544,128]{1,0:T(8,128)(2,1)S(1)}, bf16[544,128]{1,0:T(8,128)(2,1)S(1)}, u32[]{:S(2)}, u32[]{:S(2)}) collective-permute-start(bf16[544,128]{1,0:T(8,128)(2,1)S(1)} %pad_maximum_fusion.1.refs_0_), channel_id=1, source_target_pairs={{0,16},{16,0},{1,17},{17,1},{2,18},{18,2},{3,19},{19,3},{4,20},{20... | collective-permute-start | bytes 417800 | tf_op jit(solution)/shard_map/ppermute | solution.py:328
  14.4 0.0 collective-permute-done.1.refs_1_
  14.4 0.5 %collective-permute-start.3 = (bf16[544,128]{1,0:T(8,128)(2,1)S(1)}, bf16[544,128]{1,0:T(8,128)(2,1)S(1)}, u32[]{:S(2)}, u32[]{:S(2)}) collective-permute-start(bf16[544,128]{1,0:T(8,128)(2,1)S(1)} %collective-permute-done.1.refs_1_), channel_id=1, source_target_pairs={{0,16},{16,0},{1,17},{17,1},{2,18},{18,2},{3,19},{19,3},{4,20},{20... | collective-permute-start | bytes 417800 | tf_op jit(solution)/shard_map/ppermute | solution.py:328
  14.9 0.9 %collective-permute-done.4.refs_2_ = bf16[544,128]{1,0:T(8,128)(2,1)S(1)} collective-permute-done((bf16[544,128]{1,0:T(8,128)(2,1)S(1)}, bf16[544,128]{1,0:T(8,128)(2,1)S(1)}, u32[]{:S(2)}, u32[]{:S(2)}) %collective-permute-start.4) | collective-permute-done | bytes 139296 | tf_op jit(solution)/shard_map/ppermute | solution.py:322
  15.9 1.5 %collective-permute-start.6 = (bf16[544,128]{1,0:T(8,128)(2,1)S(1)}, bf16[544,128]{1,0:T(8,128)(2,1)S(1)}, u32[]{:S(2)}, u32[]{:S(2)}) collective-permute-start(bf16[544,128]{1,0:T(8,128)(2,1)S(1)} %collective-permute-done.4.refs_2_), channel_id=1, source_target_pairs={{0,16},{16,0},{1,17},{17,1},{2,18},{18,2},{3,19},{19,3},{4,20},{20... | collective-permute-start | bytes 417800 | tf_op jit(solution)/shard_map/ppermute | solution.py:328
  17.4 2.1 %collective-permute-done.2.refs_2_.refs_3_ = bf16[544,128]{1,0:T(8,128)(2,1)S(1)} collective-permute-done((bf16[544,128]{1,0:T(8,128)(2,1)S(1)}, bf16[544,128]{1,0:T(8,128)(2,1)S(1)}, u32[]{:S(2)}, u32[]{:S(2)}) %collective-permute-start.2) | collective-permute-done | bytes 139296 | tf_op jit(solution)/shard_map/ppermute | solution.py:328
  19.5 3.0 %collective-permute-done.3.refs_3_.refs_4_ = bf16[544,128]{1,0:T(8,128)(2,1)S(1)} collective-permute-done((bf16[544,128]{1,0:T(8,128)(2,1)S(1)}, bf16[544,128]{1,0:T(8,128)(2,1)S(1)}, u32[]{:S(2)}, u32[]{:S(2)}) %collective-permute-start.3) | collective-permute-done | bytes 139296 | tf_op jit(solution)/shard_map/ppermute | solution.py:328
  22.5 0.0 copy-done
  22.5 0.0 copy-done.1
  22.5 0.1 shard_map.95
  22.5 0.2 shard_map.96
  22.8 0.0 collective-permute-done.5
  22.8 0.1 pad_maximum_fusion.rows_ref
  22.8 1.2 %collective-permute-done.6.refs_5_ = bf16[544,128]{1,0:T(8,128)(2,1)S(1)} collective-permute-done((bf16[544,128]{1,0:T(8,128)(2,1)S(1)}, bf16[544,128]{1,0:T(8,128)(2,1)S(1)}, u32[]{:S(2)}, u32[]{:S(2)}) %collective-permute-start.6) | collective-permute-done | bytes 139296 | tf_op jit(solution)/shard_map/ppermute | solution.py:328
  24.1 5.3 %shard_map.97 = (bf16[512,1024]{1,0:T(8,128)(2,1)S(1)}, bf16[512,128]{1,0:T(8,128)(2,1)S(1)}, bf16[512,128]{1,0:T(8,128)(2,1)S(1)}, bf16[512,128]{1,0:T(8,128)(2...) custom-call(bf16[512,1024]{1,0:T(8,128)(2,1)S(1)} %pad_maximum_fusion.rows_ref, ...), custom_call_target="tpu_custom_call" | custom-call | flops 2415919104 | bytes 4194304 | tf_op jit(solution)/shard_map/pallas_call | solution.py:371
  29.4 1.6 %collective-permute-start.7 = (bf16[512,128]{1,0:T(8,128)(2,1)S(1)}, bf16[512,128]{1,0:T(8,128)(2,1)S(1)}, u32[]{:S(2)}, u32[]{:S(2)}) collective-permute-start(bf16[512,128]{1,0:T(8,128)(2,1)S(1)} %get-tuple-element.49), channel_id=1, source_target_pairs={{0,16},{16,0},{1,17},{17,1},{2,18},{18,2},{3,19},{19,3},{4,20},{20... | collective-permute-start | bytes 393224 | tf_op jit(solution)/shard_map/ppermute | solution.py:328
  31.0 0.5 %collective-permute-start.10 = (bf16[512,128]{1,0:T(8,128)(2,1)S(1)}, bf16[512,128]{1,0:T(8,128)(2,1)S(1)}, u32[]{:S(2)}, u32[]{:S(2)}) collective-permute-start(bf16[512,128]{1,0:T(8,128)(2,1)S(1)} %get-tuple-element.59), channel_id=1, source_target_pairs={{0,16},{16,0},{1,17},{17,1},{2,18},{18,2},{3,19},{19,3},{4,20},{20... | collective-permute-start | bytes 393224 | tf_op jit(solution)/shard_map/ppermute | solution.py:328
  31.5 0.1 collective-permute-start.9
  31.6 1.6 %collective-permute-start.12 = (bf16[512,128]{1,0:T(8,128)(2,1)S(1)}, bf16[512,128]{1,0:T(8,128)(2,1)S(1)}, u32[]{:S(2)}, u32[]{:S(2)}) collective-permute-start(bf16[512,128]{1,0:T(8,128)(2,1)S(1)} %get-tuple-element.61), channel_id=1, source_target_pairs={{0,16},{16,0},{1,17},{17,1},{2,18},{18,2},{3,19},{19,3},{4,20},{20... | collective-permute-start | bytes 393224 | tf_op jit(solution)/shard_map/ppermute | solution.py:328
  33.2 2.0 %collective-permute-done.7 = bf16[512,128]{1,0:T(8,128)(2,1)S(1)} collective-permute-done((bf16[512,128]{1,0:T(8,128)(2,1)S(1)}, bf16[512,128]{1,0:T(8,128)(2,1)S(1)}, u32[]{:S(2)}, u32[]{:S(2)}) %collective-permute-start.7) | collective-permute-done | bytes 131104 | tf_op jit(solution)/shard_map/ppermute | solution.py:328
  35.3 1.3 %collective-permute-start.8 = (bf16[512,128]{1,0:T(8,128)(2,1)S(1)}, bf16[512,128]{1,0:T(8,128)(2,1)S(1)}, u32[]{:S(2)}, u32[]{:S(2)}) collective-permute-start(bf16[512,128]{1,0:T(8,128)(2,1)S(1)} %add_convert_fusion.2), channel_id=1, source_target_pairs={{4,0},{5,1},{6,2},{7,3},{12,8},{13,9},{14,10},{15,11},{20,16},{21,... | collective-permute-start | bytes 393224 | tf_op jit(solution)/shard_map/ppermute | solution.py:325
  36.6 1.2 %collective-permute-done.10 = bf16[512,128]{1,0:T(8,128)(2,1)S(1)} collective-permute-done((bf16[512,128]{1,0:T(8,128)(2,1)S(1)}, bf16[512,128]{1,0:T(8,128)(2,1)S(1)}, u32[]{:S(2)}, u32[]{:S(2)}) %collective-permute-start.10) | collective-permute-done | bytes 131104 | tf_op jit(solution)/shard_map/ppermute | solution.py:328
  37.9 1.3 %collective-permute-start.11 = (bf16[512,128]{1,0:T(8,128)(2,1)S(1)}, bf16[512,128]{1,0:T(8,128)(2,1)S(1)}, u32[]{:S(2)}, u32[]{:S(2)}) collective-permute-start(bf16[512,128]{1,0:T(8,128)(2,1)S(1)} %add_convert_fusion.1), channel_id=1, source_target_pairs={{2,0},{3,1},{4,2},{5,3},{6,4},{7,5},{10,8},{11,9},{12,10},{13,11},... | collective-permute-start | bytes 393224 | tf_op jit(solution)/shard_map/ppermute | solution.py:325
  39.2 0.8 %shard_map.98 = (bf16[128,2048]{1,0:T(8,128)(2,1)}, bf16[128,2048]{1,0:T(8,128)(2,1)}) custom-call(bf16[512,1024]{1,0:T(8,128)(2,1)S(1)} %get-tuple-element.50.own_ref), custom_call_target="tpu_custom_call" | custom-call | bytes 4194304 | tf_op jit(solution)/shard_map/pallas_call | solution.py:399
  40.0 0.0 collective-permute-done.9.side_ref
  40.0 0.8 %shard_map.99 = (bf16[128,2048]{1,0:T(8,128)(2,1)}, bf16[128,2048]{1,0:T(8,128)(2,1)}) custom-call(bf16[256,1024]{1,0:T(8,128)(2,1)S(1)} %collective-permute-done.9.side_ref, bf16[128,2048]{1,0:T(8,128)(2,1)} %get-tuple-element.51.out_held, bf16[128,2048]{1,0:T(8,128)(2,1)} %get-tuple-element.52.query_grad_held), custom_call_target="tpu_custom_call", output_to_operand_aliasing={{0}: (1, {}), {1}: (2, {})} | custom-call | tf_op jit(solution)/shard_map/pallas_call | solution.py:418
  40.8 5.6 %collective-permute-done.8 = bf16[512,128]{1,0:T(8,128)(2,1)S(1)} collective-permute-done((bf16[512,128]{1,0:T(8,128)(2,1)S(1)}, bf16[512,128]{1,0:T(8,128)(2,1)S(1)}, u32[]{:S(2)}, u32[]{:S(2)}) %collective-permute-start.8) | collective-permute-done | bytes 131104 | tf_op jit(solution)/shard_map/ppermute | solution.py:325
  46.4 0.0 collective-permute-done.12
  46.4 0.0 collective-permute-done.11
  46.4 0.1 add_convert_fusion
  46.5 0.1 collective-permute-start.13
  46.6 1.2 %collective-permute-done.13 = bf16[256,128]{1,0:T(8,128)(2,1)S(1)} collective-permute-done((bf16[256,128]{1,0:T(8,128)(2,1)S(1)}, bf16[256,128]{1,0:T(8,128)(2,1)S(1)}, u32[]{:S(2)}, u32[]{:S(2)}) %collective-permute-start.13) | collective-permute-done | bytes 65568 | tf_op jit(solution)/shard_map/ppermute | solution.py:331
  47.8 0.7 %fusion.2 = (bf16[1,128,256]{2,1,0:T(8,128)(2,1)}, bf16[1,128,256]{2,1,0:T(8,128)(2,1)}) fusion(bf16[256,128]{1,0:T(8,128)(2,1)S(1)} %get-tuple-element.62, bf16[256,128]{1,0:T(8,128)(2,1)S(1)} %get-tuple-element.63), kind=kLoop, calls=%fused_computation.10 | loop fusion | flops 262144 | bytes 262144 | tf_op jit(solution)/shard_map/broadcast_in_dim | solution.py:435
  (6 shorter events, 0.1 us)
Async XLA Ops:
  0.6 21.8 %copy-start = (bf16[1,128,2048]{2,1,0:T(8,128)(2,1)S(1)}, bf16[1,128,2048]{2,1,0:T(8,128)(2,1)}, u32[]{:S(2)}) copy-start(bf16[1,128,2048]{2,1,0:T(8,128)(2,1)} %param.6) | copy-start | bytes 1572868
  0.6 21.8 %copy-start.1 = (bf16[1,128,2048]{2,1,0:T(8,128)(2,1)S(1)}, bf16[1,128,2048]{2,1,0:T(8,128)(2,1)}, u32[]{:S(2)}) copy-start(bf16[1,128,2048]{2,1,0:T(8,128)(2,1)} %param.9) | copy-start | bytes 1572868
  1.7 1.6 %collective-permute-start = (bf16[272,128]{1,0:T(8,128)(2,1)S(1)}, bf16[272,128]{1,0:T(8,128)(2,1)S(1)}, u32[]{:S(2)}, u32[]{:S(2)}) collective-permute-start(bf16[272,128]{1,0:T(8,128)(2,1)S(1)} %get-tuple-element.34), channel_id=1, source_target_pairs={{0,1},{1,0},{2,3},{3,2},{4,5},{5,4},{6,7},{7,6},{8,9},{9,8},{10,11... | collective-permute-start | bytes 208904 | tf_op jit(solution)/shard_map/ppermute | solution.py:331
  3.3 19.5 %collective-permute-start.5 = (bf16[256,1024]{1,0:T(8,128)(2,1)S(1)}, bf16[256,1024]{1,0:T(8,128)(2,1)S(1)}, u32[]{:S(2)}, u32[]{:S(2)}) collective-permute-start(bf16[256,1024]{1,0:T(8,128)(2,1)S(1)} %shard_map.94), channel_id=1, source_target_pairs={{0,1},{1,0},{2,3},{3,2},{4,5},{5,4},{6,7},{7,6},{8,9},{9,8},{10,11... | collective-permute-start | bytes 1572872 | tf_op jit(solution)/shard_map/ppermute | solution.py:331
  3.5 10.9 %collective-permute-start.1 = (bf16[544,128]{1,0:T(8,128)(2,1)S(1)}, bf16[544,128]{1,0:T(8,128)(2,1)S(1)}, u32[]{:S(2)}, u32[]{:S(2)}) collective-permute-start(bf16[544,128]{1,0:T(8,128)(2,1)S(1)} %pad_maximum_fusion.1.refs_0_), channel_id=1, source_target_pairs={{0,2},{1,3},{2,4},{3,5},{4,6},{5,7},{8,10},{9,11},{10,12},{11,13},... | collective-permute-start | bytes 417800 | tf_op jit(solution)/shard_map/ppermute | solution.py:322
  8.3 7.5 %collective-permute-start.4 = (bf16[544,128]{1,0:T(8,128)(2,1)S(1)}, bf16[544,128]{1,0:T(8,128)(2,1)S(1)}, u32[]{:S(2)}, u32[]{:S(2)}) collective-permute-start(bf16[544,128]{1,0:T(8,128)(2,1)S(1)} %pad_maximum_fusion.1.refs_0_), channel_id=1, source_target_pairs={{0,4},{1,5},{2,6},{3,7},{8,12},{9,13},{10,14},{11,15},{16,20},{17,... | collective-permute-start | bytes 417800 | tf_op jit(solution)/shard_map/ppermute | solution.py:322
  12.8 6.7 %collective-permute-start.2 = (bf16[544,128]{1,0:T(8,128)(2,1)S(1)}, bf16[544,128]{1,0:T(8,128)(2,1)S(1)}, u32[]{:S(2)}, u32[]{:S(2)}) collective-permute-start(bf16[544,128]{1,0:T(8,128)(2,1)S(1)} %pad_maximum_fusion.1.refs_0_), channel_id=1, source_target_pairs={{0,16},{16,0},{1,17},{17,1},{2,18},{18,2},{3,19},{19,3},{4,20},{20... | collective-permute-start | bytes 417800 | tf_op jit(solution)/shard_map/ppermute | solution.py:328
  14.4 8.0 %collective-permute-start.3 = (bf16[544,128]{1,0:T(8,128)(2,1)S(1)}, bf16[544,128]{1,0:T(8,128)(2,1)S(1)}, u32[]{:S(2)}, u32[]{:S(2)}) collective-permute-start(bf16[544,128]{1,0:T(8,128)(2,1)S(1)} %collective-permute-done.1.refs_1_), channel_id=1, source_target_pairs={{0,16},{16,0},{1,17},{17,1},{2,18},{18,2},{3,19},{19,3},{4,20},{20... | collective-permute-start | bytes 417800 | tf_op jit(solution)/shard_map/ppermute | solution.py:328
  15.9 8.2 %collective-permute-start.6 = (bf16[544,128]{1,0:T(8,128)(2,1)S(1)}, bf16[544,128]{1,0:T(8,128)(2,1)S(1)}, u32[]{:S(2)}, u32[]{:S(2)}) collective-permute-start(bf16[544,128]{1,0:T(8,128)(2,1)S(1)} %collective-permute-done.4.refs_2_), channel_id=1, source_target_pairs={{0,16},{16,0},{1,17},{17,1},{2,18},{18,2},{3,19},{19,3},{4,20},{20... | collective-permute-start | bytes 417800 | tf_op jit(solution)/shard_map/ppermute | solution.py:328
  29.4 5.8 %collective-permute-start.7 = (bf16[512,128]{1,0:T(8,128)(2,1)S(1)}, bf16[512,128]{1,0:T(8,128)(2,1)S(1)}, u32[]{:S(2)}, u32[]{:S(2)}) collective-permute-start(bf16[512,128]{1,0:T(8,128)(2,1)S(1)} %get-tuple-element.49), channel_id=1, source_target_pairs={{0,16},{16,0},{1,17},{17,1},{2,18},{18,2},{3,19},{19,3},{4,20},{20... | collective-permute-start | bytes 393224 | tf_op jit(solution)/shard_map/ppermute | solution.py:328
  31.0 6.8 %collective-permute-start.10 = (bf16[512,128]{1,0:T(8,128)(2,1)S(1)}, bf16[512,128]{1,0:T(8,128)(2,1)S(1)}, u32[]{:S(2)}, u32[]{:S(2)}) collective-permute-start(bf16[512,128]{1,0:T(8,128)(2,1)S(1)} %get-tuple-element.59), channel_id=1, source_target_pairs={{0,16},{16,0},{1,17},{17,1},{2,18},{18,2},{3,19},{19,3},{4,20},{20... | collective-permute-start | bytes 393224 | tf_op jit(solution)/shard_map/ppermute | solution.py:328
  31.5 8.5 %collective-permute-start.9 = (bf16[256,1024]{1,0:T(8,128)(2,1)S(1)}, bf16[256,1024]{1,0:T(8,128)(2,1)S(1)}, u32[]{:S(2)}, u32[]{:S(2)}) collective-permute-start(bf16[256,1024]{1,0:T(8,128)(2,1)S(1)} %slice.15), channel_id=1, source_target_pairs={{0,1},{1,0},{2,3},{3,2},{4,5},{5,4},{6,7},{7,6},{8,9},{9,8},{10,11... | collective-permute-start | bytes 1572872 | tf_op jit(solution)/shard_map/ppermute | solution.py:331
  31.6 14.8 %collective-permute-start.12 = (bf16[512,128]{1,0:T(8,128)(2,1)S(1)}, bf16[512,128]{1,0:T(8,128)(2,1)S(1)}, u32[]{:S(2)}, u32[]{:S(2)}) collective-permute-start(bf16[512,128]{1,0:T(8,128)(2,1)S(1)} %get-tuple-element.61), channel_id=1, source_target_pairs={{0,16},{16,0},{1,17},{17,1},{2,18},{18,2},{3,19},{19,3},{4,20},{20... | collective-permute-start | bytes 393224 | tf_op jit(solution)/shard_map/ppermute | solution.py:328
  35.3 11.1 %collective-permute-start.8 = (bf16[512,128]{1,0:T(8,128)(2,1)S(1)}, bf16[512,128]{1,0:T(8,128)(2,1)S(1)}, u32[]{:S(2)}, u32[]{:S(2)}) collective-permute-start(bf16[512,128]{1,0:T(8,128)(2,1)S(1)} %add_convert_fusion.2), channel_id=1, source_target_pairs={{4,0},{5,1},{6,2},{7,3},{12,8},{13,9},{14,10},{15,11},{20,16},{21,... | collective-permute-start | bytes 393224 | tf_op jit(solution)/shard_map/ppermute | solution.py:325
  37.9 8.6 %collective-permute-start.11 = (bf16[512,128]{1,0:T(8,128)(2,1)S(1)}, bf16[512,128]{1,0:T(8,128)(2,1)S(1)}, u32[]{:S(2)}, u32[]{:S(2)}) collective-permute-start(bf16[512,128]{1,0:T(8,128)(2,1)S(1)} %add_convert_fusion.1), channel_id=1, source_target_pairs={{2,0},{3,1},{4,2},{5,3},{6,4},{7,5},{10,8},{11,9},{12,10},{13,11},... | collective-permute-start | bytes 393224 | tf_op jit(solution)/shard_map/ppermute | solution.py:325
  46.5 1.3 %collective-permute-start.13 = (bf16[256,128]{1,0:T(8,128)(2,1)S(1)}, bf16[256,128]{1,0:T(8,128)(2,1)S(1)}, u32[]{:S(2)}, u32[]{:S(2)}) collective-permute-start(bf16[256,128]{1,0:T(8,128)(2,1)S(1)} %slice.21), channel_id=1, source_target_pairs={{0,1},{1,0},{2,3},{3,2},{4,5},{5,4},{6,7},{7,6},{8,9},{9,8},{10,11... | collective-permute-start | bytes 196616 | tf_op jit(solution)/shard_map/ppermute | solution.py:331

commit v6 on v5

--- a/solution.py
+++ b/solution.py
@@ -15,7 +15,7 @@
 META = 16
 DOC_ROW = NBLK
 DOC_VALUES = 16
-GROUPED = 4
+GROUPED = 2
 HALF = QUERY_PER_KEY * HEAD_SIZE
 NEG = -1e30
 F32, BF16, I32 = jnp.float32, jnp.bfloat16, jnp.int32

time: 48.6 us -> 48.7 us (level)
  no operation moved by 1% of the time
where the time goes in v6:
time: 48.7 us; the launch traced here: 48.5 us
  starting transfers between devices  19.8 us (41%)
  waiting for transfers between devices  17.3 us (36%)
  Pallas kernels  9.7 us (20%)
  other arithmetic  0.91 us (2%)
  between operations  0.83 us (2%)
    ppermute x6, waiting for transfers between devices, to_partner(): return lax.ppermute(block, 'half', [(0, 1), (1, 0)])  9.9 us
    ppermute x2, starting transfers between devices, up(): lax.ppermute(block, 'ctx', [(i, i + 2 * k) for i in range(ranks - 2 * k)])  9.29 us
    ppermute x6, starting transfers between devices, to_partner(): return lax.ppermute(block, 'half', [(0, 1), (1, 0)])  6.98 us
    pallas_call x1, Pallas kernels, local(): pl.pallas_call(functools.partial(attention_kernel, hops), out_shape=[pltp...  5.74 us
    ppermute x2, waiting for transfers between devices, down(): lax.ppermute(block, 'ctx', [(i + 2 * k, i) for i in range(ranks - 2 * k)])  5.18 us
    ppermute x2, starting transfers between devices, down(): lax.ppermute(block, 'ctx', [(i + 2 * k, i) for i in range(ranks - 2 * k)])  2.58 us
    ppermute x4, waiting for transfers between devices, to_side(): return lax.ppermute(block, 'ctx', [(i, i ^ 1) for i in range(ranks)])  1.24 us
    pallas_call x2, Pallas kernels, rows_of(): pl.pallas_call(functools.partial(rows_kernel, other), out_shape=pltpu.VME...  1.1 us
  transfers between devices with their start and end apart: 14, of which 8 were waited for; matrix products, arithmetic and copies ran while one was open for 0% of the time, Pallas kernels for 6%

profile of v6, /device:TPU:0, one launch (start us, length us, event | category | flops | bytes accessed | tf_op | source)
XLA Modules:
  0.0 48.5 jit_solution(3789098793493576754)
XLA Ops:
  0.6 0.0 copy-start
  0.6 0.0 copy-start.1
  0.7 1.0 %shard_map.93 = (bf16[272,128]{1,0:T(8,128)(2,1)S(1)}, bf16[272,128]{1,0:T(8,128)(2,1)S(1)}) custom-call(s32[4]{0:T(128)} %bitcast.19, bf16[128,256]{1,0:T(8,128)(2,1)} %bitcast.17, bf16[128,256]{1,0:T(8,128)(2,1)} %bitcast.18, s32[1,128]{1,0:T(1,128)} %docs_ref.1), custom_call_target="tpu_custom_call" | custom-call | tf_op jit(solution)/shard_map/pallas_call | solution.py:333
  1.7 0.5 %collective-permute-start = (bf16[272,128]{1,0:T(8,128)(2,1)S(1)}, bf16[272,128]{1,0:T(8,128)(2,1)S(1)}, u32[]{:S(2)}, u32[]{:S(2)}) collective-permute-start(bf16[272,128]{1,0:T(8,128)(2,1)S(1)} %get-tuple-element.34), channel_id=1, source_target_pairs={{0,1},{1,0},{2,3},{3,2},{4,5},{5,4},{6,7},{7,6},{8,9},{9,8},{10,11... | collective-permute-start | bytes 208904 | tf_op jit(solution)/shard_map/ppermute | solution.py:331
  2.2 1.0 %shard_map.94 = bf16[256,1024]{1,0:T(8,128)(2,1)S(1)} custom-call(bf16[128,2048]{1,0:T(8,128)(2,1)} %bitcast.11, bf16[128,2048]{1,0:T(8,128)(2,1)} %bitcast.13), custom_call_target="tpu_custom_call" | custom-call | tf_op jit(solution)/shard_map/pallas_call | solution.py:342
  3.2 0.0 collective-permute-done
  3.3 0.3 collective-permute-start.5
  3.5 4.8 %collective-permute-start.1 = (bf16[544,128]{1,0:T(8,128)(2,1)S(1)}, bf16[544,128]{1,0:T(8,128)(2,1)S(1)}, u32[]{:S(2)}, u32[]{:S(2)}) collective-permute-start(bf16[544,128]{1,0:T(8,128)(2,1)S(1)} %pad_maximum_fusion.1.refs_0_), channel_id=1, source_target_pairs={{0,2},{1,3},{2,4},{3,5},{4,6},{5,7},{8,10},{9,11},{10,12},{11,13},... | collective-permute-start | bytes 417800 | tf_op jit(solution)/shard_map/ppermute | solution.py:322
  8.3 4.5 %collective-permute-start.4 = (bf16[544,128]{1,0:T(8,128)(2,1)S(1)}, bf16[544,128]{1,0:T(8,128)(2,1)S(1)}, u32[]{:S(2)}, u32[]{:S(2)}) collective-permute-start(bf16[544,128]{1,0:T(8,128)(2,1)S(1)} %pad_maximum_fusion.1.refs_0_), channel_id=1, source_target_pairs={{0,4},{1,5},{2,6},{3,7},{8,12},{9,13},{10,14},{11,15},{16,20},{17,... | collective-permute-start | bytes 417800 | tf_op jit(solution)/shard_map/ppermute | solution.py:322
  12.8 1.6 %collective-permute-start.2 = (bf16[544,128]{1,0:T(8,128)(2,1)S(1)}, bf16[544,128]{1,0:T(8,128)(2,1)S(1)}, u32[]{:S(2)}, u32[]{:S(2)}) collective-permute-start(bf16[544,128]{1,0:T(8,128)(2,1)S(1)} %pad_maximum_fusion.1.refs_0_), channel_id=1, source_target_pairs={{0,16},{16,0},{1,17},{17,1},{2,18},{18,2},{3,19},{19,3},{4,20},{20... | collective-permute-start | bytes 417800 | tf_op jit(solution)/shard_map/ppermute | solution.py:328
  14.4 0.0 collective-permute-done.1.refs_1_
  14.4 0.5 %collective-permute-start.3 = (bf16[544,128]{1,0:T(8,128)(2,1)S(1)}, bf16[544,128]{1,0:T(8,128)(2,1)S(1)}, u32[]{:S(2)}, u32[]{:S(2)}) collective-permute-start(bf16[544,128]{1,0:T(8,128)(2,1)S(1)} %collective-permute-done.1.refs_1_), channel_id=1, source_target_pairs={{0,16},{16,0},{1,17},{17,1},{2,18},{18,2},{3,19},{19,3},{4,20},{20... | collective-permute-start | bytes 417800 | tf_op jit(solution)/shard_map/ppermute | solution.py:328
  14.9 0.9 %collective-permute-done.4.refs_2_ = bf16[544,128]{1,0:T(8,128)(2,1)S(1)} collective-permute-done((bf16[544,128]{1,0:T(8,128)(2,1)S(1)}, bf16[544,128]{1,0:T(8,128)(2,1)S(1)}, u32[]{:S(2)}, u32[]{:S(2)}) %collective-permute-start.4) | collective-permute-done | bytes 139296 | tf_op jit(solution)/shard_map/ppermute | solution.py:322
  15.9 1.5 %collective-permute-start.6 = (bf16[544,128]{1,0:T(8,128)(2,1)S(1)}, bf16[544,128]{1,0:T(8,128)(2,1)S(1)}, u32[]{:S(2)}, u32[]{:S(2)}) collective-permute-start(bf16[544,128]{1,0:T(8,128)(2,1)S(1)} %collective-permute-done.4.refs_2_), channel_id=1, source_target_pairs={{0,16},{16,0},{1,17},{17,1},{2,18},{18,2},{3,19},{19,3},{4,20},{20... | collective-permute-start | bytes 417800 | tf_op jit(solution)/shard_map/ppermute | solution.py:328
  17.4 2.1 %collective-permute-done.2.refs_2_.refs_3_ = bf16[544,128]{1,0:T(8,128)(2,1)S(1)} collective-permute-done((bf16[544,128]{1,0:T(8,128)(2,1)S(1)}, bf16[544,128]{1,0:T(8,128)(2,1)S(1)}, u32[]{:S(2)}, u32[]{:S(2)}) %collective-permute-start.2) | collective-permute-done | bytes 139296 | tf_op jit(solution)/shard_map/ppermute | solution.py:328
  19.5 3.0 %collective-permute-done.3.refs_3_.refs_4_ = bf16[544,128]{1,0:T(8,128)(2,1)S(1)} collective-permute-done((bf16[544,128]{1,0:T(8,128)(2,1)S(1)}, bf16[544,128]{1,0:T(8,128)(2,1)S(1)}, u32[]{:S(2)}, u32[]{:S(2)}) %collective-permute-start.3) | collective-permute-done | bytes 139296 | tf_op jit(solution)/shard_map/ppermute | solution.py:328
  22.5 0.0 copy-done
  22.5 0.0 copy-done.1
  22.5 0.1 shard_map.95
  22.5 0.2 shard_map.96
  22.8 0.0 collective-permute-done.5
  22.8 0.1 pad_maximum_fusion.rows_ref
  22.8 1.2 %collective-permute-done.6.refs_5_ = bf16[544,128]{1,0:T(8,128)(2,1)S(1)} collective-permute-done((bf16[544,128]{1,0:T(8,128)(2,1)S(1)}, bf16[544,128]{1,0:T(8,128)(2,1)S(1)}, u32[]{:S(2)}, u32[]{:S(2)}) %collective-permute-start.6) | collective-permute-done | bytes 139296 | tf_op jit(solution)/shard_map/ppermute | solution.py:328
  24.1 5.7 %shard_map.97 = (bf16[512,1024]{1,0:T(8,128)(2,1)S(1)}, bf16[512,128]{1,0:T(8,128)(2,1)S(1)}, bf16[512,128]{1,0:T(8,128)(2,1)S(1)}, bf16[512,128]{1,0:T(8,128)(2...) custom-call(bf16[512,1024]{1,0:T(8,128)(2,1)S(1)} %pad_maximum_fusion.rows_ref, ...), custom_call_target="tpu_custom_call" | custom-call | flops 2415919104 | bytes 4194304 | tf_op jit(solution)/shard_map/pallas_call | solution.py:371
  29.8 1.3 %collective-permute-start.7 = (bf16[512,128]{1,0:T(8,128)(2,1)S(1)}, bf16[512,128]{1,0:T(8,128)(2,1)S(1)}, u32[]{:S(2)}, u32[]{:S(2)}) collective-permute-start(bf16[512,128]{1,0:T(8,128)(2,1)S(1)} %get-tuple-element.49), channel_id=1, source_target_pairs={{0,16},{16,0},{1,17},{17,1},{2,18},{18,2},{3,19},{19,3},{4,20},{20... | collective-permute-start | bytes 393224 | tf_op jit(solution)/shard_map/ppermute | solution.py:328
  31.1 0.8 %collective-permute-start.10 = (bf16[512,128]{1,0:T(8,128)(2,1)S(1)}, bf16[512,128]{1,0:T(8,128)(2,1)S(1)}, u32[]{:S(2)}, u32[]{:S(2)}) collective-permute-start(bf16[512,128]{1,0:T(8,128)(2,1)S(1)} %get-tuple-element.59), channel_id=1, source_target_pairs={{0,16},{16,0},{1,17},{17,1},{2,18},{18,2},{3,19},{19,3},{4,20},{20... | collective-permute-start | bytes 393224 | tf_op jit(solution)/shard_map/ppermute | solution.py:328
  32.0 0.1 collective-permute-start.9
  32.0 1.3 %collective-permute-start.12 = (bf16[512,128]{1,0:T(8,128)(2,1)S(1)}, bf16[512,128]{1,0:T(8,128)(2,1)S(1)}, u32[]{:S(2)}, u32[]{:S(2)}) collective-permute-start(bf16[512,128]{1,0:T(8,128)(2,1)S(1)} %get-tuple-element.61), channel_id=1, source_target_pairs={{0,16},{16,0},{1,17},{17,1},{2,18},{18,2},{3,19},{19,3},{4,20},{20... | collective-permute-start | bytes 393224 | tf_op jit(solution)/shard_map/ppermute | solution.py:328
  33.3 2.3 %collective-permute-done.7 = bf16[512,128]{1,0:T(8,128)(2,1)S(1)} collective-permute-done((bf16[512,128]{1,0:T(8,128)(2,1)S(1)}, bf16[512,128]{1,0:T(8,128)(2,1)S(1)}, u32[]{:S(2)}, u32[]{:S(2)}) %collective-permute-start.7) | collective-permute-done | bytes 131104 | tf_op jit(solution)/shard_map/ppermute | solution.py:328
  35.7 1.3 %collective-permute-start.8 = (bf16[512,128]{1,0:T(8,128)(2,1)S(1)}, bf16[512,128]{1,0:T(8,128)(2,1)S(1)}, u32[]{:S(2)}, u32[]{:S(2)}) collective-permute-start(bf16[512,128]{1,0:T(8,128)(2,1)S(1)} %add_convert_fusion.2), channel_id=1, source_target_pairs={{4,0},{5,1},{6,2},{7,3},{12,8},{13,9},{14,10},{15,11},{20,16},{21,... | collective-permute-start | bytes 393224 | tf_op jit(solution)/shard_map/ppermute | solution.py:325
  37.0 1.2 %collective-permute-done.10 = bf16[512,128]{1,0:T(8,128)(2,1)S(1)} collective-permute-done((bf16[512,128]{1,0:T(8,128)(2,1)S(1)}, bf16[512,128]{1,0:T(8,128)(2,1)S(1)}, u32[]{:S(2)}, u32[]{:S(2)}) %collective-permute-start.10) | collective-permute-done | bytes 131104 | tf_op jit(solution)/shard_map/ppermute | solution.py:328
  38.3 1.3 %collective-permute-start.11 = (bf16[512,128]{1,0:T(8,128)(2,1)S(1)}, bf16[512,128]{1,0:T(8,128)(2,1)S(1)}, u32[]{:S(2)}, u32[]{:S(2)}) collective-permute-start(bf16[512,128]{1,0:T(8,128)(2,1)S(1)} %add_convert_fusion.1), channel_id=1, source_target_pairs={{2,0},{3,1},{4,2},{5,3},{6,4},{7,5},{10,8},{11,9},{12,10},{13,11},... | collective-permute-start | bytes 393224 | tf_op jit(solution)/shard_map/ppermute | solution.py:325
  39.6 0.8 %shard_map.98 = (bf16[128,2048]{1,0:T(8,128)(2,1)}, bf16[128,2048]{1,0:T(8,128)(2,1)}) custom-call(bf16[512,1024]{1,0:T(8,128)(2,1)S(1)} %get-tuple-element.50.own_ref), custom_call_target="tpu_custom_call" | custom-call | bytes 4194304 | tf_op jit(solution)/shard_map/pallas_call | solution.py:399
  40.4 0.0 collective-permute-done.9.side_ref
  40.4 0.8 %shard_map.99 = (bf16[128,2048]{1,0:T(8,128)(2,1)}, bf16[128,2048]{1,0:T(8,128)(2,1)}) custom-call(bf16[256,1024]{1,0:T(8,128)(2,1)S(1)} %collective-permute-done.9.side_ref, bf16[128,2048]{1,0:T(8,128)(2,1)} %get-tuple-element.51.out_held, bf16[128,2048]{1,0:T(8,128)(2,1)} %get-tuple-element.52.query_grad_held), custom_call_target="tpu_custom_call", output_to_operand_aliasing={{0}: (1, {}), {1}: (2, {})} | custom-call | tf_op jit(solution)/shard_map/pallas_call | solution.py:418
  41.2 5.2 %collective-permute-done.8 = bf16[512,128]{1,0:T(8,128)(2,1)S(1)} collective-permute-done((bf16[512,128]{1,0:T(8,128)(2,1)S(1)}, bf16[512,128]{1,0:T(8,128)(2,1)S(1)}, u32[]{:S(2)}, u32[]{:S(2)}) %collective-permute-start.8) | collective-permute-done | bytes 131104 | tf_op jit(solution)/shard_map/ppermute | solution.py:325
  46.4 0.0 collective-permute-done.12
  46.4 0.0 collective-permute-done.11
  46.4 0.1 add_convert_fusion
  46.5 0.1 collective-permute-start.13
  46.6 1.2 %collective-permute-done.13 = bf16[256,128]{1,0:T(8,128)(2,1)S(1)} collective-permute-done((bf16[256,128]{1,0:T(8,128)(2,1)S(1)}, bf16[256,128]{1,0:T(8,128)(2,1)S(1)}, u32[]{:S(2)}, u32[]{:S(2)}) %collective-permute-start.13) | collective-permute-done | bytes 65568 | tf_op jit(solution)/shard_map/ppermute | solution.py:331
  47.8 0.7 %fusion.2 = (bf16[1,128,256]{2,1,0:T(8,128)(2,1)}, bf16[1,128,256]{2,1,0:T(8,128)(2,1)}) fusion(bf16[256,128]{1,0:T(8,128)(2,1)S(1)} %get-tuple-element.62, bf16[256,128]{1,0:T(8,128)(2,1)S(1)} %get-tuple-element.63), kind=kLoop, calls=%fused_computation.10 | loop fusion | flops 262144 | bytes 262144 | tf_op jit(solution)/shard_map/broadcast_in_dim | solution.py:435
  (6 shorter events, 0.1 us)
Async XLA Ops:
  0.6 21.8 %copy-start = (bf16[1,128,2048]{2,1,0:T(8,128)(2,1)S(1)}, bf16[1,128,2048]{2,1,0:T(8,128)(2,1)}, u32[]{:S(2)}) copy-start(bf16[1,128,2048]{2,1,0:T(8,128)(2,1)} %param.6) | copy-start | bytes 1572868
  0.6 21.8 %copy-start.1 = (bf16[1,128,2048]{2,1,0:T(8,128)(2,1)S(1)}, bf16[1,128,2048]{2,1,0:T(8,128)(2,1)}, u32[]{:S(2)}) copy-start(bf16[1,128,2048]{2,1,0:T(8,128)(2,1)} %param.9) | copy-start | bytes 1572868
  1.7 1.6 %collective-permute-start = (bf16[272,128]{1,0:T(8,128)(2,1)S(1)}, bf16[272,128]{1,0:T(8,128)(2,1)S(1)}, u32[]{:S(2)}, u32[]{:S(2)}) collective-permute-start(bf16[272,128]{1,0:T(8,128)(2,1)S(1)} %get-tuple-element.34), channel_id=1, source_target_pairs={{0,1},{1,0},{2,3},{3,2},{4,5},{5,4},{6,7},{7,6},{8,9},{9,8},{10,11... | collective-permute-start | bytes 208904 | tf_op jit(solution)/shard_map/ppermute | solution.py:331
  3.3 19.5 %collective-permute-start.5 = (bf16[256,1024]{1,0:T(8,128)(2,1)S(1)}, bf16[256,1024]{1,0:T(8,128)(2,1)S(1)}, u32[]{:S(2)}, u32[]{:S(2)}) collective-permute-start(bf16[256,1024]{1,0:T(8,128)(2,1)S(1)} %shard_map.94), channel_id=1, source_target_pairs={{0,1},{1,0},{2,3},{3,2},{4,5},{5,4},{6,7},{7,6},{8,9},{9,8},{10,11... | collective-permute-start | bytes 1572872 | tf_op jit(solution)/shard_map/ppermute | solution.py:331
  3.5 10.9 %collective-permute-start.1 = (bf16[544,128]{1,0:T(8,128)(2,1)S(1)}, bf16[544,128]{1,0:T(8,128)(2,1)S(1)}, u32[]{:S(2)}, u32[]{:S(2)}) collective-permute-start(bf16[544,128]{1,0:T(8,128)(2,1)S(1)} %pad_maximum_fusion.1.refs_0_), channel_id=1, source_target_pairs={{0,2},{1,3},{2,4},{3,5},{4,6},{5,7},{8,10},{9,11},{10,12},{11,13},... | collective-permute-start | bytes 417800 | tf_op jit(solution)/shard_map/ppermute | solution.py:322
  8.3 7.5 %collective-permute-start.4 = (bf16[544,128]{1,0:T(8,128)(2,1)S(1)}, bf16[544,128]{1,0:T(8,128)(2,1)S(1)}, u32[]{:S(2)}, u32[]{:S(2)}) collective-permute-start(bf16[544,128]{1,0:T(8,128)(2,1)S(1)} %pad_maximum_fusion.1.refs_0_), channel_id=1, source_target_pairs={{0,4},{1,5},{2,6},{3,7},{8,12},{9,13},{10,14},{11,15},{16,20},{17,... | collective-permute-start | bytes 417800 | tf_op jit(solution)/shard_map/ppermute | solution.py:322
  12.8 6.7 %collective-permute-start.2 = (bf16[544,128]{1,0:T(8,128)(2,1)S(1)}, bf16[544,128]{1,0:T(8,128)(2,1)S(1)}, u32[]{:S(2)}, u32[]{:S(2)}) collective-permute-start(bf16[544,128]{1,0:T(8,128)(2,1)S(1)} %pad_maximum_fusion.1.refs_0_), channel_id=1, source_target_pairs={{0,16},{16,0},{1,17},{17,1},{2,18},{18,2},{3,19},{19,3},{4,20},{20... | collective-permute-start | bytes 417800 | tf_op jit(solution)/shard_map/ppermute | solution.py:328
  14.4 8.0 %collective-permute-start.3 = (bf16[544,128]{1,0:T(8,128)(2,1)S(1)}, bf16[544,128]{1,0:T(8,128)(2,1)S(1)}, u32[]{:S(2)}, u32[]{:S(2)}) collective-permute-start(bf16[544,128]{1,0:T(8,128)(2,1)S(1)} %collective-permute-done.1.refs_1_), channel_id=1, source_target_pairs={{0,16},{16,0},{1,17},{17,1},{2,18},{18,2},{3,19},{19,3},{4,20},{20... | collective-permute-start | bytes 417800 | tf_op jit(solution)/shard_map/ppermute | solution.py:328
  15.9 8.2 %collective-permute-start.6 = (bf16[544,128]{1,0:T(8,128)(2,1)S(1)}, bf16[544,128]{1,0:T(8,128)(2,1)S(1)}, u32[]{:S(2)}, u32[]{:S(2)}) collective-permute-start(bf16[544,128]{1,0:T(8,128)(2,1)S(1)} %collective-permute-done.4.refs_2_), channel_id=1, source_target_pairs={{0,16},{16,0},{1,17},{17,1},{2,18},{18,2},{3,19},{19,3},{4,20},{20... | collective-permute-start | bytes 417800 | tf_op jit(solution)/shard_map/ppermute | solution.py:328
  29.8 5.8 %collective-permute-start.7 = (bf16[512,128]{1,0:T(8,128)(2,1)S(1)}, bf16[512,128]{1,0:T(8,128)(2,1)S(1)}, u32[]{:S(2)}, u32[]{:S(2)}) collective-permute-start(bf16[512,128]{1,0:T(8,128)(2,1)S(1)} %get-tuple-element.49), channel_id=1, source_target_pairs={{0,16},{16,0},{1,17},{17,1},{2,18},{18,2},{3,19},{19,3},{4,20},{20... | collective-permute-start | bytes 393224 | tf_op jit(solution)/shard_map/ppermute | solution.py:328
  31.1 7.1 %collective-permute-start.10 = (bf16[512,128]{1,0:T(8,128)(2,1)S(1)}, bf16[512,128]{1,0:T(8,128)(2,1)S(1)}, u32[]{:S(2)}, u32[]{:S(2)}) collective-permute-start(bf16[512,128]{1,0:T(8,128)(2,1)S(1)} %get-tuple-element.59), channel_id=1, source_target_pairs={{0,16},{16,0},{1,17},{17,1},{2,18},{18,2},{3,19},{19,3},{4,20},{20... | collective-permute-start | bytes 393224 | tf_op jit(solution)/shard_map/ppermute | solution.py:328
  32.0 8.4 %collective-permute-start.9 = (bf16[256,1024]{1,0:T(8,128)(2,1)S(1)}, bf16[256,1024]{1,0:T(8,128)(2,1)S(1)}, u32[]{:S(2)}, u32[]{:S(2)}) collective-permute-start(bf16[256,1024]{1,0:T(8,128)(2,1)S(1)} %slice.15), channel_id=1, source_target_pairs={{0,1},{1,0},{2,3},{3,2},{4,5},{5,4},{6,7},{7,6},{8,9},{9,8},{10,11... | collective-permute-start | bytes 1572872 | tf_op jit(solution)/shard_map/ppermute | solution.py:331
  32.0 14.4 %collective-permute-start.12 = (bf16[512,128]{1,0:T(8,128)(2,1)S(1)}, bf16[512,128]{1,0:T(8,128)(2,1)S(1)}, u32[]{:S(2)}, u32[]{:S(2)}) collective-permute-start(bf16[512,128]{1,0:T(8,128)(2,1)S(1)} %get-tuple-element.61), channel_id=1, source_target_pairs={{0,16},{16,0},{1,17},{17,1},{2,18},{18,2},{3,19},{19,3},{4,20},{20... | collective-permute-start | bytes 393224 | tf_op jit(solution)/shard_map/ppermute | solution.py:328
  35.7 10.7 %collective-permute-start.8 = (bf16[512,128]{1,0:T(8,128)(2,1)S(1)}, bf16[512,128]{1,0:T(8,128)(2,1)S(1)}, u32[]{:S(2)}, u32[]{:S(2)}) collective-permute-start(bf16[512,128]{1,0:T(8,128)(2,1)S(1)} %add_convert_fusion.2), channel_id=1, source_target_pairs={{4,0},{5,1},{6,2},{7,3},{12,8},{13,9},{14,10},{15,11},{20,16},{21,... | collective-permute-start | bytes 393224 | tf_op jit(solution)/shard_map/ppermute | solution.py:325
  38.3 8.1 %collective-permute-start.11 = (bf16[512,128]{1,0:T(8,128)(2,1)S(1)}, bf16[512,128]{1,0:T(8,128)(2,1)S(1)}, u32[]{:S(2)}, u32[]{:S(2)}) collective-permute-start(bf16[512,128]{1,0:T(8,128)(2,1)S(1)} %add_convert_fusion.1), channel_id=1, source_target_pairs={{2,0},{3,1},{4,2},{5,3},{6,4},{7,5},{10,8},{11,9},{12,10},{13,11},... | collective-permute-start | bytes 393224 | tf_op jit(solution)/shard_map/ppermute | solution.py:325
  46.5 1.3 %collective-permute-start.13 = (bf16[256,128]{1,0:T(8,128)(2,1)S(1)}, bf16[256,128]{1,0:T(8,128)(2,1)S(1)}, u32[]{:S(2)}, u32[]{:S(2)}) collective-permute-start(bf16[256,128]{1,0:T(8,128)(2,1)S(1)} %slice.21), channel_id=1, source_target_pairs={{0,1},{1,0},{2,3},{3,2},{4,5},{5,4},{6,7},{7,6},{8,9},{9,8},{10,11... | collective-permute-start | bytes 196616 | tf_op jit(solution)/shard_map/ppermute | solution.py:331
